TPU v7x, 256 devices: a whole 4x4x8 slice. The times are simulated.
256 devices in a mesh: dp: 4 (over x), mp: 64 (over y, z, core).
Axes of the slice: x: 4, y: 4, z: 8, core: 2. Of those that a mesh axis runs over, the one named last changes fastest.
Arguments:
- grads: bfloat16 [4, 14336, 4096], P('dp', 'mp'), may hold values from -24 to 24
- errors: float32 [4, 14336, 4096], P('dp', 'mp'), may hold values from -6 to 6
- q_start: bfloat16 [14336, 32], P('mp'), may hold values from -6 to 6
Outputs:
- update: bfloat16 [14336, 4096], P('mp')
- new_errors: float32 [4, 14336, 4096], P('dp', 'mp')
- new_q: float32 [14336, 32], P('mp')
All inputs are finite; a program needn't handle non-finite values.
Results may differ from a plain program's by a relative error of at most 0.0066.
Values sent between devices are 32-bit elements; how exact they have to be, the bound alone decides.
No kernel may reach another device: no remote copies, remote signals or barrier semaphores. Data moves between devices by JAX's collectives and lax.ppermute only.
A program may use at most 64 MiB of HBM per device.

v0:
```python
import jax
import jax.numpy as jnp
from jax import lax
from jax.sharding import PartitionSpec as P


def orthonormal(factor, gram):
    lower = jnp.linalg.cholesky(gram)
    return lax.linalg.triangular_solve(lower, factor, left_side=False, lower=True, transpose_a=True)


def shards(grads, errors, q_start):
    compensated = grads[0].astype(jnp.float32) + errors[0]
    comp_low = compensated.astype(jnp.bfloat16)
    partial_p = lax.dot_general(
        comp_low, q_start, (((0,), (0,)), ((), ())), preferred_element_type=jnp.float32
    )
    p_full = lax.psum(partial_p, ("dp", "mp"))
    gram = jnp.dot(p_full.T, p_full, precision=lax.Precision.HIGHEST)
    ortho = orthonormal(p_full, gram)
    ortho_low = ortho.astype(jnp.bfloat16)
    local_q = jnp.dot(comp_low, ortho_low, preferred_element_type=jnp.float32)
    new_q = lax.psum(local_q, "dp") / lax.axis_size("dp")
    approx = jnp.dot(new_q, ortho.T, precision=lax.Precision.HIGHEST)
    new_errors = (compensated - approx)[None]
    return (approx.astype(jnp.bfloat16), new_errors, new_q)


def solution(mesh):
    return jax.shard_map(
        shards,
        mesh=mesh,
        in_specs=(P("dp", "mp", None), P("dp", "mp", None), P("mp", None)),
        out_specs=(P("mp", None), P("dp", "mp", None), P("mp", None)),
        check_vma=False,
    )
```

profile of v0, /device:TPU:1, one launch (start us, length us, event | category | flops | bytes accessed | tf_op | source)
XLA Modules:
  0.0 308.1 jit_solution(5122788060113921355)
XLA Ops:
  7.2 0.0 copy-start
  7.2 0.0 copy-start.1
  7.2 0.0 all-reduce.2.cloned.1.call-start
  7.2 0.7 copy-done
  7.9 3.9 %fusion.7 = f32[4096,32]{0,1:T(8,128)} fusion(bf16[224,32]{0,1:T(8,128)(2,1)S(1)} %copy-done, f32[1,224,4096]{2,1,0:T(8,128)} %param.4, bf16[1,224,4096]{2,1,0:T(8,128)(2,1)} %param.3), kind=kOutput, calls=%fused_computation.17 | convolution fusion | flops 61472768 | bytes 6043648 | tf_op jit(solution)/shard_map/dot_general | solution.py:15
  11.8 0.0 all-reduce.2.cloned.1.call-update
  11.8 256.8 %all-reduce.2.cloned.1.call-done = f32[4096,32]{0,1:T(8,128)} async-done(((f32[4096,32]{0,1:T(8,128)}), f32[4096,32]{0,1:T(8,128)}) %all-reduce.2.cloned.1.call-update) | async-done | bytes 524304 | tf_op jit(solution)/shard_map/psum | solution.py:18
  268.6 1.8 fusion.8
  270.3 0.1 copy.6
  270.4 2.9 cholesky.16
  273.4 0.6 compare_reduce_fusion
  274.0 0.7 fusion.3
  274.7 2.4 custom-call.6
  277.1 1.7 fusion.4
  278.8 0.0 copy-done.1
  278.8 2.7 fusion.1
  281.5 13.1 %psum.15 = f32[224,32]{0,1:T(8,128)S(1)} all-reduce(f32[224,32]{0,1:T(8,128)S(1)} %fusion.1), channel_id=1, replica_groups=mesh['dp'=4,'mp'=64] {'dp'}, use_global_device_ids=true, to_apply=%region_3.4 | all-reduce | flops 7168 | bytes 57344 | tf_op jit(solution)/shard_map/psum | solution.py:23
  294.7 0.0 copy-start.2
  294.7 6.6 %fusion = (f32[1,224,4096]{2,1,0:T(8,128)}, bf16[224,4096]{1,0:T(8,128)(2,1)}) fusion(f32[1,224,4096]{2,1,0:T(8,128)} %param.4, bf16[1,224,4096]{2,1,0:T(8,128)(2,1)S(1)} %copy-done.1, f32[224,32]{0,1:T(8,128)S(1)} %broadcast_multiply_fusion, f32[4096,32]{0,1:T(8,128)S(1)} %fusion.4), kind=kOutput, calls=%fused_computation.2 | convolution fusion | flops 355991552 | bytes 11563008 | tf_op jit(solution)/shard_map/dot_general | solution.py:24
  301.3 0.0 copy-done.2
  (3 shorter events, 0.0 us)
Async XLA Ops:
  7.2 0.7 copy-start
  7.2 271.6 %copy-start.1 = (bf16[1,224,4096]{2,1,0:T(8,128)(2,1)S(1)}, bf16[1,224,4096]{2,1,0:T(8,128)(2,1)}, u32[]{:S(2)}) copy-start(bf16[1,224,4096]{2,1,0:T(8,128)(2,1)} %param.3) | copy-start | bytes 5505028
  7.2 261.4 %all-reduce.2.cloned.1.call-start = ((), (), s32[]{:S(2)}) async-start(), calls=%async_computation | async-start | bytes 1048576 | tf_op jit(solution)/shard_map/psum | solution.py:18
  294.7 6.6 %copy-start.2 = (f32[224,32]{0,1:T(8,128)}, f32[224,32]{0,1:T(8,128)S(1)}, u32[]{:S(2)}) copy-start(f32[224,32]{0,1:T(8,128)S(1)} %broadcast_multiply_fusion) | copy-start | bytes 86020
Sparse Core Ops, SparseCore 0:
  14.1 254.4 all-reduce.1
where the time goes:
time: 312 us; the launch traced here: 308 us
  waiting for transfers between devices  257 us (82%)
  matrix products  16.6 us (5%)
  between operations  14.1 us (5%)
  blocking collectives  13.1 us (4%)
  other arithmetic  6.69 us (2%)
    psum x1, waiting for transfers between devices, shards(): p_full = lax.psum(partial_p, ('dp', 'mp'))  257 us
    psum x1, blocking collectives, shards(): new_q = lax.psum(local_q, 'dp') / lax.axis_size('dp')  13.1 us
    dot_general x1, matrix products, shards(): approx = jnp.dot(new_q, ortho.T, precision=lax.Precision.HIGHEST)  6.59 us
  transfers between devices with their start and end apart: 1, of which 1 were waited for; matrix products, arithmetic and copies ran while one was open for 0% of the time, Pallas kernels for 0%

commit v1 on v0

v1 whole, which is shorter than its diff:
```python
import jax
import jax.numpy as jnp
from jax import lax
from jax.sharding import Mesh
from jax.sharding import PartitionSpec as P

X, Y, Z, C = 4, 4, 8, 2
RANK = 32
HALF = RANK // C
FEATURES = 4096
BLOCK = FEATURES // (X * Y)


def shift(array, axis, size, step):
    return lax.ppermute(array, axis, [(i, (i + step) % size) for i in range(size)])


def sum_everywhere(partial):
    core = lax.axis_index("c")
    halves = partial.reshape(C, HALF, FEATURES)
    mine = jnp.where(core == 0, halves[0], halves[1])
    other = jnp.where(core == 0, halves[1], halves[0])
    mine = mine + shift(other, "c", C, 1)
    blocks = mine.reshape(HALF, X * Y, BLOCK).transpose(1, 0, 2)
    block = jnp.sum(lax.all_to_all(blocks, ("x", "y"), 0, 0), 0)
    block = jnp.sum(lax.all_to_all(jnp.broadcast_to(block, (Z,) + block.shape), "z", 0, 0), 0)
    blocks = lax.all_to_all(jnp.broadcast_to(block, (X * Y,) + block.shape), ("x", "y"), 0, 0)
    mine = blocks.transpose(1, 0, 2).reshape(HALF, FEATURES)
    other = shift(mine, "c", C, 1)
    return jnp.concatenate([jnp.where(core == 0, mine, other), jnp.where(core == 0, other, mine)])


def shards(grads, errors, q_start):
    compensated = grads[0].astype(jnp.float32) + errors[0]
    comp_low = compensated.astype(jnp.bfloat16)
    partial_p = lax.dot_general(
        q_start, comp_low, (((0,), (0,)), ((), ())), preferred_element_type=jnp.float32
    )
    p_t = sum_everywhere(partial_p)
    gram = jnp.dot(p_t, p_t.T, precision=lax.Precision.HIGHEST)
    lower = jnp.linalg.cholesky(gram)
    ortho_t = lax.linalg.triangular_solve(lower, p_t, left_side=True, lower=True)
    ortho_low = ortho_t.astype(jnp.bfloat16)
    local_q = lax.dot_general(
        ortho_low, comp_low, (((1,), (1,)), ((), ())), preferred_element_type=jnp.float32
    )
    left, right, across = (shift(local_q, "x", X, step) for step in (1, 3, 2))
    total_q = (local_q + across) + (left + right)
    new_q = (total_q / X).T
    approx = jnp.dot(new_q, ortho_t, precision=lax.Precision.HIGHEST)
    new_errors = (compensated - approx)[None]
    return (approx.astype(jnp.bfloat16), new_errors, new_q)


def solution(mesh):
    split = Mesh(mesh.devices.reshape(X, Y, Z, C), ("x", "y", "z", "c"))
    rows = ("y", "z", "c")
    return jax.shard_map(
        shards,
        mesh=split,
        in_specs=(P("x", rows, None), P("x", rows, None), P(rows, None)),
        out_specs=(P(rows, None), P("x", rows, None), P(rows, None)),
        check_vma=False,
    )
```

time: 312 us -> 76.5 us (0.25); the launches traced: 308 us -> 76.1 us
  waiting for transfers between devices: 257 us -> 5.55 us
  blocking collectives: 13.1 us -> 39.1 us
  between operations: 14.1 us -> 0.77 us
  starting transfers between devices: 0.04 us -> 10.4 us
  matrix products: 16.6 us -> 12.5 us
    psum x1 -> x0, waiting for transfers between devices: 257 us -> none  [shards(): p_full = lax.psum(partial_p, ('dp', 'mp'))]
    all_to_all x0 -> x3, blocking collectives: none -> 39.1 us  [the longest x1 16 us: sum_everywhere(): lax.all_to_all(jnp.broadcast_to(block, (Z,) + block.shape), 'z', 0, 0)]
    psum x1 -> x0, blocking collectives: 13.1 us -> none  [shards(): new_q = lax.psum(local_q, 'dp') / lax.axis_size('dp')]
    ppermute x0 -> x5, starting transfers between devices: none -> 10.4 us  [shift(): lax.ppermute(array, axis, [(i, (i + step) % size) for i in range(size)])]
    ppermute x0 -> x5, waiting for transfers between devices: none -> 5.55 us  [shift(): lax.ppermute(array, axis, [(i, (i + step) % size) for i in range(size)])]
  transfers between devices with their start and end apart: 1 -> 5, of which waited for: 1 -> 5; matrix products, arithmetic and copies ran while one was open for 0% -> 0% of each run, Pallas kernels for 0% -> 0%
where the time goes in v1:
time: 76.5 us; the launch traced here: 76.1 us
  blocking collectives  39.1 us (51%)
  matrix products  12.5 us (16%)
  starting transfers between devices  10.4 us (14%)
  other arithmetic  6.85 us (9%)
  waiting for transfers between devices  5.55 us (7%)
  local copies, waits for them, and re-layouts  0.86 us (1%)
  between operations  0.77 us (1%)
    all_to_all x1, blocking collectives, sum_everywhere(): lax.all_to_all(jnp.broadcast_to(block, (Z,) + block.shape), 'z', 0, 0)  16 us
    all_to_all x1, blocking collectives, sum_everywhere(): block = jnp.sum(lax.all_to_all(blocks, ('x', 'y'), 0, 0), 0)  12.4 us
    all_to_all x1, blocking collectives, sum_everywhere(): lax.all_to_all(jnp.broadcast_to(block, (X * Y,) + block.shape), ('x', 'y'...  10.7 us
    ppermute x5, starting transfers between devices, shift(): lax.ppermute(array, axis, [(i, (i + step) % size) for i in range(size)])  10.4 us
    ppermute x5, waiting for transfers between devices, shift(): lax.ppermute(array, axis, [(i, (i + step) % size) for i in range(size)])  5.55 us
    dot_general x1, matrix products, shards(): approx = jnp.dot(new_q, ortho_t, precision=lax.Precision.HIGHEST)  5.21 us
    another operation x3, other arithmetic, shards(): lower = jnp.linalg.cholesky(gram)  3.6 us
    another operation x2, other arithmetic, shards(): lax.linalg.triangular_solve(lower, p_t, left_side=True, lower=True)  3.09 us
  transfers between devices with their start and end apart: 5, of which 5 were waited for; matrix products, arithmetic and copies ran while one was open for 0% of the time, Pallas kernels for 0%

profile of v1, /device:TPU:1, one launch (start us, length us, event | category | flops | bytes accessed | tf_op | source)
XLA Modules:
  0.0 76.1 jit_solution(8766862443271566967)
XLA Ops:
  0.6 0.0 copy-start
  0.7 0.7 copy-done
  1.4 3.1 %convolution_bitcast_fusion = f32[32,4096]{1,0:T(8,128)S(1)} fusion(bf16[224,32]{0,1:T(8,128)(2,1)S(1)} %copy-done, f32[1,224,4096]{2,1,0:T(8,128)} %param.4, bf16[1,224,4096]{2,1,0:T(8,128)(2,1)} %param.3), kind=kOutput, calls=%fused_computation | convolution fusion | flops 61472768 | bytes 6043648 | tf_op jit(solution)/shard_map/dot_general | solution.py:36
  4.5 0.0 copy-start.2
  4.5 3.3 %collective-permute-start = (f32[16,4096]{1,0:T(8,128)S(1)}, f32[16,4096]{1,0:T(8,128)S(1)}, u32[]{:S(2)}, u32[]{:S(2)}) collective-permute-start(f32[16,4096]{1,0:T(8,128)S(1)} %slice_select_fusion), channel_id=1, source_target_pairs={{0,1},{1,0},{2,3},{3,2},{4,5},{5,4},{6,7},{7,6},{8,9},{9,8},{10,11... | collective-permute-start | bytes 786440 | tf_op jit(solution)/shard_map/ppermute | solution.py:15
  7.8 1.2 %collective-permute-done = f32[16,4096]{1,0:T(8,128)S(1)} collective-permute-done((f32[16,4096]{1,0:T(8,128)S(1)}, f32[16,4096]{1,0:T(8,128)S(1)}, u32[]{:S(2)}, u32[]{:S(2)}) %collective-permute-start) | collective-permute-done | bytes 262176 | tf_op jit(solution)/shard_map/ppermute | solution.py:15
  9.1 12.4 %all_to_all.15 = f32[16,16,256]{2,1,0:T(8,128)S(1)} all-to-all(f32[16,16,256]{2,1,0:T(8,128)S(1)} %bitcast.34), channel_id=1, replica_groups=mesh['x'=4,'y'=4,'z'=8,'c'=2] {'x','y'}, dimensions={0} | all-to-all | bytes 524288 | tf_op jit(solution)/shard_map/all_to_all | solution.py:25
  21.5 16.0 %all_to_all.16 = f32[8,16,256]{2,1,0:T(8,128)S(1)} all-to-all(f32[8,16,256]{2,1,0:T(8,128)S(1)} %broadcast_in_dim.11), channel_id=1, replica_groups=mesh['x'=4,'y'=4,'z'=8,'c'=2] {'z'}, dimensions={0} | all-to-all | bytes 262144 | tf_op jit(solution)/shard_map/all_to_all | solution.py:26
  37.5 10.7 %all_to_all.17 = f32[16,16,256]{2,1,0:T(8,128)S(1)} all-to-all(f32[16,16,256]{2,1,0:T(8,128)S(1)} %broadcast_in_dim.12), channel_id=1, replica_groups=mesh['x'=4,'y'=4,'z'=8,'c'=2] {'x','y'}, dimensions={0} | all-to-all | bytes 524288 | tf_op jit(solution)/shard_map/all_to_all | solution.py:27
  48.3 4.5 %collective-permute-start.1 = (f32[16,4096]{1,0:T(8,128)S(1)}, f32[16,4096]{1,0:T(8,128)S(1)}, u32[]{:S(2)}, u32[]{:S(2)}) collective-permute-start(f32[16,4096]{1,0:T(8,128)S(1)} %bitcast.36), channel_id=1, source_target_pairs={{0,1},{1,0},{2,3},{3,2},{4,5},{5,4},{6,7},{7,6},{8,9},{9,8},{10,11... | collective-permute-start | bytes 786440 | tf_op jit(solution)/shard_map/ppermute | solution.py:15
  52.8 1.2 %collective-permute-done.1 = f32[16,4096]{1,0:T(8,128)S(1)} collective-permute-done((f32[16,4096]{1,0:T(8,128)S(1)}, f32[16,4096]{1,0:T(8,128)S(1)}, u32[]{:S(2)}, u32[]{:S(2)}) %collective-permute-start.1) | collective-permute-done | bytes 262176 | tf_op jit(solution)/shard_map/ppermute | solution.py:15
  54.0 0.6 fusion.2
  54.5 0.1 copy.12
  54.6 2.9 %cholesky.16 = f32[32,32]{1,0:T(8,128)S(1)} custom-call(f32[32,32]{1,0:T(8,128)S(1)} %fusion.7), custom_call_target="Cholesky" | custom-call | tf_op jit(solution)/shard_map/jit(cholesky)/cholesky | solution.py:41
  57.6 0.6 compare_reduce_fusion
  58.2 0.7 fusion.5
  58.9 2.4 %custom-call.6 = f32[1,32,32]{1,2,0:T(8,128)S(1)} custom-call(f32[1,32,32]{2,1,0:T(8,128)S(1)} %fusion.5), custom_call_target="InvertDiagBlocksLowerTriangular" | custom-call | tf_op jit(solution)/shard_map/triangular_solve | solution.py:42
  61.3 0.0 copy-start.1
  61.3 0.6 fusion.1
  62.0 0.0 copy-done.2
  62.0 3.0 %fusion.3 = f32[32,224]{1,0:T(8,128)S(1)} fusion(f32[32,4096]{1,0:T(8,128)S(1)} %fusion.1, f32[1,224,4096]{2,1,0:T(8,128)} %param.4, bf16[1,224,4096]{2,1,0:T(8,128)(2,1)S(1)} %copy-done.2), kind=kOutput, calls=%fused_computation.9 | convolution fusion | flops 61603840 | bytes 6057984 | tf_op jit(solution)/shard_map/dot_general | solution.py:44
  65.0 0.9 %collective-permute-start.4 = (f32[32,224]{1,0:T(8,128)S(1)}, f32[32,224]{1,0:T(8,128)S(1)}, u32[]{:S(2)}, u32[]{:S(2)}) collective-permute-start(f32[32,224]{1,0:T(8,128)S(1)} %fusion.3), channel_id=1, source_target_pairs={{0,192},{64,0},{128,64},{192,128},{1,193},{65,1},{129,65},{193,129... | collective-permute-start | bytes 86024 | tf_op jit(solution)/shard_map/ppermute | solution.py:15
  65.9 0.7 collective-permute-start.3
  66.6 1.1 %collective-permute-start.2 = (f32[32,224]{1,0:T(8,128)S(1)}, f32[32,224]{1,0:T(8,128)S(1)}, u32[]{:S(2)}, u32[]{:S(2)}) collective-permute-start(f32[32,224]{1,0:T(8,128)S(1)} %fusion.3), channel_id=1, source_target_pairs={{0,128},{64,192},{128,0},{192,64},{1,129},{65,193},{129,1},{193,65... | collective-permute-start | bytes 86024 | tf_op jit(solution)/shard_map/ppermute | solution.py:15
  67.6 0.2 collective-permute-done.4
  67.9 2.0 %collective-permute-done.3 = f32[32,224]{1,0:T(8,128)S(1)} collective-permute-done((f32[32,224]{1,0:T(8,128)S(1)}, f32[32,224]{1,0:T(8,128)S(1)}, u32[]{:S(2)}, u32[]{:S(2)}) %collective-permute-start.3) | collective-permute-done | bytes 28704 | tf_op jit(solution)/shard_map/ppermute | solution.py:15
  69.9 1.0 %collective-permute-done.2 = f32[32,224]{1,0:T(8,128)S(1)} collective-permute-done((f32[32,224]{1,0:T(8,128)S(1)}, f32[32,224]{1,0:T(8,128)S(1)}, u32[]{:S(2)}, u32[]{:S(2)}) %collective-permute-start.2) | collective-permute-done | bytes 28704 | tf_op jit(solution)/shard_map/ppermute | solution.py:15
  70.9 0.0 copy-done.1
  70.9 0.0 copy-start.3
  70.9 5.2 %fusion = (f32[1,224,4096]{2,1,0:T(8,128)}, bf16[224,4096]{1,0:T(8,128)(2,1)}) fusion(f32[1,224,4096]{2,1,0:T(8,128)S(1)} %copy-done.1, bf16[1,224,4096]{2,1,0:T(8,128)(2,1)S(1)} %copy-done.2, f32[32,224]{1,0:T(8,128)S(1)} %add_multiply_fusion, f32[32,4096]{1,0:T(8,128)S(1)} %fusion.1), kind=kOutput, calls=%fused_computation.3 | convolution fusion | flops 355991552 | bytes 11563008 | tf_op jit(solution)/shard_map/dot_general | solution.py:50
  76.1 0.0 copy-done.3
  (12 shorter events, 0.3 us)
Async XLA Ops:
  0.6 0.7 copy-start
  4.5 57.5 %copy-start.2 = (bf16[1,224,4096]{2,1,0:T(8,128)(2,1)S(1)}, bf16[1,224,4096]{2,1,0:T(8,128)(2,1)}, u32[]{:S(2)}) copy-start(bf16[1,224,4096]{2,1,0:T(8,128)(2,1)} %param.3) | copy-start | bytes 5505028
  4.5 4.5 %collective-permute-start = (f32[16,4096]{1,0:T(8,128)S(1)}, f32[16,4096]{1,0:T(8,128)S(1)}, u32[]{:S(2)}, u32[]{:S(2)}) collective-permute-start(f32[16,4096]{1,0:T(8,128)S(1)} %slice_select_fusion), channel_id=1, source_target_pairs={{0,1},{1,0},{2,3},{3,2},{4,5},{5,4},{6,7},{7,6},{8,9},{9,8},{10,11... | collective-permute-start | bytes 786440 | tf_op jit(solution)/shard_map/ppermute | solution.py:15
  48.3 5.6 %collective-permute-start.1 = (f32[16,4096]{1,0:T(8,128)S(1)}, f32[16,4096]{1,0:T(8,128)S(1)}, u32[]{:S(2)}, u32[]{:S(2)}) collective-permute-start(f32[16,4096]{1,0:T(8,128)S(1)} %bitcast.36), channel_id=1, source_target_pairs={{0,1},{1,0},{2,3},{3,2},{4,5},{5,4},{6,7},{7,6},{8,9},{9,8},{10,11... | collective-permute-start | bytes 786440 | tf_op jit(solution)/shard_map/ppermute | solution.py:15
  61.3 9.6 %copy-start.1 = (f32[1,224,4096]{2,1,0:T(8,128)S(1)}, f32[1,224,4096]{2,1,0:T(8,128)}, u32[]{:S(2)}) copy-start(f32[1,224,4096]{2,1,0:T(8,128)} %param.4) | copy-start | bytes 11010052
  65.0 2.8 %collective-permute-start.4 = (f32[32,224]{1,0:T(8,128)S(1)}, f32[32,224]{1,0:T(8,128)S(1)}, u32[]{:S(2)}, u32[]{:S(2)}) collective-permute-start(f32[32,224]{1,0:T(8,128)S(1)} %fusion.3), channel_id=1, source_target_pairs={{0,192},{64,0},{128,64},{192,128},{1,193},{65,1},{129,65},{193,129... | collective-permute-start | bytes 86024 | tf_op jit(solution)/shard_map/ppermute | solution.py:15
  65.9 4.0 %collective-permute-start.3 = (f32[32,224]{1,0:T(8,128)S(1)}, f32[32,224]{1,0:T(8,128)S(1)}, u32[]{:S(2)}, u32[]{:S(2)}) collective-permute-start(f32[32,224]{1,0:T(8,128)S(1)} %fusion.3), channel_id=1, source_target_pairs={{0,64},{64,128},{128,192},{192,0},{1,65},{65,129},{129,193},{193,1... | collective-permute-start | bytes 86024 | tf_op jit(solution)/shard_map/ppermute | solution.py:15
  66.6 4.3 %collective-permute-start.2 = (f32[32,224]{1,0:T(8,128)S(1)}, f32[32,224]{1,0:T(8,128)S(1)}, u32[]{:S(2)}, u32[]{:S(2)}) collective-permute-start(f32[32,224]{1,0:T(8,128)S(1)} %fusion.3), channel_id=1, source_target_pairs={{0,128},{64,192},{128,0},{192,64},{1,129},{65,193},{129,1},{193,65... | collective-permute-start | bytes 86024 | tf_op jit(solution)/shard_map/ppermute | solution.py:15
  70.9 5.2 %copy-start.3 = (f32[32,224]{1,0:T(8,128)}, f32[32,224]{1,0:T(8,128)S(1)}, u32[]{:S(2)}) copy-start(f32[32,224]{1,0:T(8,128)S(1)} %add_multiply_fusion) | copy-start | bytes 86020

commit v2 on v1

v2 whole, which is shorter than its diff:
```python
import jax
import jax.numpy as jnp
from jax import lax
from jax.experimental import pallas as pl
from jax.experimental.pallas import tpu as pltpu
from jax.sharding import Mesh
from jax.sharding import PartitionSpec as P

X, Y, Z, C = 4, 4, 8, 2
RANK = 32
HALF = RANK // C
ROWS = 224
PAD = 256
FEATURES = 4096
BLOCKS = X * Y
BLOCK = FEATURES // BLOCKS
CHUNKS = 8
WIDTH = FEATURES // CHUNKS
F32, BF16 = jnp.float32, jnp.bfloat16
VMEM_LIMIT = 40 * 2**20


def columns(chunk):
    return pl.ds(chunk * WIDTH, WIDTH)


def two_terms(value):
    high = value.astype(BF16)
    return high, (value - high.astype(F32)).astype(BF16)


def three_terms(value):
    high, rest = value.astype(BF16), value
    rest = value - high.astype(F32)
    middle = rest.astype(BF16)
    return high, middle, (rest - middle.astype(F32)).astype(BF16)


def compensate_kernel(
    grads, errors, q_hbm, comp, low, mine, other, grad_buf, q_t, q_sem, grad_sems, error_sems
):
    q_copy = pltpu.make_async_copy(q_hbm, q_t, q_sem)
    q_copy.start()
    copies = []
    for chunk in range(CHUNKS):
        cols = columns(chunk)
        pair = (
            pltpu.make_async_copy(grads.at[:, cols], grad_buf.at[:, cols], grad_sems.at[chunk]),
            pltpu.make_async_copy(errors.at[:, cols], comp.at[:, cols], error_sems.at[chunk]),
        )
        for copy in pair:
            copy.start()
        copies.append(pair)
    q_copy.wait()
    first = lax.axis_index("c") == 0
    top, bottom = q_t[:HALF, :], q_t[HALF:, :]
    factor = jnp.concatenate([jnp.where(first, top, bottom), jnp.where(first, bottom, top)])
    for chunk in range(CHUNKS):
        for copy in copies[chunk]:
            copy.wait()
        cols = columns(chunk)
        total = grad_buf[:, cols].astype(F32) + comp[:, cols]
        comp[:, cols] = total
        rounded = total.astype(BF16)
        low[:, cols] = rounded
        partial = jnp.dot(factor, rounded, preferred_element_type=F32)
        for part in range(WIDTH // BLOCK):
            block = chunk * (WIDTH // BLOCK) + part
            at = slice(part * BLOCK, (part + 1) * BLOCK)
            mine[block] = partial[:HALF, at]
            other[block] = partial[HALF:, at]


def compensate(grads, errors, q_t):
    vmem = pl.BlockSpec(memory_space=pltpu.VMEM)
    hbm = pl.BlockSpec(memory_space=pltpu.HBM)
    half = pltpu.VMEM((BLOCKS, HALF, BLOCK), F32)
    return pl.pallas_call(
        compensate_kernel,
        out_shape=(
            pltpu.VMEM((ROWS, FEATURES), F32),
            pltpu.VMEM((ROWS, FEATURES), BF16),
            half,
            half,
        ),
        in_specs=[hbm] * 3,
        out_specs=[vmem] * 4,
        scratch_shapes=[
            pltpu.VMEM((ROWS, FEATURES), BF16),
            pltpu.VMEM((RANK, ROWS), BF16),
            pltpu.SemaphoreType.DMA,
            pltpu.SemaphoreType.DMA((CHUNKS,)),
            pltpu.SemaphoreType.DMA((CHUNKS,)),
        ],
        compiler_params=pltpu.CompilerParams(vmem_limit_bytes=VMEM_LIMIT),
        name="compensate",
    )(
        pltpu.with_memory_space_constraint(grads, pltpu.HBM),
        pltpu.with_memory_space_constraint(errors, pltpu.HBM),
        pltpu.with_memory_space_constraint(q_t, pltpu.HBM),
    )


def project_kernel(low, mine, other, product, terms):
    core = lax.axis_index("c")
    for block in range(BLOCKS):
        for half, row in ((mine, core * HALF), (other, (1 - core) * HALF)):
            for term, value in enumerate(three_terms(half[block])):
                rows = pl.ds(pl.multiple_of(term * RANK + row, HALF), HALF)
                terms[rows, block * BLOCK : (block + 1) * BLOCK] = value
    stacked = lax.dot_general(low[...], terms[...], (((1,), (1,)), ((), ())), preferred_element_type=F32)
    total = stacked[:, :RANK] + (stacked[:, RANK : 2 * RANK] + stacked[:, 2 * RANK :])
    padded = jnp.concatenate([total, jnp.zeros((PAD - ROWS, RANK), F32)])
    product[...] = padded.T


def project(low, mine, other):
    vmem = pl.BlockSpec(memory_space=pltpu.VMEM)
    return pl.pallas_call(
        project_kernel,
        out_shape=(pltpu.VMEM((RANK, PAD), F32), pltpu.VMEM((3 * RANK, FEATURES), BF16)),
        in_specs=[vmem] * 3,
        out_specs=[vmem] * 2,
        compiler_params=pltpu.CompilerParams(vmem_limit_bytes=VMEM_LIMIT),
        name="project",
    )(pltpu.with_memory_space_constraint(low, pltpu.VMEM), mine, other)


def inverse_of_lower(gram):
    row = lax.broadcasted_iota(jnp.int32, (RANK, RANK), 0)
    column = lax.broadcasted_iota(jnp.int32, (RANK, RANK), 1)
    work = jnp.concatenate([gram, (row == column).astype(F32)], axis=1)
    index = lax.broadcasted_iota(jnp.int32, (RANK, 2 * RANK), 0)
    scale = jnp.zeros((RANK, 2 * RANK), F32)
    for step in range(RANK):
        pivot_row = jnp.broadcast_to(work[step : step + 1, :], work.shape)
        pivot = jnp.broadcast_to(work[step : step + 1, step : step + 1], work.shape)
        multiplier = jnp.broadcast_to(work[:, step : step + 1], work.shape) / pivot
        scale = jnp.where(index == step, pivot, scale)
        work = jnp.where(index > step, work - multiplier * pivot_row, work)
    return (work / jnp.sqrt(scale))[:, RANK:]


def factor_kernel(terms, inverse, ortho):
    stacked = lax.dot_general(terms[...], terms[...], (((1,), (1,)), ((), ())), preferred_element_type=F32)

    def part(left, right):
        return stacked[left * RANK : (left + 1) * RANK, right * RANK : (right + 1) * RANK]

    small = part(0, 2) + part(2, 0) + part(1, 1)
    gram = part(0, 0) + ((part(0, 1) + part(1, 0)) + small)
    lower_inverse = inverse_of_lower(gram)
    inverse[...] = lower_inverse
    for chunk in range(CHUNKS):
        cols = columns(chunk)
        p_t = (
            terms[:RANK, cols].astype(F32)
            + terms[RANK : 2 * RANK, cols].astype(F32)
            + terms[2 * RANK :, cols].astype(F32)
        )
        ortho_t = jnp.dot(
            lower_inverse, p_t, precision=lax.Precision.HIGHEST, preferred_element_type=F32
        )
        high, low = two_terms(ortho_t)
        ortho[:RANK, cols] = high
        ortho[RANK : 2 * RANK, cols] = low
        ortho[2 * RANK :, cols] = high


def factor(terms):
    vmem = pl.BlockSpec(memory_space=pltpu.VMEM)
    return pl.pallas_call(
        factor_kernel,
        out_shape=(pltpu.VMEM((RANK, RANK), F32), pltpu.VMEM((3 * RANK, FEATURES), BF16)),
        in_specs=[vmem],
        out_specs=[vmem] * 2,
        compiler_params=pltpu.CompilerParams(vmem_limit_bytes=VMEM_LIMIT),
        cost_estimate=pl.CostEstimate(flops=10**9, bytes_accessed=10**7, transcendentals=0),
        name="factor",
    )(terms)


def apply_kernel(
    comp, own, across, left, right, inverse, ortho, new_errors, update, new_q, error_buf, update_buf, error_sems, update_sems
):
    total = (own[...] + across[...]) + (left[...] + right[...])
    q_t = jnp.dot(
        inverse[...], total * (1.0 / X), precision=lax.Precision.HIGHEST, preferred_element_type=F32
    )
    new_q[...] = q_t[:, :ROWS]
    high = q_t.astype(BF16).astype(F32)
    stacked = jnp.concatenate([high, high, q_t - high]).T[:ROWS].astype(BF16)
    copies = []
    for chunk in range(CHUNKS):
        cols = columns(chunk)
        approx = jnp.dot(stacked, ortho[:, cols], preferred_element_type=F32)
        error_buf[:, cols] = comp[:, cols] - approx
        update_buf[:, cols] = approx.astype(BF16)
        copies += [
            pltpu.make_async_copy(error_buf.at[:, cols], new_errors.at[:, cols], error_sems.at[chunk]),
            pltpu.make_async_copy(update_buf.at[:, cols], update.at[:, cols], update_sems.at[chunk]),
        ]
        for copy in copies[-2:]:
            copy.start()
    for copy in copies:
        copy.wait()


def apply(comp, own, across, left, right, inverse, ortho):
    vmem = pl.BlockSpec(memory_space=pltpu.VMEM)
    hbm = pl.BlockSpec(memory_space=pl.ANY)
    return pl.pallas_call(
        apply_kernel,
        out_shape=(
            jax.ShapeDtypeStruct((ROWS, FEATURES), F32),
            jax.ShapeDtypeStruct((ROWS, FEATURES), BF16),
            jax.ShapeDtypeStruct((RANK, ROWS), F32),
        ),
        in_specs=[vmem] * 7,
        out_specs=[hbm, hbm, vmem],
        scratch_shapes=[
            pltpu.VMEM((ROWS, FEATURES), F32),
            pltpu.VMEM((ROWS, FEATURES), BF16),
            pltpu.SemaphoreType.DMA((CHUNKS,)),
            pltpu.SemaphoreType.DMA((CHUNKS,)),
        ],
        compiler_params=pltpu.CompilerParams(vmem_limit_bytes=VMEM_LIMIT),
        name="apply",
    )(pltpu.with_memory_space_constraint(comp, pltpu.VMEM), own, across, left, right, inverse, ortho)


def shift(array, axis, size, step):
    return lax.ppermute(array, axis, [(i, (i + step) % size) for i in range(size)])


def repeat(block, times):
    return jnp.broadcast_to(block, (times,) + block.shape)


def sum_everywhere(mine, other):
    mine = mine + shift(other, "c", C, 1)
    block = jnp.sum(lax.all_to_all(mine, ("x", "y"), 0, 0), 0)
    block = jnp.sum(lax.all_to_all(repeat(block, Z), "z", 0, 0), 0)
    mine = lax.all_to_all(repeat(block, BLOCKS), ("x", "y"), 0, 0)
    return mine, shift(mine, "c", C, 1)


def shards(grads, errors, q_start):
    comp, low, mine, other = compensate(grads[0], errors[0], q_start.T)
    mine, other = sum_everywhere(mine, other)
    product, terms = project(low, mine, other)
    across, left, right = (shift(product, "x", X, step) for step in (2, 1, 3))
    inverse, ortho = factor(terms)
    new_errors, update, new_q = apply(comp, product, across, left, right, inverse, ortho)
    return (update, new_errors[None], new_q.T)


def solution(mesh):
    split = Mesh(mesh.devices.reshape(X, Y, Z, C), ("x", "y", "z", "c"))
    rows = ("y", "z", "c")
    return jax.shard_map(
        shards,
        mesh=split,
        in_specs=(P("x", rows, None), P("x", rows, None), P(rows, None)),
        out_specs=(P(rows, None), P("x", rows, None), P(rows, None)),
        check_vma=False,
    )
```

time: 76.5 us -> 68.7 us (0.90)
  Pallas kernels: 0 us -> 13.9 us
  matrix products: 12.5 us -> 0 us
  other arithmetic: 6.85 us -> 0.07 us
  waiting for transfers between devices: 5.55 us -> 2.33 us
  local copies, waits for them, and re-layouts: 0.86 us -> 1.87 us
    pallas_call x0 -> x4, Pallas kernels: none -> 13.9 us  [the longest x1 5.66 us: factor(): pl.pallas_call(factor_kernel, out_shape=(pltpu.VMEM((RANK, RANK), F32), p...]
    dot_general x4 -> x0, matrix products: 11.9 us -> none  [the longest x1 5.21 us: shards(): approx = jnp.dot(new_q, ortho_t, precision=lax.Precision.HIGHEST)]
    another operation x5 -> x0, other arithmetic: 6.68 us -> none  [the longest x3 3.6 us: shards(): lower = jnp.linalg.cholesky(gram)]
    ppermute x5, waiting for transfers between devices: 5.55 us -> 2.33 us  [shift(): lax.ppermute(array, axis, [(i, (i + step) % size) for i in range(size)])]
    unnamed x8 -> x4, local copies, waits for them, and re-layouts: 0.73 us -> 1.84 us
  transfers between devices with their start and end apart: 5 -> 5, of which waited for: 5 -> 2; matrix products, arithmetic and copies ran while one was open for 0% -> 0% of each run, Pallas kernels for 0% -> 8%
where the time goes in v2:
time: 68.7 us; the launch traced here: 68.5 us
  blocking collectives  39.4 us (57%)
  Pallas kernels  13.9 us (20%)
  starting transfers between devices  10.2 us (15%)
  waiting for transfers between devices  2.33 us (3%)
  local copies, waits for them, and re-layouts  1.87 us (3%)
  between operations  0.72 us (1%)
    all_to_all x1, blocking collectives, sum_everywhere(): block = jnp.sum(lax.all_to_all(repeat(block, Z), 'z', 0, 0), 0)  16 us
    all_to_all x1, blocking collectives, sum_everywhere(): block = jnp.sum(lax.all_to_all(mine, ('x', 'y'), 0, 0), 0)  12.4 us
    all_to_all x1, blocking collectives, sum_everywhere(): mine = lax.all_to_all(repeat(block, BLOCKS), ('x', 'y'), 0, 0)  11 us
    ppermute x5, starting transfers between devices, shift(): lax.ppermute(array, axis, [(i, (i + step) % size) for i in range(size)])  10.2 us
    pallas_call x1, Pallas kernels, factor(): pl.pallas_call(factor_kernel, out_shape=(pltpu.VMEM((RANK, RANK), F32), p...  5.66 us
    pallas_call x1, Pallas kernels, compensate(): pl.pallas_call(compensate_kernel, out_shape=(pltpu.VMEM((ROWS, FEATURES),...  3.78 us
    pallas_call x1, Pallas kernels, apply(): pl.pallas_call(apply_kernel, out_shape=(jax.ShapeDtypeStruct((ROWS, FEATU...  3.62 us
    ppermute x5, waiting for transfers between devices, shift(): lax.ppermute(array, axis, [(i, (i + step) % size) for i in range(size)])  2.33 us
  transfers between devices with their start and end apart: 5, of which 2 were waited for; matrix products, arithmetic and copies ran while one was open for 0% of the time, Pallas kernels for 8%

profile of v2, /device:TPU:1, one launch (start us, length us, event | category | flops | bytes accessed | tf_op | source)
XLA Modules:
  0.0 68.5 jit_solution(16681509528020703509)
XLA Ops:
  0.6 3.8 %compensate.1 = (f32[224,4096]{1,0:T(8,128)S(1)}, bf16[224,4096]{1,0:T(8,128)(2,1)S(1)}, f32[16,16,256]{2,1,0:T(8,128)S(1)}, f32[16,16,256]{2,1,0:T(8,128)S(1)}) custom-call(bf16[224,4096]{1,0:T(8,128)(2,1)} %bitcast.6, f32[224,4096]{1,0:T(8,128)} %bitcast.5, bf16[32,224]{1,0:T(8,128)(2,1)} %bitcast.7), custom_call_target="tpu_custom_call" | custom-call | tf_op jit(solution)/shard_map/compensate/pallas_call | solution.py:78
  4.4 0.0 copy-start
  4.4 1.8 %copy-done = f32[224,4096]{1,0:T(8,128)} copy-done((f32[224,4096]{1,0:T(8,128)}, f32[224,4096]{1,0:T(8,128)S(1)}, u32[]{:S(2)}) %copy-start) | copy-done | bytes 3670040
  6.3 3.2 %collective-permute-start = (f32[16,16,256]{2,1,0:T(8,128)S(1)}, f32[16,16,256]{2,1,0:T(8,128)S(1)}, u32[]{:S(2)}, u32[]{:S(2)}) collective-permute-start(f32[16,16,256]{2,1,0:T(8,128)S(1)} %get-tuple-element.17), channel_id=1, source_target_pairs={{0,1},{1,0},{2,3},{3,2},{4,5},{5,4},{6,7},{7,6},{8,9},{9,8},{10,11... | collective-permute-start | bytes 786440 | tf_op jit(solution)/shard_map/ppermute | solution.py:233
  9.5 1.2 %collective-permute-done = f32[16,16,256]{2,1,0:T(8,128)S(1)} collective-permute-done((f32[16,16,256]{2,1,0:T(8,128)S(1)}, f32[16,16,256]{2,1,0:T(8,128)S(1)}, u32[]{:S(2)}, u32[]{:S(2)}) %collective-permute-start) | collective-permute-done | bytes 262176 | tf_op jit(solution)/shard_map/ppermute | solution.py:233
  10.7 12.4 %all_to_all.15 = f32[16,16,256]{2,1,0:T(8,128)S(1)} all-to-all(f32[16,16,256]{2,1,0:T(8,128)S(1)} %add.3), channel_id=1, replica_groups=mesh['x'=4,'y'=4,'z'=8,'c'=2] {'x','y'}, dimensions={0} | all-to-all | bytes 524288 | tf_op jit(solution)/shard_map/all_to_all | solution.py:242
  23.1 16.0 %all_to_all.16 = f32[8,16,256]{2,1,0:T(8,128)S(1)} all-to-all(f32[8,16,256]{2,1,0:T(8,128)S(1)} %broadcast_in_dim.9), channel_id=1, replica_groups=mesh['x'=4,'y'=4,'z'=8,'c'=2] {'z'}, dimensions={0} | all-to-all | bytes 262144 | tf_op jit(solution)/shard_map/all_to_all | solution.py:243
  39.2 0.0 copy-start.1
  39.2 11.0 %all_to_all.17.mine = f32[16,16,256]{2,1,0:T(8,128)S(1)} all-to-all(f32[16,16,256]{2,1,0:T(8,128)S(1)} %broadcast_in_dim.10), channel_id=1, replica_groups=mesh['x'=4,'y'=4,'z'=8,'c'=2] {'x','y'}, dimensions={0} | all-to-all | bytes 524288 | tf_op jit(solution)/shard_map/all_to_all | solution.py:244
  50.2 4.4 %collective-permute-start.1 = (f32[16,16,256]{2,1,0:T(8,128)S(1)}, f32[16,16,256]{2,1,0:T(8,128)S(1)}, u32[]{:S(2)}, u32[]{:S(2)}) collective-permute-start(f32[16,16,256]{2,1,0:T(8,128)S(1)} %all_to_all.17.mine), channel_id=1, source_target_pairs={{0,1},{1,0},{2,3},{3,2},{4,5},{5,4},{6,7},{7,6},{8,9},{9,8},{10,11... | collective-permute-start | bytes 786440 | tf_op jit(solution)/shard_map/ppermute | solution.py:233
  54.6 1.2 %collective-permute-done.1.other = f32[16,16,256]{2,1,0:T(8,128)S(1)} collective-permute-done((f32[16,16,256]{2,1,0:T(8,128)S(1)}, f32[16,16,256]{2,1,0:T(8,128)S(1)}, u32[]{:S(2)}, u32[]{:S(2)}) %collective-permute-start.1) | collective-permute-done | bytes 262176 | tf_op jit(solution)/shard_map/ppermute | solution.py:233
  55.7 0.9 %project.1 = (f32[32,256]{1,0:T(8,128)S(1)}, bf16[96,4096]{1,0:T(8,128)(2,1)S(1)}) custom-call(bf16[224,4096]{1,0:T(8,128)(2,1)S(1)} %get-tuple-element.15.low, f32[16,16,256]{2,1,0:T(8,128)S(1)} %all_to_all.17.mine, f32[16,16,256]{2,1,0:T(8,128)S(1)} %collective-permute-done.1.other), custom_call_target="tpu_custom_call" | custom-call | tf_op jit(solution)/shard_map/project/pallas_call | solution.py:119
  56.6 0.8 %collective-permute-start.4 = (f32[32,256]{1,0:T(8,128)S(1)}, f32[32,256]{1,0:T(8,128)S(1)}, u32[]{:S(2)}, u32[]{:S(2)}) collective-permute-start(f32[32,256]{1,0:T(8,128)S(1)} %get-tuple-element.18.own), channel_id=1, source_target_pairs={{0,192},{64,0},{128,64},{192,128},{1,193},{65,1},{129,65},{193,129... | collective-permute-start | bytes 98312 | tf_op jit(solution)/shard_map/ppermute | solution.py:233
  57.4 0.7 collective-permute-start.3
  58.1 1.1 %collective-permute-start.2 = (f32[32,256]{1,0:T(8,128)S(1)}, f32[32,256]{1,0:T(8,128)S(1)}, u32[]{:S(2)}, u32[]{:S(2)}) collective-permute-start(f32[32,256]{1,0:T(8,128)S(1)} %get-tuple-element.18.own), channel_id=1, source_target_pairs={{0,128},{64,192},{128,0},{192,64},{1,129},{65,193},{129,1},{193,65... | collective-permute-start | bytes 98312 | tf_op jit(solution)/shard_map/ppermute | solution.py:233
  59.2 5.7 %factor.1 = (f32[32,32]{1,0:T(8,128)S(1)}, bf16[96,4096]{1,0:T(8,128)(2,1)S(1)}) custom-call(bf16[96,4096]{1,0:T(8,128)(2,1)S(1)} %get-tuple-element.19.terms), custom_call_target="tpu_custom_call" | custom-call | flops 1000000000 | bytes 10000000 | tf_op jit(solution)/shard_map/factor/pallas_call | solution.py:172
  64.8 0.0 collective-permute-done.4.right
  64.8 0.0 collective-permute-done.3.left
  64.9 0.0 collective-permute-done.2.across
  64.9 0.0 copy-done.1
  64.9 3.6 %apply.1 = (f32[224,4096]{1,0:T(8,128)}, bf16[224,4096]{1,0:T(8,128)(2,1)}, f32[32,224]{1,0:T(8,128)}) custom-call(f32[224,4096]{1,0:T(8,128)S(1)} %copy-done.1, f32[32,256]{1,0:T(8,128)S(1)} %get-tuple-element.18.own, f32[32,256]{1,0:T(8,128)S(1)} %collective-permute-done.2.across, f32[32,256]{1,0:T(8,128)S(1)} %collective-permute-done.3.left, ...), custom_call_target="tpu_custom_call" | custom-call | tf_op jit(solution)/shard_map/apply/pallas_call | solution.py:212
  (5 shorter events, 0.1 us)
Async XLA Ops:
  4.4 1.8 %copy-start = (f32[224,4096]{1,0:T(8,128)}, f32[224,4096]{1,0:T(8,128)S(1)}, u32[]{:S(2)}) copy-start(f32[224,4096]{1,0:T(8,128)S(1)} %get-tuple-element.14.comp) | copy-start | bytes 11010052
  6.3 4.4 %collective-permute-start = (f32[16,16,256]{2,1,0:T(8,128)S(1)}, f32[16,16,256]{2,1,0:T(8,128)S(1)}, u32[]{:S(2)}, u32[]{:S(2)}) collective-permute-start(f32[16,16,256]{2,1,0:T(8,128)S(1)} %get-tuple-element.17), channel_id=1, source_target_pairs={{0,1},{1,0},{2,3},{3,2},{4,5},{5,4},{6,7},{7,6},{8,9},{9,8},{10,11... | collective-permute-start | bytes 786440 | tf_op jit(solution)/shard_map/ppermute | solution.py:233
  39.2 25.7 %copy-start.1 = (f32[224,4096]{1,0:T(8,128)S(1)}, f32[224,4096]{1,0:T(8,128)}, u32[]{:S(2)}) copy-start(f32[224,4096]{1,0:T(8,128)} %copy-done) | copy-start | bytes 11010052
  50.2 5.5 %collective-permute-start.1 = (f32[16,16,256]{2,1,0:T(8,128)S(1)}, f32[16,16,256]{2,1,0:T(8,128)S(1)}, u32[]{:S(2)}, u32[]{:S(2)}) collective-permute-start(f32[16,16,256]{2,1,0:T(8,128)S(1)} %all_to_all.17.mine), channel_id=1, source_target_pairs={{0,1},{1,0},{2,3},{3,2},{4,5},{5,4},{6,7},{7,6},{8,9},{9,8},{10,11... | collective-permute-start | bytes 786440 | tf_op jit(solution)/shard_map/ppermute | solution.py:233
  56.6 8.2 %collective-permute-start.4 = (f32[32,256]{1,0:T(8,128)S(1)}, f32[32,256]{1,0:T(8,128)S(1)}, u32[]{:S(2)}, u32[]{:S(2)}) collective-permute-start(f32[32,256]{1,0:T(8,128)S(1)} %get-tuple-element.18.own), channel_id=1, source_target_pairs={{0,192},{64,0},{128,64},{192,128},{1,193},{65,1},{129,65},{193,129... | collective-permute-start | bytes 98312 | tf_op jit(solution)/shard_map/ppermute | solution.py:233
  57.4 7.4 %collective-permute-start.3 = (f32[32,256]{1,0:T(8,128)S(1)}, f32[32,256]{1,0:T(8,128)S(1)}, u32[]{:S(2)}, u32[]{:S(2)}) collective-permute-start(f32[32,256]{1,0:T(8,128)S(1)} %get-tuple-element.18.own), channel_id=1, source_target_pairs={{0,64},{64,128},{128,192},{192,0},{1,65},{65,129},{129,193},{193,1... | collective-permute-start | bytes 98312 | tf_op jit(solution)/shard_map/ppermute | solution.py:233
  58.1 6.7 %collective-permute-start.2 = (f32[32,256]{1,0:T(8,128)S(1)}, f32[32,256]{1,0:T(8,128)S(1)}, u32[]{:S(2)}, u32[]{:S(2)}) collective-permute-start(f32[32,256]{1,0:T(8,128)S(1)} %get-tuple-element.18.own), channel_id=1, source_target_pairs={{0,128},{64,192},{128,0},{192,64},{1,129},{65,193},{129,1},{193,65... | collective-permute-start | bytes 98312 | tf_op jit(solution)/shard_map/ppermute | solution.py:233

commit v3 on v2

--- a/solution.py
+++ b/solution.py
@@ -14,10 +14,11 @@
 FEATURES = 4096
 BLOCKS = X * Y
 BLOCK = FEATURES // BLOCKS
-CHUNKS = 8
+CHUNKS = 4
+GROUP = 8
 WIDTH = FEATURES // CHUNKS
 F32, BF16 = jnp.float32, jnp.bfloat16
-VMEM_LIMIT = 40 * 2**20
+VMEM_LIMIT = 20 * 2**20
 
 
 def columns(chunk):
@@ -127,18 +128,41 @@
 
 
 def inverse_of_lower(gram):
+    shape = (GROUP, 2 * RANK)
+    groups = RANK // GROUP
     row = lax.broadcasted_iota(jnp.int32, (RANK, RANK), 0)
     column = lax.broadcasted_iota(jnp.int32, (RANK, RANK), 1)
-    work = jnp.concatenate([gram, (row == column).astype(F32)], axis=1)
-    index = lax.broadcasted_iota(jnp.int32, (RANK, 2 * RANK), 0)
-    scale = jnp.zeros((RANK, 2 * RANK), F32)
-    for step in range(RANK):
-        pivot_row = jnp.broadcast_to(work[step : step + 1, :], work.shape)
-        pivot = jnp.broadcast_to(work[step : step + 1, step : step + 1], work.shape)
-        multiplier = jnp.broadcast_to(work[:, step : step + 1], work.shape) / pivot
-        scale = jnp.where(index == step, pivot, scale)
-        work = jnp.where(index > step, work - multiplier * pivot_row, work)
-    return (work / jnp.sqrt(scale))[:, RANK:]
+    whole = jnp.concatenate([gram, (row == column).astype(F32)], axis=1)
+    work = [whole[g * GROUP : (g + 1) * GROUP] for g in range(groups)]
+    index = lax.broadcasted_iota(jnp.int32, shape, 0)
+    scale = [jnp.zeros(shape, F32) for _ in range(groups)]
+    inside = range(GROUP)
+    for g in range(groups):
+        rows = [jnp.broadcast_to(work[g][p : p + 1, :], shape) for p in inside]
+        cols = [
+            [jnp.broadcast_to(work[i][:, g * GROUP + p : g * GROUP + p + 1], shape) for i in range(g, groups)]
+            for p in inside
+        ]
+        entry = {
+            (q, p): jnp.broadcast_to(cols[p][0][q : q + 1, :], shape) for p in inside for q in range(p, GROUP)
+        }
+        for p in inside:
+            reciprocal = 1.0 / entry[p, p]
+            scale[g] = jnp.where(index == p, entry[p, p], scale[g])
+            for q in range(p + 1, GROUP):
+                multiplier = entry[q, p] * reciprocal
+                for t in range(q, GROUP):
+                    entry[t, q] = entry[t, q] - multiplier * entry[t, p]
+                rows[q] = rows[q] - multiplier * rows[p]
+                cols[q] = [mine - multiplier * pivot for mine, pivot in zip(cols[q], cols[p])]
+            rows[p] = rows[p] * reciprocal
+        for i in range(g, groups):
+            for p in inside:
+                factor = cols[p][i - g]
+                if i == g:
+                    factor = jnp.where(index > p, factor, 0.0)
+                work[i] = work[i] - factor * rows[p]
+    return jnp.concatenate([w * lax.rsqrt(d) for w, d in zip(work, scale)])[:, RANK:]
 
 
 def factor_kernel(terms, inverse, ortho):
@@ -233,14 +257,21 @@
     return lax.ppermute(array, axis, [(i, (i + step) % size) for i in range(size)])
 
 
+def add_up(blocks):
+    terms = [blocks[i] for i in range(blocks.shape[0])]
+    while len(terms) > 1:
+        terms = [left + right for left, right in zip(terms[::2], terms[1::2])]
+    return terms[0]
+
+
 def repeat(block, times):
     return jnp.broadcast_to(block, (times,) + block.shape)
 
 
 def sum_everywhere(mine, other):
     mine = mine + shift(other, "c", C, 1)
-    block = jnp.sum(lax.all_to_all(mine, ("x", "y"), 0, 0), 0)
-    block = jnp.sum(lax.all_to_all(repeat(block, Z), "z", 0, 0), 0)
+    block = add_up(lax.all_to_all(mine, ("x", "y"), 0, 0))
+    block = add_up(lax.all_to_all(repeat(block, Z), "z", 0, 0))
     mine = lax.all_to_all(repeat(block, BLOCKS), ("x", "y"), 0, 0)
     return mine, shift(mine, "c", C, 1)
 

time: 68.7 us -> 63.6 us (0.926)
  Pallas kernels: 13.9 us -> 10.1 us
  local copies, waits for them, and re-layouts: 1.87 us -> 0.03 us
    pallas_call x1, Pallas kernels: 5.66 us -> 2.56 us  [factor(): pl.pallas_call(factor_kernel, out_shape=(pltpu.VMEM((RANK, RANK), F32), p...]
    unnamed x4 -> x0, local copies, waits for them, and re-layouts: 1.84 us -> none
    pallas_call x1, Pallas kernels: 3.78 us -> 3.06 us  [compensate(): pl.pallas_call(compensate_kernel, out_shape=(pltpu.VMEM((ROWS, FEATURES),...]
  transfers between devices with their start and end apart: 5 -> 5, of which waited for: 2 -> 3; matrix products, arithmetic and copies ran while one was open for 0% -> 0% of each run, Pallas kernels for 8% -> 4%
where the time goes in v3:
time: 63.6 us; the launch traced here: 63.3 us
  blocking collectives  39.1 us (61%)
  starting transfers between devices  10.3 us (16%)
  Pallas kernels  10.1 us (16%)
  waiting for transfers between devices  2.98 us (5%)
  between operations  0.69 us (1%)
    all_to_all x1, blocking collectives, sum_everywhere(): block = add_up(lax.all_to_all(repeat(block, Z), 'z', 0, 0))  16 us
    all_to_all x1, blocking collectives, sum_everywhere(): block = add_up(lax.all_to_all(mine, ('x', 'y'), 0, 0))  12.4 us
    all_to_all x1, blocking collectives, sum_everywhere(): mine = lax.all_to_all(repeat(block, BLOCKS), ('x', 'y'), 0, 0)  10.7 us
    ppermute x5, starting transfers between devices, shift(): lax.ppermute(array, axis, [(i, (i + step) % size) for i in range(size)])  10.3 us
    pallas_call x1, Pallas kernels, apply(): pl.pallas_call(apply_kernel, out_shape=(jax.ShapeDtypeStruct((ROWS, FEATU...  3.63 us
    pallas_call x1, Pallas kernels, compensate(): pl.pallas_call(compensate_kernel, out_shape=(pltpu.VMEM((ROWS, FEATURES),...  3.06 us
    ppermute x5, waiting for transfers between devices, shift(): lax.ppermute(array, axis, [(i, (i + step) % size) for i in range(size)])  2.98 us
    pallas_call x1, Pallas kernels, factor(): pl.pallas_call(factor_kernel, out_shape=(pltpu.VMEM((RANK, RANK), F32), p...  2.56 us
  transfers between devices with their start and end apart: 5, of which 3 were waited for; matrix products, arithmetic and copies ran while one was open for 0% of the time, Pallas kernels for 4%

profile of v3, /device:TPU:1, one launch (start us, length us, event | category | flops | bytes accessed | tf_op | source)
XLA Modules:
  0.0 63.3 jit_solution(14451649173345403387)
XLA Ops:
  0.6 3.1 %compensate.1 = (f32[224,4096]{1,0:T(8,128)S(1)}, bf16[224,4096]{1,0:T(8,128)(2,1)S(1)}, f32[16,16,256]{2,1,0:T(8,128)S(1)}, f32[16,16,256]{2,1,0:T(8,128)S(1)}) custom-call(bf16[224,4096]{1,0:T(8,128)(2,1)} %bitcast.10, f32[224,4096]{1,0:T(8,128)} %bitcast.9, bf16[32,224]{1,0:T(8,128)(2,1)} %bitcast.11), custom_call_target="tpu_custom_call" | custom-call | tf_op jit(solution)/shard_map/compensate/pallas_call | solution.py:79
  3.7 3.3 %collective-permute-start = (f32[16,16,256]{2,1,0:T(8,128)S(1)}, f32[16,16,256]{2,1,0:T(8,128)S(1)}, u32[]{:S(2)}, u32[]{:S(2)}) collective-permute-start(f32[16,16,256]{2,1,0:T(8,128)S(1)} %get-tuple-element.17), channel_id=1, source_target_pairs={{0,1},{1,0},{2,3},{3,2},{4,5},{5,4},{6,7},{7,6},{8,9},{9,8},{10,11... | collective-permute-start | bytes 786440 | tf_op jit(solution)/shard_map/ppermute | solution.py:257
  7.0 1.2 %collective-permute-done = f32[16,16,256]{2,1,0:T(8,128)S(1)} collective-permute-done((f32[16,16,256]{2,1,0:T(8,128)S(1)}, f32[16,16,256]{2,1,0:T(8,128)S(1)}, u32[]{:S(2)}, u32[]{:S(2)}) %collective-permute-start) | collective-permute-done | bytes 262176 | tf_op jit(solution)/shard_map/ppermute | solution.py:257
  8.2 12.4 %all_to_all.15 = f32[16,16,256]{2,1,0:T(8,128)S(1)} all-to-all(f32[16,16,256]{2,1,0:T(8,128)S(1)} %add.95), channel_id=1, replica_groups=mesh['x'=4,'y'=4,'z'=8,'c'=2] {'x','y'}, dimensions={0} | all-to-all | bytes 524288 | tf_op jit(solution)/shard_map/all_to_all | solution.py:273
  20.6 16.0 %all_to_all.16 = f32[8,16,256]{2,1,0:T(8,128)S(1)} all-to-all(f32[8,16,256]{2,1,0:T(8,128)S(1)} %broadcast_in_dim.9), channel_id=1, replica_groups=mesh['x'=4,'y'=4,'z'=8,'c'=2] {'z'}, dimensions={0} | all-to-all | bytes 262144 | tf_op jit(solution)/shard_map/all_to_all | solution.py:274
  36.7 10.7 %all_to_all.17.mine = f32[16,16,256]{2,1,0:T(8,128)S(1)} all-to-all(f32[16,16,256]{2,1,0:T(8,128)S(1)} %broadcast_in_dim.10), channel_id=1, replica_groups=mesh['x'=4,'y'=4,'z'=8,'c'=2] {'x','y'}, dimensions={0} | all-to-all | bytes 524288 | tf_op jit(solution)/shard_map/all_to_all | solution.py:275
  47.4 4.4 %collective-permute-start.1 = (f32[16,16,256]{2,1,0:T(8,128)S(1)}, f32[16,16,256]{2,1,0:T(8,128)S(1)}, u32[]{:S(2)}, u32[]{:S(2)}) collective-permute-start(f32[16,16,256]{2,1,0:T(8,128)S(1)} %all_to_all.17.mine), channel_id=1, source_target_pairs={{0,1},{1,0},{2,3},{3,2},{4,5},{5,4},{6,7},{7,6},{8,9},{9,8},{10,11... | collective-permute-start | bytes 786440 | tf_op jit(solution)/shard_map/ppermute | solution.py:257
  51.8 1.2 %collective-permute-done.1.other = f32[16,16,256]{2,1,0:T(8,128)S(1)} collective-permute-done((f32[16,16,256]{2,1,0:T(8,128)S(1)}, f32[16,16,256]{2,1,0:T(8,128)S(1)}, u32[]{:S(2)}, u32[]{:S(2)}) %collective-permute-start.1) | collective-permute-done | bytes 262176 | tf_op jit(solution)/shard_map/ppermute | solution.py:257
  53.0 0.9 %project.1 = (f32[32,256]{1,0:T(8,128)S(1)}, bf16[96,4096]{1,0:T(8,128)(2,1)S(1)}) custom-call(bf16[224,4096]{1,0:T(8,128)(2,1)S(1)} %get-tuple-element.15.low, f32[16,16,256]{2,1,0:T(8,128)S(1)} %all_to_all.17.mine, f32[16,16,256]{2,1,0:T(8,128)S(1)} %collective-permute-done.1.other), custom_call_target="tpu_custom_call" | custom-call | tf_op jit(solution)/shard_map/project/pallas_call | solution.py:120
  53.9 0.8 %collective-permute-start.4 = (f32[32,256]{1,0:T(8,128)S(1)}, f32[32,256]{1,0:T(8,128)S(1)}, u32[]{:S(2)}, u32[]{:S(2)}) collective-permute-start(f32[32,256]{1,0:T(8,128)S(1)} %get-tuple-element.18.own), channel_id=1, source_target_pairs={{0,192},{64,0},{128,64},{192,128},{1,193},{65,1},{129,65},{193,129... | collective-permute-start | bytes 98312 | tf_op jit(solution)/shard_map/ppermute | solution.py:257
  54.7 0.7 %collective-permute-start.3 = (f32[32,256]{1,0:T(8,128)S(1)}, f32[32,256]{1,0:T(8,128)S(1)}, u32[]{:S(2)}, u32[]{:S(2)}) collective-permute-start(f32[32,256]{1,0:T(8,128)S(1)} %get-tuple-element.18.own), channel_id=1, source_target_pairs={{0,64},{64,128},{128,192},{192,0},{1,65},{65,129},{129,193},{193,1... | collective-permute-start | bytes 98312 | tf_op jit(solution)/shard_map/ppermute | solution.py:257
  55.4 1.1 %collective-permute-start.2 = (f32[32,256]{1,0:T(8,128)S(1)}, f32[32,256]{1,0:T(8,128)S(1)}, u32[]{:S(2)}, u32[]{:S(2)}) collective-permute-start(f32[32,256]{1,0:T(8,128)S(1)} %get-tuple-element.18.own), channel_id=1, source_target_pairs={{0,128},{64,192},{128,0},{192,64},{1,129},{65,193},{129,1},{193,65... | collective-permute-start | bytes 98312 | tf_op jit(solution)/shard_map/ppermute | solution.py:257
  56.4 2.6 %factor.1 = (f32[32,32]{1,0:T(8,128)S(1)}, bf16[96,4096]{1,0:T(8,128)(2,1)S(1)}) custom-call(bf16[96,4096]{1,0:T(8,128)(2,1)S(1)} %get-tuple-element.19.terms), custom_call_target="tpu_custom_call" | custom-call | flops 1000000000 | bytes 10000000 | tf_op jit(solution)/shard_map/factor/pallas_call | solution.py:196
  59.0 0.0 collective-permute-done.4.right
  59.0 0.0 collective-permute-done.3.left
  59.0 0.6 %collective-permute-done.2.across = f32[32,256]{1,0:T(8,128)S(1)} collective-permute-done((f32[32,256]{1,0:T(8,128)S(1)}, f32[32,256]{1,0:T(8,128)S(1)}, u32[]{:S(2)}, u32[]{:S(2)}) %collective-permute-start.2) | collective-permute-done | bytes 32800 | tf_op jit(solution)/shard_map/ppermute | solution.py:257
  59.7 3.6 %apply.1 = (f32[224,4096]{1,0:T(8,128)}, bf16[224,4096]{1,0:T(8,128)(2,1)}, f32[32,224]{1,0:T(8,128)}) custom-call(f32[224,4096]{1,0:T(8,128)S(1)} %get-tuple-element.14.comp, f32[32,256]{1,0:T(8,128)S(1)} %get-tuple-element.18.own, f32[32,256]{1,0:T(8,128)S(1)} %collective-permute-done.2.across, f32[32,256]{1,0:T(8,128)S(1)} %collective-permute-done.3.left, ...), custom_call_target="tpu_custom_call" | custom-call | tf_op jit(solution)/shard_map/apply/pallas_call | solution.py:236
  (5 shorter events, 0.1 us)
Async XLA Ops:
  3.7 4.5 %collective-permute-start = (f32[16,16,256]{2,1,0:T(8,128)S(1)}, f32[16,16,256]{2,1,0:T(8,128)S(1)}, u32[]{:S(2)}, u32[]{:S(2)}) collective-permute-start(f32[16,16,256]{2,1,0:T(8,128)S(1)} %get-tuple-element.17), channel_id=1, source_target_pairs={{0,1},{1,0},{2,3},{3,2},{4,5},{5,4},{6,7},{7,6},{8,9},{9,8},{10,11... | collective-permute-start | bytes 786440 | tf_op jit(solution)/shard_map/ppermute | solution.py:257
  47.4 5.5 %collective-permute-start.1 = (f32[16,16,256]{2,1,0:T(8,128)S(1)}, f32[16,16,256]{2,1,0:T(8,128)S(1)}, u32[]{:S(2)}, u32[]{:S(2)}) collective-permute-start(f32[16,16,256]{2,1,0:T(8,128)S(1)} %all_to_all.17.mine), channel_id=1, source_target_pairs={{0,1},{1,0},{2,3},{3,2},{4,5},{5,4},{6,7},{7,6},{8,9},{9,8},{10,11... | collective-permute-start | bytes 786440 | tf_op jit(solution)/shard_map/ppermute | solution.py:257
  53.9 5.1 %collective-permute-start.4 = (f32[32,256]{1,0:T(8,128)S(1)}, f32[32,256]{1,0:T(8,128)S(1)}, u32[]{:S(2)}, u32[]{:S(2)}) collective-permute-start(f32[32,256]{1,0:T(8,128)S(1)} %get-tuple-element.18.own), channel_id=1, source_target_pairs={{0,192},{64,0},{128,64},{192,128},{1,193},{65,1},{129,65},{193,129... | collective-permute-start | bytes 98312 | tf_op jit(solution)/shard_map/ppermute | solution.py:257
  54.7 4.3 %collective-permute-start.3 = (f32[32,256]{1,0:T(8,128)S(1)}, f32[32,256]{1,0:T(8,128)S(1)}, u32[]{:S(2)}, u32[]{:S(2)}) collective-permute-start(f32[32,256]{1,0:T(8,128)S(1)} %get-tuple-element.18.own), channel_id=1, source_target_pairs={{0,64},{64,128},{128,192},{192,0},{1,65},{65,129},{129,193},{193,1... | collective-permute-start | bytes 98312 | tf_op jit(solution)/shard_map/ppermute | solution.py:257
  55.4 4.3 %collective-permute-start.2 = (f32[32,256]{1,0:T(8,128)S(1)}, f32[32,256]{1,0:T(8,128)S(1)}, u32[]{:S(2)}, u32[]{:S(2)}) collective-permute-start(f32[32,256]{1,0:T(8,128)S(1)} %get-tuple-element.18.own), channel_id=1, source_target_pairs={{0,128},{64,192},{128,0},{192,64},{1,129},{65,193},{129,1},{193,65... | collective-permute-start | bytes 98312 | tf_op jit(solution)/shard_map/ppermute | solution.py:257

commit v4 on v3

v4 whole, which is shorter than its diff:
```python
import functools

import jax
import jax.numpy as jnp
from jax import lax
from jax.experimental import pallas as pl
from jax.experimental.pallas import tpu as pltpu
from jax.sharding import Mesh
from jax.sharding import PartitionSpec as P

X, Y, Z, C = 4, 4, 8, 2
RANK = 32
ROWS = 224
PAD = 256
FEATURES = 4096
HALF = FEATURES // C
BLOCKS = X * Y
BLOCK = HALF // BLOCKS
CHUNKS = 2
WIDTH = HALF // CHUNKS
GROUP = 8
F32, BF16 = jnp.float32, jnp.bfloat16
CONTRACT_LAST = (((1,), (1,)), ((), ()))
VMEM = pl.BlockSpec(memory_space=pltpu.VMEM)
HBM = pl.BlockSpec(memory_space=pltpu.HBM)


def half_start(own):
    core = lax.axis_index("c")
    return (core if own else 1 - core) * HALF


def in_hbm(start, chunk):
    return pl.ds(pl.multiple_of(start + chunk * WIDTH, WIDTH), WIDTH)


def in_half(chunk):
    return slice(chunk * WIDTH, (chunk + 1) * WIDTH)


def params(mebibytes):
    return pltpu.CompilerParams(vmem_limit_bytes=mebibytes * 2**20)


def two_terms(value):
    high = value.astype(BF16)
    return high, (value - high.astype(F32)).astype(BF16)


def three_terms(value):
    high = value.astype(BF16)
    rest = value - high.astype(F32)
    middle = rest.astype(BF16)
    return high, middle, (rest - middle.astype(F32)).astype(BF16)


def compensate_kernel(
    own, grads, errors, q_hbm, comp, low, partial, grad_buf, q_t, q_sem, grad_sems, error_sems
):
    start = half_start(own)
    copies = []
    for chunk in range(CHUNKS):
        at, cols = in_hbm(start, chunk), in_half(chunk)
        pair = (
            pltpu.make_async_copy(grads.at[:, at], grad_buf.at[:, cols], grad_sems.at[chunk]),
            pltpu.make_async_copy(errors.at[:, at], comp.at[:, cols], error_sems.at[chunk]),
        )
        for copy in pair:
            copy.start()
        copies.append(pair)
    q_copy = pltpu.make_async_copy(q_hbm, q_t, q_sem)
    q_copy.start()
    q_copy.wait()
    factor = q_t[...]
    for chunk in range(CHUNKS):
        for copy in copies[chunk]:
            copy.wait()
        cols = in_half(chunk)
        total = grad_buf[:, cols].astype(F32) + comp[:, cols]
        comp[:, cols] = total
        rounded = total.astype(BF16)
        low[:, cols] = rounded
        product = jnp.dot(factor, rounded, preferred_element_type=F32)
        for part in range(WIDTH // BLOCK):
            partial[chunk * (WIDTH // BLOCK) + part] = product[:, part * BLOCK : (part + 1) * BLOCK]


def compensate(grads, errors, q_t, own):
    operands = [pltpu.with_memory_space_constraint(a, pltpu.HBM) for a in (grads, errors, q_t)]
    return pl.pallas_call(
        functools.partial(compensate_kernel, own),
        out_shape=(
            pltpu.VMEM((ROWS, HALF), F32),
            pltpu.VMEM((ROWS, HALF), BF16),
            pltpu.VMEM((BLOCKS, RANK, BLOCK), F32),
        ),
        in_specs=[HBM] * 3,
        out_specs=[VMEM] * 3,
        scratch_shapes=[
            pltpu.VMEM((ROWS, HALF), BF16),
            pltpu.VMEM((RANK, ROWS), BF16),
            pltpu.SemaphoreType.DMA,
            pltpu.SemaphoreType.DMA((CHUNKS,)),
            pltpu.SemaphoreType.DMA((CHUNKS,)),
        ],
        compiler_params=params(12),
        cost_estimate=pl.CostEstimate(
            flops=2 * ROWS * HALF * RANK, bytes_accessed=6 * ROWS * HALF, transcendentals=0
        ),
        name="compensate_own" if own else "compensate_other",
    )(*operands)


def project_kernel(low, blocks, *refs):
    product, terms = refs[-2:]
    for block in range(BLOCKS):
        cols = slice(block * BLOCK, (block + 1) * BLOCK)
        for term, value in enumerate(three_terms(blocks[block])):
            terms[term * RANK : (term + 1) * RANK, cols] = value
    stacked = lax.dot_general(terms[...], low[...], CONTRACT_LAST, preferred_element_type=F32)
    total = stacked[:RANK] + (stacked[RANK : 2 * RANK] + stacked[2 * RANK :])
    if len(refs) == 3:
        total = total + refs[0][:, :ROWS]
    product[...] = jnp.zeros(product.shape, F32)
    product[:, :ROWS] = total


def project(low, blocks, *before):
    return pl.pallas_call(
        project_kernel,
        out_shape=(pltpu.VMEM((RANK, PAD), F32), pltpu.VMEM((3 * RANK, HALF), BF16)),
        in_specs=[VMEM] * (2 + len(before)),
        out_specs=[VMEM] * 2,
        compiler_params=params(12),
        cost_estimate=pl.CostEstimate(
            flops=6 * ROWS * HALF * RANK, bytes_accessed=2 * ROWS * HALF, transcendentals=0
        ),
        name="project",
    )(pltpu.with_memory_space_constraint(low, pltpu.VMEM), blocks, *before)


def inverse_of_lower(gram):
    shape = (GROUP, 2 * RANK)
    groups = RANK // GROUP
    row = lax.broadcasted_iota(jnp.int32, (RANK, RANK), 0)
    column = lax.broadcasted_iota(jnp.int32, (RANK, RANK), 1)
    whole = jnp.concatenate([gram, (row == column).astype(F32)], axis=1)
    work = [whole[g * GROUP : (g + 1) * GROUP] for g in range(groups)]
    index = lax.broadcasted_iota(jnp.int32, shape, 0)
    scale = [jnp.zeros(shape, F32) for _ in range(groups)]
    inside = range(GROUP)
    for g in range(groups):
        rows = [jnp.broadcast_to(work[g][p : p + 1, :], shape) for p in inside]
        cols = [
            [jnp.broadcast_to(work[i][:, g * GROUP + p : g * GROUP + p + 1], shape) for i in range(g, groups)]
            for p in inside
        ]
        entry = {
            (q, p): jnp.broadcast_to(cols[p][0][q : q + 1, :], shape) for p in inside for q in range(p, GROUP)
        }
        for p in inside:
            reciprocal = 1.0 / entry[p, p]
            scale[g] = jnp.where(index == p, entry[p, p], scale[g])
            for q in range(p + 1, GROUP):
                multiplier = entry[q, p] * reciprocal
                for t in range(q, GROUP):
                    entry[t, q] = entry[t, q] - multiplier * entry[t, p]
                rows[q] = rows[q] - multiplier * rows[p]
                cols[q] = [mine - multiplier * pivot for mine, pivot in zip(cols[q], cols[p])]
            rows[p] = rows[p] * reciprocal
        for i in range(g, groups):
            for p in inside:
                factor = cols[p][i - g]
                if i == g:
                    factor = jnp.where(index > p, factor, 0.0)
                work[i] = work[i] - factor * rows[p]
    return jnp.concatenate([w * lax.rsqrt(d) for w, d in zip(work, scale)])[:, RANK:]


def factor_kernel(own_terms, other_terms, inverse, own_ortho, other_ortho):
    stacked = sum(
        lax.dot_general(terms[...], terms[...], CONTRACT_LAST, preferred_element_type=F32)
        for terms in (own_terms, other_terms)
    )

    def part(left, right):
        return stacked[left * RANK : (left + 1) * RANK, right * RANK : (right + 1) * RANK]

    small = part(0, 2) + part(2, 0) + part(1, 1)
    gram = part(0, 0) + ((part(0, 1) + part(1, 0)) + small)
    lower_inverse = inverse_of_lower(gram)
    inverse[...] = lower_inverse
    for terms, ortho in ((own_terms, own_ortho), (other_terms, other_ortho)):
        for chunk in range(CHUNKS):
            cols = in_half(chunk)
            p_t = (
                terms[:RANK, cols].astype(F32)
                + terms[RANK : 2 * RANK, cols].astype(F32)
                + terms[2 * RANK :, cols].astype(F32)
            )
            ortho_t = jnp.dot(
                lower_inverse, p_t, precision=lax.Precision.HIGHEST, preferred_element_type=F32
            )
            high, low = two_terms(ortho_t)
            ortho[:RANK, cols] = high
            ortho[RANK : 2 * RANK, cols] = low
            ortho[2 * RANK :, cols] = high


def factor(own_terms, other_terms):
    ortho = pltpu.VMEM((3 * RANK, HALF), BF16)
    return pl.pallas_call(
        factor_kernel,
        out_shape=(pltpu.VMEM((RANK, RANK), F32), ortho, ortho),
        in_specs=[VMEM] * 2,
        out_specs=[VMEM] * 3,
        compiler_params=params(12),
        cost_estimate=pl.CostEstimate(flops=10**9, bytes_accessed=10**7, transcendentals=0),
        name="factor",
    )(own_terms, other_terms)


def apply_kernel(
    own_comp,
    other_comp,
    own,
    across,
    left,
    right,
    inverse,
    own_ortho,
    other_ortho,
    new_errors,
    update,
    new_q,
    error_buf,
    update_buf,
    q_buf,
    error_sems,
    update_sems,
    q_sem,
):
    total = (own[...] + across[...]) + (left[...] + right[...])
    q_t = jnp.dot(
        inverse[...], total * (1.0 / X), precision=lax.Precision.HIGHEST, preferred_element_type=F32
    )
    q_buf[...] = q_t[:, :ROWS]
    copies = [pltpu.make_async_copy(q_buf, new_q, q_sem)]
    copies[0].start()
    high = q_t.astype(BF16).astype(F32)
    stacked = jnp.concatenate([high, high, q_t - high]).T[:ROWS].astype(BF16)
    for half, (comp, ortho) in enumerate(((own_comp, own_ortho), (other_comp, other_ortho))):
        start = half_start(half == 0)
        for chunk in range(CHUNKS):
            cols, at = in_half(chunk), in_hbm(start, chunk)
            approx = jnp.dot(stacked, ortho[:, cols], preferred_element_type=F32)
            error_buf[half, :, cols] = comp[:, cols] - approx
            update_buf[half, :, cols] = approx.astype(BF16)
            pair = [
                pltpu.make_async_copy(
                    error_buf.at[half, :, cols], new_errors.at[:, at], error_sems.at[half, chunk]
                ),
                pltpu.make_async_copy(
                    update_buf.at[half, :, cols], update.at[:, at], update_sems.at[half, chunk]
                ),
            ]
            for copy in pair:
                copy.start()
            copies += pair
    for copy in copies:
        copy.wait()


def apply(own_comp, other_comp, own, across, left, right, inverse, own_ortho, other_ortho):
    comps = [pltpu.with_memory_space_constraint(a, pltpu.VMEM) for a in (own_comp, other_comp)]
    return pl.pallas_call(
        apply_kernel,
        out_shape=(
            jax.ShapeDtypeStruct((ROWS, FEATURES), F32),
            jax.ShapeDtypeStruct((ROWS, FEATURES), BF16),
            jax.ShapeDtypeStruct((RANK, ROWS), F32),
        ),
        in_specs=[VMEM] * 9,
        out_specs=[HBM] * 3,
        scratch_shapes=[
            pltpu.VMEM((C, ROWS, HALF), F32),
            pltpu.VMEM((C, ROWS, HALF), BF16),
            pltpu.VMEM((RANK, ROWS), F32),
            pltpu.SemaphoreType.DMA((C, CHUNKS)),
            pltpu.SemaphoreType.DMA((C, CHUNKS)),
            pltpu.SemaphoreType.DMA,
        ],
        compiler_params=params(20),
        name="apply",
    )(*comps, own, across, left, right, inverse, own_ortho, other_ortho)


def shift(array, axis, size, step):
    return lax.ppermute(array, axis, [(i, (i + step) % size) for i in range(size)])


def add_up(blocks):
    terms = [blocks[i] for i in range(blocks.shape[0])]
    while len(terms) > 1:
        terms = [left + right for left, right in zip(terms[::2], terms[1::2])]
    return terms[0]


def repeat(block, times):
    return jnp.broadcast_to(block, (times,) + block.shape)


def reduce_and_gather(mine):
    block = add_up(lax.all_to_all(mine, ("x", "y"), 0, 0))
    block = add_up(lax.all_to_all(repeat(block, Z), "z", 0, 0))
    return lax.all_to_all(repeat(block, BLOCKS), ("x", "y"), 0, 0)


def shards(grads, errors, q_start):
    q_t = q_start.T
    other_comp, other_low, other = compensate(grads[0], errors[0], q_t, False)
    received = shift(other, "c", C, 1)
    own_comp, own_low, mine = compensate(grads[0], errors[0], q_t, True)
    mine = reduce_and_gather(mine + received)
    other = shift(mine, "c", C, 1)
    product, own_terms = project(own_low, mine)
    product, other_terms = project(other_low, other, product)
    across, left, right = (shift(product, "x", X, step) for step in (2, 1, 3))
    inverse, own_ortho, other_ortho = factor(own_terms, other_terms)
    new_errors, update, new_q = apply(
        own_comp, other_comp, product, across, left, right, inverse, own_ortho, other_ortho
    )
    return (update, new_errors[None], new_q.T)


def solution(mesh):
    split = Mesh(mesh.devices.reshape(X, Y, Z, C), ("x", "y", "z", "c"))
    rows = ("y", "z", "c")
    return jax.shard_map(
        shards,
        mesh=split,
        in_specs=(P("x", rows, None), P("x", rows, None), P(rows, None)),
        out_specs=(P(rows, None), P("x", rows, None), P(rows, None)),
        check_vma=False,
    )
```

time: 63.6 us -> 62.7 us (0.986)
  waiting for transfers between devices: 2.98 us -> 1.4 us
    ppermute x5, waiting for transfers between devices: 2.98 us -> 1.4 us  [shift(): lax.ppermute(array, axis, [(i, (i + step) % size) for i in range(size)])]
    pallas_call x2 -> x3, Pallas kernels: 5.62 us -> 6.73 us  [the longest x2 4.17 us: compensate(): pl.pallas_call(functools.partial(compensate_kernel, own), out_shape=(pltp...]
  transfers between devices with their start and end apart: 5 -> 5, of which waited for: 3 -> 2; matrix products, arithmetic and copies ran while one was open for 0% -> 0% of each run, Pallas kernels for 4% -> 8%
where the time goes in v4:
time: 62.7 us; the launch traced here: 62.2 us
  blocking collectives  39.7 us (63%)
  Pallas kernels  10.6 us (17%)
  starting transfers between devices  9.71 us (15%)
  waiting for transfers between devices  1.4 us (2%)
  between operations  0.71 us (1%)
    all_to_all x1, blocking collectives, reduce_and_gather(): block = add_up(lax.all_to_all(repeat(block, Z), 'z', 0, 0))  16 us
    all_to_all x1, blocking collectives, reduce_and_gather(): block = add_up(lax.all_to_all(mine, ('x', 'y'), 0, 0))  12.6 us
    all_to_all x1, blocking collectives, reduce_and_gather(): return lax.all_to_all(repeat(block, BLOCKS), ('x', 'y'), 0, 0)  11.1 us
    ppermute x5, starting transfers between devices, shift(): lax.ppermute(array, axis, [(i, (i + step) % size) for i in range(size)])  9.71 us
    pallas_call x2, Pallas kernels, compensate(): pl.pallas_call(functools.partial(compensate_kernel, own), out_shape=(pltp...  4.17 us
    pallas_call x1, Pallas kernels, apply(): pl.pallas_call(apply_kernel, out_shape=(jax.ShapeDtypeStruct((ROWS, FEATU...  3.03 us
    pallas_call x1, Pallas kernels, factor(): pl.pallas_call(factor_kernel, out_shape=(pltpu.VMEM((RANK, RANK), F32), o...  2.56 us
    ppermute x5, waiting for transfers between devices, shift(): lax.ppermute(array, axis, [(i, (i + step) % size) for i in range(size)])  1.4 us
  transfers between devices with their start and end apart: 5, of which 2 were waited for; matrix products, arithmetic and copies ran while one was open for 0% of the time, Pallas kernels for 8%

profile of v4, /device:TPU:1, one launch (start us, length us, event | category | flops | bytes accessed | tf_op | source)
XLA Modules:
  0.0 62.2 jit_solution(100963653598422664)
XLA Ops:
  0.6 2.1 %compensate_other.1 = (f32[224,2048]{1,0:T(8,128)S(1)}, bf16[224,2048]{1,0:T(8,128)(2,1)S(1)}, f32[16,32,128]{2,1,0:T(8,128)S(1)}) custom-call(bf16[224,4096]{1,0:T(8,128)(2,1)} %bitcast.11, f32[224,4096]{1,0:T(8,128)} %bitcast.9, bf16[32,224]{1,0:T(8,128)(2,1)} %bitcast.13), custom_call_target="tpu_custom_call" | custom-call | flops 29360128 | bytes 2752512 | tf_op jit(solution)/shard_map/compensate_other/pallas_call | solution.py:90
  2.7 3.3 %collective-permute-start = (f32[16,32,128]{2,1,0:T(8,128)S(1)}, f32[16,32,128]{2,1,0:T(8,128)S(1)}, u32[]{:S(2)}, u32[]{:S(2)}) collective-permute-start(f32[16,32,128]{2,1,0:T(8,128)S(1)} %get-tuple-element.23), channel_id=1, source_target_pairs={{0,1},{1,0},{2,3},{3,2},{4,5},{5,4},{6,7},{7,6},{8,9},{9,8},{10,11... | collective-permute-start | bytes 786440 | tf_op jit(solution)/shard_map/ppermute | solution.py:299
  6.0 2.1 %compensate_own.1 = (f32[224,2048]{1,0:T(8,128)S(1)}, bf16[224,2048]{1,0:T(8,128)(2,1)S(1)}, f32[16,32,128]{2,1,0:T(8,128)S(1)}) custom-call(bf16[224,4096]{1,0:T(8,128)(2,1)} %bitcast.12, f32[224,4096]{1,0:T(8,128)} %bitcast.10, bf16[32,224]{1,0:T(8,128)(2,1)} %bitcast.14), custom_call_target="tpu_custom_call" | custom-call | flops 29360128 | bytes 2752512 | tf_op jit(solution)/shard_map/compensate_own/pallas_call | solution.py:90
  8.1 0.0 collective-permute-done
  8.2 12.6 %all_to_all.15 = f32[16,32,128]{2,1,0:T(8,128)S(1)} all-to-all(f32[16,32,128]{2,1,0:T(8,128)S(1)} %add.95), channel_id=1, replica_groups=mesh['x'=4,'y'=4,'z'=8,'c'=2] {'x','y'}, dimensions={0} | all-to-all | bytes 524288 | tf_op jit(solution)/shard_map/all_to_all | solution.py:314
  20.8 16.0 %all_to_all.16 = f32[8,32,128]{2,1,0:T(8,128)S(1)} all-to-all(f32[8,32,128]{2,1,0:T(8,128)S(1)} %broadcast_in_dim.9), channel_id=1, replica_groups=mesh['x'=4,'y'=4,'z'=8,'c'=2] {'z'}, dimensions={0} | all-to-all | bytes 262144 | tf_op jit(solution)/shard_map/all_to_all | solution.py:315
  36.9 11.1 %all_to_all.17.blocks = f32[16,32,128]{2,1,0:T(8,128)S(1)} all-to-all(f32[16,32,128]{2,1,0:T(8,128)S(1)} %broadcast_in_dim.10), channel_id=1, replica_groups=mesh['x'=4,'y'=4,'z'=8,'c'=2] {'x','y'}, dimensions={0} | all-to-all | bytes 524288 | tf_op jit(solution)/shard_map/all_to_all | solution.py:316
  47.9 3.8 %collective-permute-start.1 = (f32[16,32,128]{2,1,0:T(8,128)S(1)}, f32[16,32,128]{2,1,0:T(8,128)S(1)}, u32[]{:S(2)}, u32[]{:S(2)}) collective-permute-start(f32[16,32,128]{2,1,0:T(8,128)S(1)} %all_to_all.17.blocks), channel_id=1, source_target_pairs={{0,1},{1,0},{2,3},{3,2},{4,5},{5,4},{6,7},{7,6},{8,9},{9,8},{10,11... | collective-permute-start | bytes 786440 | tf_op jit(solution)/shard_map/ppermute | solution.py:299
  51.8 0.4 project.2
  52.2 0.8 %collective-permute-done.1.blocks = f32[16,32,128]{2,1,0:T(8,128)S(1)} collective-permute-done((f32[16,32,128]{2,1,0:T(8,128)S(1)}, f32[16,32,128]{2,1,0:T(8,128)S(1)}, u32[]{:S(2)}, u32[]{:S(2)}) %collective-permute-start.1) | collective-permute-done | bytes 262176 | tf_op jit(solution)/shard_map/ppermute | solution.py:299
  52.9 0.4 project.3
  53.4 0.9 %collective-permute-start.4 = (f32[32,256]{1,0:T(8,128)S(1)}, f32[32,256]{1,0:T(8,128)S(1)}, u32[]{:S(2)}, u32[]{:S(2)}) collective-permute-start(f32[32,256]{1,0:T(8,128)S(1)} %get-tuple-element.26.own), channel_id=1, source_target_pairs={{0,192},{64,0},{128,64},{192,128},{1,193},{65,1},{129,65},{193,129... | collective-permute-start | bytes 98312 | tf_op jit(solution)/shard_map/ppermute | solution.py:299
  54.2 0.7 %collective-permute-start.3 = (f32[32,256]{1,0:T(8,128)S(1)}, f32[32,256]{1,0:T(8,128)S(1)}, u32[]{:S(2)}, u32[]{:S(2)}) collective-permute-start(f32[32,256]{1,0:T(8,128)S(1)} %get-tuple-element.26.own), channel_id=1, source_target_pairs={{0,64},{64,128},{128,192},{192,0},{1,65},{65,129},{129,193},{193,1... | collective-permute-start | bytes 98312 | tf_op jit(solution)/shard_map/ppermute | solution.py:299
  54.9 1.1 %collective-permute-start.2 = (f32[32,256]{1,0:T(8,128)S(1)}, f32[32,256]{1,0:T(8,128)S(1)}, u32[]{:S(2)}, u32[]{:S(2)}) collective-permute-start(f32[32,256]{1,0:T(8,128)S(1)} %get-tuple-element.26.own), channel_id=1, source_target_pairs={{0,128},{64,192},{128,0},{192,64},{1,129},{65,193},{129,1},{193,65... | collective-permute-start | bytes 98312 | tf_op jit(solution)/shard_map/ppermute | solution.py:299
  56.0 2.6 %factor.1 = (f32[32,32]{1,0:T(8,128)S(1)}, bf16[96,2048]{1,0:T(8,128)(2,1)S(1)}, bf16[96,2048]{1,0:T(8,128)(2,1)S(1)}) custom-call(bf16[96,2048]{1,0:T(8,128)(2,1)S(1)} %get-tuple-element.27.own_terms, bf16[96,2048]{1,0:T(8,128)(2,1)S(1)} %get-tuple-element.28.other_terms), custom_call_target="tpu_custom_call" | custom-call | flops 1000000000 | bytes 10000000 | tf_op jit(solution)/shard_map/factor/pallas_call | solution.py:212
  58.5 0.0 collective-permute-done.4.right
  58.6 0.0 collective-permute-done.3.left
  58.6 0.6 %collective-permute-done.2.across = f32[32,256]{1,0:T(8,128)S(1)} collective-permute-done((f32[32,256]{1,0:T(8,128)S(1)}, f32[32,256]{1,0:T(8,128)S(1)}, u32[]{:S(2)}, u32[]{:S(2)}) %collective-permute-start.2) | collective-permute-done | bytes 32800 | tf_op jit(solution)/shard_map/ppermute | solution.py:299
  59.2 3.0 %apply.1 = (f32[224,4096]{1,0:T(8,128)}, bf16[224,4096]{1,0:T(8,128)(2,1)}, f32[32,224]{1,0:T(8,128)}) custom-call(f32[224,2048]{1,0:T(8,128)S(1)} %get-tuple-element.19.own_comp, f32[224,2048]{1,0:T(8,128)S(1)} %get-tuple-element.20.other_comp, f32[32,256]{1,0:T(8,128)S(1)} %get-tuple-element.26.own, f32[32,256]{1,0:T(8,128)S(1)} %collective-permute-done.2.across, ...), custom_call_target="tpu_custom_call" | custom-call | tf_op jit(solution)/shard_map/apply/pallas_call | solution.py:276
  (5 shorter events, 0.1 us)
Async XLA Ops:
  2.7 5.4 %collective-permute-start = (f32[16,32,128]{2,1,0:T(8,128)S(1)}, f32[16,32,128]{2,1,0:T(8,128)S(1)}, u32[]{:S(2)}, u32[]{:S(2)}) collective-permute-start(f32[16,32,128]{2,1,0:T(8,128)S(1)} %get-tuple-element.23), channel_id=1, source_target_pairs={{0,1},{1,0},{2,3},{3,2},{4,5},{5,4},{6,7},{7,6},{8,9},{9,8},{10,11... | collective-permute-start | bytes 786440 | tf_op jit(solution)/shard_map/ppermute | solution.py:299
  47.9 5.0 %collective-permute-start.1 = (f32[16,32,128]{2,1,0:T(8,128)S(1)}, f32[16,32,128]{2,1,0:T(8,128)S(1)}, u32[]{:S(2)}, u32[]{:S(2)}) collective-permute-start(f32[16,32,128]{2,1,0:T(8,128)S(1)} %all_to_all.17.blocks), channel_id=1, source_target_pairs={{0,1},{1,0},{2,3},{3,2},{4,5},{5,4},{6,7},{7,6},{8,9},{9,8},{10,11... | collective-permute-start | bytes 786440 | tf_op jit(solution)/shard_map/ppermute | solution.py:299
  53.4 5.2 %collective-permute-start.4 = (f32[32,256]{1,0:T(8,128)S(1)}, f32[32,256]{1,0:T(8,128)S(1)}, u32[]{:S(2)}, u32[]{:S(2)}) collective-permute-start(f32[32,256]{1,0:T(8,128)S(1)} %get-tuple-element.26.own), channel_id=1, source_target_pairs={{0,192},{64,0},{128,64},{192,128},{1,193},{65,1},{129,65},{193,129... | collective-permute-start | bytes 98312 | tf_op jit(solution)/shard_map/ppermute | solution.py:299
  54.2 4.3 %collective-permute-start.3 = (f32[32,256]{1,0:T(8,128)S(1)}, f32[32,256]{1,0:T(8,128)S(1)}, u32[]{:S(2)}, u32[]{:S(2)}) collective-permute-start(f32[32,256]{1,0:T(8,128)S(1)} %get-tuple-element.26.own), channel_id=1, source_target_pairs={{0,64},{64,128},{128,192},{192,0},{1,65},{65,129},{129,193},{193,1... | collective-permute-start | bytes 98312 | tf_op jit(solution)/shard_map/ppermute | solution.py:299
  54.9 4.3 %collective-permute-start.2 = (f32[32,256]{1,0:T(8,128)S(1)}, f32[32,256]{1,0:T(8,128)S(1)}, u32[]{:S(2)}, u32[]{:S(2)}) collective-permute-start(f32[32,256]{1,0:T(8,128)S(1)} %get-tuple-element.26.own), channel_id=1, source_target_pairs={{0,128},{64,192},{128,0},{192,64},{1,129},{65,193},{129,1},{193,65... | collective-permute-start | bytes 98312 | tf_op jit(solution)/shard_map/ppermute | solution.py:299

commit v5 on v4

--- a/solution.py
+++ b/solution.py
@@ -58,6 +58,8 @@
     own, grads, errors, q_hbm, comp, low, partial, grad_buf, q_t, q_sem, grad_sems, error_sems
 ):
     start = half_start(own)
+    q_copy = pltpu.make_async_copy(q_hbm, q_t, q_sem)
+    q_copy.start()
     copies = []
     for chunk in range(CHUNKS):
         at, cols = in_hbm(start, chunk), in_half(chunk)
@@ -68,8 +70,6 @@
         for copy in pair:
             copy.start()
         copies.append(pair)
-    q_copy = pltpu.make_async_copy(q_hbm, q_t, q_sem)
-    q_copy.start()
     q_copy.wait()
     factor = q_t[...]
     for chunk in range(CHUNKS):
@@ -190,25 +190,20 @@
     gram = part(0, 0) + ((part(0, 1) + part(1, 0)) + small)
     lower_inverse = inverse_of_lower(gram)
     inverse[...] = lower_inverse
+    one, two, three = (term.astype(F32) for term in three_terms(lower_inverse))
+    weights = jnp.concatenate([one, one, two, one, two, three], axis=1).astype(BF16)
     for terms, ortho in ((own_terms, own_ortho), (other_terms, other_ortho)):
         for chunk in range(CHUNKS):
             cols = in_half(chunk)
-            p_t = (
-                terms[:RANK, cols].astype(F32)
-                + terms[RANK : 2 * RANK, cols].astype(F32)
-                + terms[2 * RANK :, cols].astype(F32)
-            )
-            ortho_t = jnp.dot(
-                lower_inverse, p_t, precision=lax.Precision.HIGHEST, preferred_element_type=F32
-            )
-            high, low = two_terms(ortho_t)
+            one, two, three = (terms[t * RANK : (t + 1) * RANK, cols] for t in range(3))
+            stack = jnp.concatenate([one, two, one, three, two, one])
+            high, low = two_terms(jnp.dot(weights, stack, preferred_element_type=F32))
             ortho[:RANK, cols] = high
-            ortho[RANK : 2 * RANK, cols] = low
-            ortho[2 * RANK :, cols] = high
+            ortho[RANK:, cols] = low
 
 
 def factor(own_terms, other_terms):
-    ortho = pltpu.VMEM((3 * RANK, HALF), BF16)
+    ortho = pltpu.VMEM((2 * RANK, HALF), BF16)
     return pl.pallas_call(
         factor_kernel,
         out_shape=(pltpu.VMEM((RANK, RANK), F32), ortho, ortho),
@@ -253,7 +248,9 @@
         start = half_start(half == 0)
         for chunk in range(CHUNKS):
             cols, at = in_half(chunk), in_hbm(start, chunk)
-            approx = jnp.dot(stacked, ortho[:, cols], preferred_element_type=F32)
+            terms = ortho[:, cols]
+            terms = jnp.concatenate([terms, terms[:RANK]])
+            approx = jnp.dot(stacked, terms, preferred_element_type=F32)
             error_buf[half, :, cols] = comp[:, cols] - approx
             update_buf[half, :, cols] = approx.astype(BF16)
             pair = [

time: 62.7 us -> 62.7 us (level)
  no operation moved by 1% of the time
where the time goes in v5:
time: 62.7 us; the launch traced here: 62.2 us
  blocking collectives  39.7 us (63%)
  Pallas kernels  10.2 us (16%)
  starting transfers between devices  9.72 us (16%)
  waiting for transfers between devices  1.66 us (3%)
  between operations  0.72 us (1%)
    all_to_all x1, blocking collectives, reduce_and_gather(): block = add_up(lax.all_to_all(repeat(block, Z), 'z', 0, 0))  16 us
    all_to_all x1, blocking collectives, reduce_and_gather(): block = add_up(lax.all_to_all(mine, ('x', 'y'), 0, 0))  12.6 us
    all_to_all x1, blocking collectives, reduce_and_gather(): return lax.all_to_all(repeat(block, BLOCKS), ('x', 'y'), 0, 0)  11.1 us
    ppermute x5, starting transfers between devices, shift(): lax.ppermute(array, axis, [(i, (i + step) % size) for i in range(size)])  9.72 us
    pallas_call x2, Pallas kernels, compensate(): pl.pallas_call(functools.partial(compensate_kernel, own), out_shape=(pltp...  4.07 us
    pallas_call x1, Pallas kernels, apply(): pl.pallas_call(apply_kernel, out_shape=(jax.ShapeDtypeStruct((ROWS, FEATU...  3.03 us
    pallas_call x1, Pallas kernels, factor(): pl.pallas_call(factor_kernel, out_shape=(pltpu.VMEM((RANK, RANK), F32), o...  2.3 us
    ppermute x5, waiting for transfers between devices, shift(): lax.ppermute(array, axis, [(i, (i + step) % size) for i in range(size)])  1.66 us
  transfers between devices with their start and end apart: 5, of which 2 were waited for; matrix products, arithmetic and copies ran while one was open for 0% of the time, Pallas kernels for 8%

profile of v5, /device:TPU:1, one launch (start us, length us, event | category | flops | bytes accessed | tf_op | source)
XLA Modules:
  0.0 62.2 jit_solution(15503076444559090207)
XLA Ops:
  0.6 2.0 %compensate_other.1 = (f32[224,2048]{1,0:T(8,128)S(1)}, bf16[224,2048]{1,0:T(8,128)(2,1)S(1)}, f32[16,32,128]{2,1,0:T(8,128)S(1)}) custom-call(bf16[224,4096]{1,0:T(8,128)(2,1)} %bitcast.11, f32[224,4096]{1,0:T(8,128)} %bitcast.9, bf16[32,224]{1,0:T(8,128)(2,1)} %bitcast.13), custom_call_target="tpu_custom_call" | custom-call | flops 29360128 | bytes 2752512 | tf_op jit(solution)/shard_map/compensate_other/pallas_call | solution.py:90
  2.7 3.3 %collective-permute-start = (f32[16,32,128]{2,1,0:T(8,128)S(1)}, f32[16,32,128]{2,1,0:T(8,128)S(1)}, u32[]{:S(2)}, u32[]{:S(2)}) collective-permute-start(f32[16,32,128]{2,1,0:T(8,128)S(1)} %get-tuple-element.23), channel_id=1, source_target_pairs={{0,1},{1,0},{2,3},{3,2},{4,5},{5,4},{6,7},{7,6},{8,9},{9,8},{10,11... | collective-permute-start | bytes 786440 | tf_op jit(solution)/shard_map/ppermute | solution.py:296
  6.0 2.0 %compensate_own.1 = (f32[224,2048]{1,0:T(8,128)S(1)}, bf16[224,2048]{1,0:T(8,128)(2,1)S(1)}, f32[16,32,128]{2,1,0:T(8,128)S(1)}) custom-call(bf16[224,4096]{1,0:T(8,128)(2,1)} %bitcast.12, f32[224,4096]{1,0:T(8,128)} %bitcast.10, bf16[32,224]{1,0:T(8,128)(2,1)} %bitcast.14), custom_call_target="tpu_custom_call" | custom-call | flops 29360128 | bytes 2752512 | tf_op jit(solution)/shard_map/compensate_own/pallas_call | solution.py:90
  8.0 0.0 collective-permute-done
  8.1 12.6 %all_to_all.15 = f32[16,32,128]{2,1,0:T(8,128)S(1)} all-to-all(f32[16,32,128]{2,1,0:T(8,128)S(1)} %add.95), channel_id=1, replica_groups=mesh['x'=4,'y'=4,'z'=8,'c'=2] {'x','y'}, dimensions={0} | all-to-all | bytes 524288 | tf_op jit(solution)/shard_map/all_to_all | solution.py:311
  20.8 16.0 %all_to_all.16 = f32[8,32,128]{2,1,0:T(8,128)S(1)} all-to-all(f32[8,32,128]{2,1,0:T(8,128)S(1)} %broadcast_in_dim.9), channel_id=1, replica_groups=mesh['x'=4,'y'=4,'z'=8,'c'=2] {'z'}, dimensions={0} | all-to-all | bytes 262144 | tf_op jit(solution)/shard_map/all_to_all | solution.py:312
  36.8 11.1 %all_to_all.17.blocks = f32[16,32,128]{2,1,0:T(8,128)S(1)} all-to-all(f32[16,32,128]{2,1,0:T(8,128)S(1)} %broadcast_in_dim.10), channel_id=1, replica_groups=mesh['x'=4,'y'=4,'z'=8,'c'=2] {'x','y'}, dimensions={0} | all-to-all | bytes 524288 | tf_op jit(solution)/shard_map/all_to_all | solution.py:313
  47.9 3.8 %collective-permute-start.1 = (f32[16,32,128]{2,1,0:T(8,128)S(1)}, f32[16,32,128]{2,1,0:T(8,128)S(1)}, u32[]{:S(2)}, u32[]{:S(2)}) collective-permute-start(f32[16,32,128]{2,1,0:T(8,128)S(1)} %all_to_all.17.blocks), channel_id=1, source_target_pairs={{0,1},{1,0},{2,3},{3,2},{4,5},{5,4},{6,7},{7,6},{8,9},{9,8},{10,11... | collective-permute-start | bytes 786440 | tf_op jit(solution)/shard_map/ppermute | solution.py:296
  51.7 0.4 project.2
  52.1 0.8 %collective-permute-done.1.blocks = f32[16,32,128]{2,1,0:T(8,128)S(1)} collective-permute-done((f32[16,32,128]{2,1,0:T(8,128)S(1)}, f32[16,32,128]{2,1,0:T(8,128)S(1)}, u32[]{:S(2)}, u32[]{:S(2)}) %collective-permute-start.1) | collective-permute-done | bytes 262176 | tf_op jit(solution)/shard_map/ppermute | solution.py:296
  52.9 0.4 project.3
  53.3 0.9 %collective-permute-start.4 = (f32[32,256]{1,0:T(8,128)S(1)}, f32[32,256]{1,0:T(8,128)S(1)}, u32[]{:S(2)}, u32[]{:S(2)}) collective-permute-start(f32[32,256]{1,0:T(8,128)S(1)} %get-tuple-element.26.own), channel_id=1, source_target_pairs={{0,192},{64,0},{128,64},{192,128},{1,193},{65,1},{129,65},{193,129... | collective-permute-start | bytes 98312 | tf_op jit(solution)/shard_map/ppermute | solution.py:296
  54.2 0.7 %collective-permute-start.3 = (f32[32,256]{1,0:T(8,128)S(1)}, f32[32,256]{1,0:T(8,128)S(1)}, u32[]{:S(2)}, u32[]{:S(2)}) collective-permute-start(f32[32,256]{1,0:T(8,128)S(1)} %get-tuple-element.26.own), channel_id=1, source_target_pairs={{0,64},{64,128},{128,192},{192,0},{1,65},{65,129},{129,193},{193,1... | collective-permute-start | bytes 98312 | tf_op jit(solution)/shard_map/ppermute | solution.py:296
  54.8 1.1 %collective-permute-start.2 = (f32[32,256]{1,0:T(8,128)S(1)}, f32[32,256]{1,0:T(8,128)S(1)}, u32[]{:S(2)}, u32[]{:S(2)}) collective-permute-start(f32[32,256]{1,0:T(8,128)S(1)} %get-tuple-element.26.own), channel_id=1, source_target_pairs={{0,128},{64,192},{128,0},{192,64},{1,129},{65,193},{129,1},{193,65... | collective-permute-start | bytes 98312 | tf_op jit(solution)/shard_map/ppermute | solution.py:296
  55.9 2.3 %factor.1 = (f32[32,32]{1,0:T(8,128)S(1)}, bf16[64,2048]{1,0:T(8,128)(2,1)S(1)}, bf16[64,2048]{1,0:T(8,128)(2,1)S(1)}) custom-call(bf16[96,2048]{1,0:T(8,128)(2,1)S(1)} %get-tuple-element.27.own_terms, bf16[96,2048]{1,0:T(8,128)(2,1)S(1)} %get-tuple-element.28.other_terms), custom_call_target="tpu_custom_call" | custom-call | flops 1000000000 | bytes 10000000 | tf_op jit(solution)/shard_map/factor/pallas_call | solution.py:207
  58.2 0.0 collective-permute-done.4.right
  58.2 0.0 collective-permute-done.3.left
  58.2 0.9 %collective-permute-done.2.across = f32[32,256]{1,0:T(8,128)S(1)} collective-permute-done((f32[32,256]{1,0:T(8,128)S(1)}, f32[32,256]{1,0:T(8,128)S(1)}, u32[]{:S(2)}, u32[]{:S(2)}) %collective-permute-start.2) | collective-permute-done | bytes 32800 | tf_op jit(solution)/shard_map/ppermute | solution.py:296
  59.1 3.0 %apply.1 = (f32[224,4096]{1,0:T(8,128)}, bf16[224,4096]{1,0:T(8,128)(2,1)}, f32[32,224]{1,0:T(8,128)}) custom-call(f32[224,2048]{1,0:T(8,128)S(1)} %get-tuple-element.19.own_comp, f32[224,2048]{1,0:T(8,128)S(1)} %get-tuple-element.20.other_comp, f32[32,256]{1,0:T(8,128)S(1)} %get-tuple-element.26.own, f32[32,256]{1,0:T(8,128)S(1)} %collective-permute-done.2.across, ...), custom_call_target="tpu_custom_call" | custom-call | tf_op jit(solution)/shard_map/apply/pallas_call | solution.py:273
  (5 shorter events, 0.1 us)
Async XLA Ops:
  2.7 5.4 %collective-permute-start = (f32[16,32,128]{2,1,0:T(8,128)S(1)}, f32[16,32,128]{2,1,0:T(8,128)S(1)}, u32[]{:S(2)}, u32[]{:S(2)}) collective-permute-start(f32[16,32,128]{2,1,0:T(8,128)S(1)} %get-tuple-element.23), channel_id=1, source_target_pairs={{0,1},{1,0},{2,3},{3,2},{4,5},{5,4},{6,7},{7,6},{8,9},{9,8},{10,11... | collective-permute-start | bytes 786440 | tf_op jit(solution)/shard_map/ppermute | solution.py:296
  47.9 5.0 %collective-permute-start.1 = (f32[16,32,128]{2,1,0:T(8,128)S(1)}, f32[16,32,128]{2,1,0:T(8,128)S(1)}, u32[]{:S(2)}, u32[]{:S(2)}) collective-permute-start(f32[16,32,128]{2,1,0:T(8,128)S(1)} %all_to_all.17.blocks), channel_id=1, source_target_pairs={{0,1},{1,0},{2,3},{3,2},{4,5},{5,4},{6,7},{7,6},{8,9},{9,8},{10,11... | collective-permute-start | bytes 786440 | tf_op jit(solution)/shard_map/ppermute | solution.py:296
  53.3 4.9 %collective-permute-start.4 = (f32[32,256]{1,0:T(8,128)S(1)}, f32[32,256]{1,0:T(8,128)S(1)}, u32[]{:S(2)}, u32[]{:S(2)}) collective-permute-start(f32[32,256]{1,0:T(8,128)S(1)} %get-tuple-element.26.own), channel_id=1, source_target_pairs={{0,192},{64,0},{128,64},{192,128},{1,193},{65,1},{129,65},{193,129... | collective-permute-start | bytes 98312 | tf_op jit(solution)/shard_map/ppermute | solution.py:296
  54.2 4.1 %collective-permute-start.3 = (f32[32,256]{1,0:T(8,128)S(1)}, f32[32,256]{1,0:T(8,128)S(1)}, u32[]{:S(2)}, u32[]{:S(2)}) collective-permute-start(f32[32,256]{1,0:T(8,128)S(1)} %get-tuple-element.26.own), channel_id=1, source_target_pairs={{0,64},{64,128},{128,192},{192,0},{1,65},{65,129},{129,193},{193,1... | collective-permute-start | bytes 98312 | tf_op jit(solution)/shard_map/ppermute | solution.py:296
  54.8 4.3 %collective-permute-start.2 = (f32[32,256]{1,0:T(8,128)S(1)}, f32[32,256]{1,0:T(8,128)S(1)}, u32[]{:S(2)}, u32[]{:S(2)}) collective-permute-start(f32[32,256]{1,0:T(8,128)S(1)} %get-tuple-element.26.own), channel_id=1, source_target_pairs={{0,128},{64,192},{128,0},{192,64},{1,129},{65,193},{129,1},{193,65... | collective-permute-start | bytes 98312 | tf_op jit(solution)/shard_map/ppermute | solution.py:296

commit v6 on v5

--- a/solution.py
+++ b/solution.py
@@ -19,6 +19,8 @@
 CHUNKS = 2
 WIDTH = HALF // CHUNKS
 GROUP = 8
+SWAP = (1, 0)
+REPLICAS = ((1, 0, 3, 2), (3, 2, 0, 1), (2, 3, 1, 0))
 F32, BF16 = jnp.float32, jnp.bfloat16
 CONTRACT_LAST = (((1,), (1,)), ((), ()))
 VMEM = pl.BlockSpec(memory_space=pltpu.VMEM)
@@ -219,9 +221,9 @@
     own_comp,
     other_comp,
     own,
-    across,
-    left,
-    right,
+    pair,
+    first,
+    second,
     inverse,
     own_ortho,
     other_ortho,
@@ -235,7 +237,7 @@
     update_sems,
     q_sem,
 ):
-    total = (own[...] + across[...]) + (left[...] + right[...])
+    total = (own[...] + pair[...]) + (first[...] + second[...])
     q_t = jnp.dot(
         inverse[...], total * (1.0 / X), precision=lax.Precision.HIGHEST, preferred_element_type=F32
     )
@@ -253,7 +255,7 @@
             approx = jnp.dot(stacked, terms, preferred_element_type=F32)
             error_buf[half, :, cols] = comp[:, cols] - approx
             update_buf[half, :, cols] = approx.astype(BF16)
-            pair = [
+            outgoing = [
                 pltpu.make_async_copy(
                     error_buf.at[half, :, cols], new_errors.at[:, at], error_sems.at[half, chunk]
                 ),
@@ -261,14 +263,14 @@
                     update_buf.at[half, :, cols], update.at[:, at], update_sems.at[half, chunk]
                 ),
             ]
-            for copy in pair:
+            for copy in outgoing:
                 copy.start()
-            copies += pair
+            copies += outgoing
     for copy in copies:
         copy.wait()
 
 
-def apply(own_comp, other_comp, own, across, left, right, inverse, own_ortho, other_ortho):
+def apply(own_comp, other_comp, own, pair, first, second, inverse, own_ortho, other_ortho):
     comps = [pltpu.with_memory_space_constraint(a, pltpu.VMEM) for a in (own_comp, other_comp)]
     return pl.pallas_call(
         apply_kernel,
@@ -289,11 +291,11 @@
         ],
         compiler_params=params(20),
         name="apply",
-    )(*comps, own, across, left, right, inverse, own_ortho, other_ortho)
-
-
-def shift(array, axis, size, step):
-    return lax.ppermute(array, axis, [(i, (i + step) % size) for i in range(size)])
+    )(*comps, own, pair, first, second, inverse, own_ortho, other_ortho)
+
+
+def send(array, axis, targets):
+    return lax.ppermute(array, axis, list(enumerate(targets)))
 
 
 def add_up(blocks):
@@ -316,16 +318,16 @@
 def shards(grads, errors, q_start):
     q_t = q_start.T
     other_comp, other_low, other = compensate(grads[0], errors[0], q_t, False)
-    received = shift(other, "c", C, 1)
+    received = send(other, "c", SWAP)
     own_comp, own_low, mine = compensate(grads[0], errors[0], q_t, True)
     mine = reduce_and_gather(mine + received)
-    other = shift(mine, "c", C, 1)
+    other = send(mine, "c", SWAP)
     product, own_terms = project(own_low, mine)
     product, other_terms = project(other_low, other, product)
-    across, left, right = (shift(product, "x", X, step) for step in (2, 1, 3))
+    pair, first, second = (send(product, "x", targets) for targets in REPLICAS)
     inverse, own_ortho, other_ortho = factor(own_terms, other_terms)
     new_errors, update, new_q = apply(
-        own_comp, other_comp, product, across, left, right, inverse, own_ortho, other_ortho
+        own_comp, other_comp, product, pair, first, second, inverse, own_ortho, other_ortho
     )
     return (update, new_errors[None], new_q.T)
 

time: 62.7 us -> 62.3 us (level)
  transfers between devices with their start and end apart: 5 -> 5, of which waited for: 2 -> 3; matrix products, arithmetic and copies ran while one was open for 0% -> 0% of each run, Pallas kernels for 8% -> 8%
where the time goes in v6:
time: 62.3 us; the launch traced here: 61.9 us
  blocking collectives  39.7 us (64%)
  Pallas kernels  10.2 us (16%)
  starting transfers between devices  9.88 us (16%)
  waiting for transfers between devices  1.2 us (2%)
  between operations  0.71 us (1%)
    all_to_all x1, blocking collectives, reduce_and_gather(): block = add_up(lax.all_to_all(repeat(block, Z), 'z', 0, 0))  16 us
    all_to_all x1, blocking collectives, reduce_and_gather(): block = add_up(lax.all_to_all(mine, ('x', 'y'), 0, 0))  12.6 us
    all_to_all x1, blocking collectives, reduce_and_gather(): return lax.all_to_all(repeat(block, BLOCKS), ('x', 'y'), 0, 0)  11.1 us
    ppermute x5, starting transfers between devices, send(): return lax.ppermute(array, axis, list(enumerate(targets)))  9.88 us
    pallas_call x2, Pallas kernels, compensate(): pl.pallas_call(functools.partial(compensate_kernel, own), out_shape=(pltp...  4.07 us
    pallas_call x1, Pallas kernels, apply(): pl.pallas_call(apply_kernel, out_shape=(jax.ShapeDtypeStruct((ROWS, FEATU...  3.03 us
    pallas_call x1, Pallas kernels, factor(): pl.pallas_call(factor_kernel, out_shape=(pltpu.VMEM((RANK, RANK), F32), o...  2.3 us
  transfers between devices with their start and end apart: 5, of which 3 were waited for; matrix products, arithmetic and copies ran while one was open for 0% of the time, Pallas kernels for 8%

profile of v6, /device:TPU:1, one launch (start us, length us, event | category | flops | bytes accessed | tf_op | source)
XLA Modules:
  0.0 61.9 jit_solution(10454457941920277641)
XLA Ops:
  0.6 2.0 %compensate_other.1 = (f32[224,2048]{1,0:T(8,128)S(1)}, bf16[224,2048]{1,0:T(8,128)(2,1)S(1)}, f32[16,32,128]{2,1,0:T(8,128)S(1)}) custom-call(bf16[224,4096]{1,0:T(8,128)(2,1)} %bitcast.11, f32[224,4096]{1,0:T(8,128)} %bitcast.9, bf16[32,224]{1,0:T(8,128)(2,1)} %bitcast.13), custom_call_target="tpu_custom_call" | custom-call | flops 29360128 | bytes 2752512 | tf_op jit(solution)/shard_map/compensate_other/pallas_call | solution.py:92
  2.7 3.3 %collective-permute-start = (f32[16,32,128]{2,1,0:T(8,128)S(1)}, f32[16,32,128]{2,1,0:T(8,128)S(1)}, u32[]{:S(2)}, u32[]{:S(2)}) collective-permute-start(f32[16,32,128]{2,1,0:T(8,128)S(1)} %get-tuple-element.23), channel_id=1, source_target_pairs={{0,1},{1,0},{2,3},{3,2},{4,5},{5,4},{6,7},{7,6},{8,9},{9,8},{10,11... | collective-permute-start | bytes 786440 | tf_op jit(solution)/shard_map/ppermute | solution.py:298
  6.0 2.0 %compensate_own.1 = (f32[224,2048]{1,0:T(8,128)S(1)}, bf16[224,2048]{1,0:T(8,128)(2,1)S(1)}, f32[16,32,128]{2,1,0:T(8,128)S(1)}) custom-call(bf16[224,4096]{1,0:T(8,128)(2,1)} %bitcast.12, f32[224,4096]{1,0:T(8,128)} %bitcast.10, bf16[32,224]{1,0:T(8,128)(2,1)} %bitcast.14), custom_call_target="tpu_custom_call" | custom-call | flops 29360128 | bytes 2752512 | tf_op jit(solution)/shard_map/compensate_own/pallas_call | solution.py:92
  8.0 0.0 collective-permute-done
  8.1 12.6 %all_to_all.15 = f32[16,32,128]{2,1,0:T(8,128)S(1)} all-to-all(f32[16,32,128]{2,1,0:T(8,128)S(1)} %add.95), channel_id=1, replica_groups=mesh['x'=4,'y'=4,'z'=8,'c'=2] {'x','y'}, dimensions={0} | all-to-all | bytes 524288 | tf_op jit(solution)/shard_map/all_to_all | solution.py:313
  20.8 16.0 %all_to_all.16 = f32[8,32,128]{2,1,0:T(8,128)S(1)} all-to-all(f32[8,32,128]{2,1,0:T(8,128)S(1)} %broadcast_in_dim.9), channel_id=1, replica_groups=mesh['x'=4,'y'=4,'z'=8,'c'=2] {'z'}, dimensions={0} | all-to-all | bytes 262144 | tf_op jit(solution)/shard_map/all_to_all | solution.py:314
  36.8 11.1 %all_to_all.17.blocks = f32[16,32,128]{2,1,0:T(8,128)S(1)} all-to-all(f32[16,32,128]{2,1,0:T(8,128)S(1)} %broadcast_in_dim.10), channel_id=1, replica_groups=mesh['x'=4,'y'=4,'z'=8,'c'=2] {'x','y'}, dimensions={0} | all-to-all | bytes 524288 | tf_op jit(solution)/shard_map/all_to_all | solution.py:315
  47.9 3.8 %collective-permute-start.1 = (f32[16,32,128]{2,1,0:T(8,128)S(1)}, f32[16,32,128]{2,1,0:T(8,128)S(1)}, u32[]{:S(2)}, u32[]{:S(2)}) collective-permute-start(f32[16,32,128]{2,1,0:T(8,128)S(1)} %all_to_all.17.blocks), channel_id=1, source_target_pairs={{0,1},{1,0},{2,3},{3,2},{4,5},{5,4},{6,7},{7,6},{8,9},{9,8},{10,11... | collective-permute-start | bytes 786440 | tf_op jit(solution)/shard_map/ppermute | solution.py:298
  51.7 0.4 project.2
  52.1 0.8 %collective-permute-done.1.blocks = f32[16,32,128]{2,1,0:T(8,128)S(1)} collective-permute-done((f32[16,32,128]{2,1,0:T(8,128)S(1)}, f32[16,32,128]{2,1,0:T(8,128)S(1)}, u32[]{:S(2)}, u32[]{:S(2)}) %collective-permute-start.1) | collective-permute-done | bytes 262176 | tf_op jit(solution)/shard_map/ppermute | solution.py:298
  52.9 0.4 project.3
  53.3 1.1 %collective-permute-start.4 = (f32[32,256]{1,0:T(8,128)S(1)}, f32[32,256]{1,0:T(8,128)S(1)}, u32[]{:S(2)}, u32[]{:S(2)}) collective-permute-start(f32[32,256]{1,0:T(8,128)S(1)} %get-tuple-element.26.own), channel_id=1, source_target_pairs={{0,128},{64,192},{128,64},{192,0},{1,129},{65,193},{129,65},{193,1... | collective-permute-start | bytes 98312 | tf_op jit(solution)/shard_map/ppermute | solution.py:298
  54.4 1.6 %collective-permute-start.3 = (f32[32,256]{1,0:T(8,128)S(1)}, f32[32,256]{1,0:T(8,128)S(1)}, u32[]{:S(2)}, u32[]{:S(2)}) collective-permute-start(f32[32,256]{1,0:T(8,128)S(1)} %get-tuple-element.26.own), channel_id=1, source_target_pairs={{0,192},{64,128},{128,0},{192,64},{1,193},{65,129},{129,1},{193,65... | collective-permute-start | bytes 98312 | tf_op jit(solution)/shard_map/ppermute | solution.py:298
  56.1 0.0 collective-permute-start.2
  56.1 2.3 %factor.1 = (f32[32,32]{1,0:T(8,128)S(1)}, bf16[64,2048]{1,0:T(8,128)(2,1)S(1)}, bf16[64,2048]{1,0:T(8,128)(2,1)S(1)}) custom-call(bf16[96,2048]{1,0:T(8,128)(2,1)S(1)} %get-tuple-element.27.own_terms, bf16[96,2048]{1,0:T(8,128)(2,1)S(1)} %get-tuple-element.28.other_terms), custom_call_target="tpu_custom_call" | custom-call | flops 1000000000 | bytes 10000000 | tf_op jit(solution)/shard_map/factor/pallas_call | solution.py:209
  58.4 0.0 collective-permute-done.4.second
  58.4 0.3 collective-permute-done.3.first
  58.7 0.1 collective-permute-done.2.pair
  58.8 3.0 %apply.1 = (f32[224,4096]{1,0:T(8,128)}, bf16[224,4096]{1,0:T(8,128)(2,1)}, f32[32,224]{1,0:T(8,128)}) custom-call(f32[224,2048]{1,0:T(8,128)S(1)} %get-tuple-element.19.own_comp, f32[224,2048]{1,0:T(8,128)S(1)} %get-tuple-element.20.other_comp, f32[32,256]{1,0:T(8,128)S(1)} %get-tuple-element.26.own, f32[32,256]{1,0:T(8,128)S(1)} %collective-permute-done.2.pair, ...), custom_call_target="tpu_custom_call" | custom-call | tf_op jit(solution)/shard_map/apply/pallas_call | solution.py:275
  (5 shorter events, 0.1 us)
Async XLA Ops:
  2.7 5.4 %collective-permute-start = (f32[16,32,128]{2,1,0:T(8,128)S(1)}, f32[16,32,128]{2,1,0:T(8,128)S(1)}, u32[]{:S(2)}, u32[]{:S(2)}) collective-permute-start(f32[16,32,128]{2,1,0:T(8,128)S(1)} %get-tuple-element.23), channel_id=1, source_target_pairs={{0,1},{1,0},{2,3},{3,2},{4,5},{5,4},{6,7},{7,6},{8,9},{9,8},{10,11... | collective-permute-start | bytes 786440 | tf_op jit(solution)/shard_map/ppermute | solution.py:298
  47.9 5.0 %collective-permute-start.1 = (f32[16,32,128]{2,1,0:T(8,128)S(1)}, f32[16,32,128]{2,1,0:T(8,128)S(1)}, u32[]{:S(2)}, u32[]{:S(2)}) collective-permute-start(f32[16,32,128]{2,1,0:T(8,128)S(1)} %all_to_all.17.blocks), channel_id=1, source_target_pairs={{0,1},{1,0},{2,3},{3,2},{4,5},{5,4},{6,7},{7,6},{8,9},{9,8},{10,11... | collective-permute-start | bytes 786440 | tf_op jit(solution)/shard_map/ppermute | solution.py:298
  53.3 5.1 %collective-permute-start.4 = (f32[32,256]{1,0:T(8,128)S(1)}, f32[32,256]{1,0:T(8,128)S(1)}, u32[]{:S(2)}, u32[]{:S(2)}) collective-permute-start(f32[32,256]{1,0:T(8,128)S(1)} %get-tuple-element.26.own), channel_id=1, source_target_pairs={{0,128},{64,192},{128,64},{192,0},{1,129},{65,193},{129,65},{193,1... | collective-permute-start | bytes 98312 | tf_op jit(solution)/shard_map/ppermute | solution.py:298
  54.4 4.3 %collective-permute-start.3 = (f32[32,256]{1,0:T(8,128)S(1)}, f32[32,256]{1,0:T(8,128)S(1)}, u32[]{:S(2)}, u32[]{:S(2)}) collective-permute-start(f32[32,256]{1,0:T(8,128)S(1)} %get-tuple-element.26.own), channel_id=1, source_target_pairs={{0,192},{64,128},{128,0},{192,64},{1,193},{65,129},{129,1},{193,65... | collective-permute-start | bytes 98312 | tf_op jit(solution)/shard_map/ppermute | solution.py:298
  56.1 2.8 %collective-permute-start.2 = (f32[32,256]{1,0:T(8,128)S(1)}, f32[32,256]{1,0:T(8,128)S(1)}, u32[]{:S(2)}, u32[]{:S(2)}) collective-permute-start(f32[32,256]{1,0:T(8,128)S(1)} %get-tuple-element.26.own), channel_id=1, source_target_pairs={{0,64},{64,0},{128,192},{192,128},{1,65},{65,1},{129,193},{193,129... | collective-permute-start | bytes 98312 | tf_op jit(solution)/shard_map/ppermute | solution.py:298

commit v7 on v6

--- a/solution.py
+++ b/solution.py
@@ -20,7 +20,7 @@
 WIDTH = HALF // CHUNKS
 GROUP = 8
 SWAP = (1, 0)
-REPLICAS = ((1, 0, 3, 2), (3, 2, 0, 1), (2, 3, 1, 0))
+REPLICAS = ((1, 0, 3, 2), (2, 3, 0, 1), (3, 2, 1, 0))
 F32, BF16 = jnp.float32, jnp.bfloat16
 CONTRACT_LAST = (((1,), (1,)), ((), ()))
 VMEM = pl.BlockSpec(memory_space=pltpu.VMEM)
@@ -253,19 +253,17 @@
             terms = ortho[:, cols]
             terms = jnp.concatenate([terms, terms[:RANK]])
             approx = jnp.dot(stacked, terms, preferred_element_type=F32)
+            update_buf[half, :, cols] = approx.astype(BF16)
+            update_copy = pltpu.make_async_copy(
+                update_buf.at[half, :, cols], update.at[:, at], update_sems.at[half, chunk]
+            )
+            update_copy.start()
             error_buf[half, :, cols] = comp[:, cols] - approx
-            update_buf[half, :, cols] = approx.astype(BF16)
-            outgoing = [
-                pltpu.make_async_copy(
-                    error_buf.at[half, :, cols], new_errors.at[:, at], error_sems.at[half, chunk]
-                ),
-                pltpu.make_async_copy(
-                    update_buf.at[half, :, cols], update.at[:, at], update_sems.at[half, chunk]
-                ),
-            ]
-            for copy in outgoing:
-                copy.start()
-            copies += outgoing
+            error_copy = pltpu.make_async_copy(
+                error_buf.at[half, :, cols], new_errors.at[:, at], error_sems.at[half, chunk]
+            )
+            error_copy.start()
+            copies += [update_copy, error_copy]
     for copy in copies:
         copy.wait()
 

time: 62.3 us -> 62.4 us (level)
  transfers between devices with their start and end apart: 5 -> 5, of which waited for: 3 -> 1; matrix products, arithmetic and copies ran while one was open for 0% -> 0% of each run, Pallas kernels for 8% -> 8%
where the time goes in v7:
time: 62.4 us; the launch traced here: 62 us
  blocking collectives  39.7 us (64%)
  starting transfers between devices  10.5 us (17%)
  Pallas kernels  10.3 us (17%)
  waiting for transfers between devices  0.77 us (1%)
  between operations  0.72 us (1%)
    all_to_all x1, blocking collectives, reduce_and_gather(): block = add_up(lax.all_to_all(repeat(block, Z), 'z', 0, 0))  16 us
    all_to_all x1, blocking collectives, reduce_and_gather(): block = add_up(lax.all_to_all(mine, ('x', 'y'), 0, 0))  12.6 us
    all_to_all x1, blocking collectives, reduce_and_gather(): return lax.all_to_all(repeat(block, BLOCKS), ('x', 'y'), 0, 0)  11.1 us
    ppermute x5, starting transfers between devices, send(): return lax.ppermute(array, axis, list(enumerate(targets)))  10.5 us
    pallas_call x2, Pallas kernels, compensate(): pl.pallas_call(functools.partial(compensate_kernel, own), out_shape=(pltp...  4.07 us
    pallas_call x1, Pallas kernels, apply(): pl.pallas_call(apply_kernel, out_shape=(jax.ShapeDtypeStruct((ROWS, FEATU...  3.04 us
    pallas_call x1, Pallas kernels, factor(): pl.pallas_call(factor_kernel, out_shape=(pltpu.VMEM((RANK, RANK), F32), o...  2.3 us
  transfers between devices with their start and end apart: 5, of which 1 were waited for; matrix products, arithmetic and copies ran while one was open for 0% of the time, Pallas kernels for 8%

profile of v7, /device:TPU:1, one launch (start us, length us, event | category | flops | bytes accessed | tf_op | source)
XLA Modules:
  0.0 62.0 jit_solution(11948207201638088597)
XLA Ops:
  0.6 2.0 %compensate_other.1 = (f32[224,2048]{1,0:T(8,128)S(1)}, bf16[224,2048]{1,0:T(8,128)(2,1)S(1)}, f32[16,32,128]{2,1,0:T(8,128)S(1)}) custom-call(bf16[224,4096]{1,0:T(8,128)(2,1)} %bitcast.11, f32[224,4096]{1,0:T(8,128)} %bitcast.9, bf16[32,224]{1,0:T(8,128)(2,1)} %bitcast.13), custom_call_target="tpu_custom_call" | custom-call | flops 29360128 | bytes 2752512 | tf_op jit(solution)/shard_map/compensate_other/pallas_call | solution.py:92
  2.7 3.3 %collective-permute-start = (f32[16,32,128]{2,1,0:T(8,128)S(1)}, f32[16,32,128]{2,1,0:T(8,128)S(1)}, u32[]{:S(2)}, u32[]{:S(2)}) collective-permute-start(f32[16,32,128]{2,1,0:T(8,128)S(1)} %get-tuple-element.23), channel_id=1, source_target_pairs={{0,1},{1,0},{2,3},{3,2},{4,5},{5,4},{6,7},{7,6},{8,9},{9,8},{10,11... | collective-permute-start | bytes 786440 | tf_op jit(solution)/shard_map/ppermute | solution.py:296
  6.0 2.0 %compensate_own.1 = (f32[224,2048]{1,0:T(8,128)S(1)}, bf16[224,2048]{1,0:T(8,128)(2,1)S(1)}, f32[16,32,128]{2,1,0:T(8,128)S(1)}) custom-call(bf16[224,4096]{1,0:T(8,128)(2,1)} %bitcast.12, f32[224,4096]{1,0:T(8,128)} %bitcast.10, bf16[32,224]{1,0:T(8,128)(2,1)} %bitcast.14), custom_call_target="tpu_custom_call" | custom-call | flops 29360128 | bytes 2752512 | tf_op jit(solution)/shard_map/compensate_own/pallas_call | solution.py:92
  8.0 0.0 collective-permute-done
  8.1 12.6 %all_to_all.15 = f32[16,32,128]{2,1,0:T(8,128)S(1)} all-to-all(f32[16,32,128]{2,1,0:T(8,128)S(1)} %add.95), channel_id=1, replica_groups=mesh['x'=4,'y'=4,'z'=8,'c'=2] {'x','y'}, dimensions={0} | all-to-all | bytes 524288 | tf_op jit(solution)/shard_map/all_to_all | solution.py:311
  20.8 16.0 %all_to_all.16 = f32[8,32,128]{2,1,0:T(8,128)S(1)} all-to-all(f32[8,32,128]{2,1,0:T(8,128)S(1)} %broadcast_in_dim.9), channel_id=1, replica_groups=mesh['x'=4,'y'=4,'z'=8,'c'=2] {'z'}, dimensions={0} | all-to-all | bytes 262144 | tf_op jit(solution)/shard_map/all_to_all | solution.py:312
  36.8 11.1 %all_to_all.17.blocks = f32[16,32,128]{2,1,0:T(8,128)S(1)} all-to-all(f32[16,32,128]{2,1,0:T(8,128)S(1)} %broadcast_in_dim.10), channel_id=1, replica_groups=mesh['x'=4,'y'=4,'z'=8,'c'=2] {'x','y'}, dimensions={0} | all-to-all | bytes 524288 | tf_op jit(solution)/shard_map/all_to_all | solution.py:313
  47.9 3.8 %collective-permute-start.1 = (f32[16,32,128]{2,1,0:T(8,128)S(1)}, f32[16,32,128]{2,1,0:T(8,128)S(1)}, u32[]{:S(2)}, u32[]{:S(2)}) collective-permute-start(f32[16,32,128]{2,1,0:T(8,128)S(1)} %all_to_all.17.blocks), channel_id=1, source_target_pairs={{0,1},{1,0},{2,3},{3,2},{4,5},{5,4},{6,7},{7,6},{8,9},{9,8},{10,11... | collective-permute-start | bytes 786440 | tf_op jit(solution)/shard_map/ppermute | solution.py:296
  51.7 0.4 project.2
  52.1 0.8 %collective-permute-done.1.blocks = f32[16,32,128]{2,1,0:T(8,128)S(1)} collective-permute-done((f32[16,32,128]{2,1,0:T(8,128)S(1)}, f32[16,32,128]{2,1,0:T(8,128)S(1)}, u32[]{:S(2)}, u32[]{:S(2)}) %collective-permute-start.1) | collective-permute-done | bytes 262176 | tf_op jit(solution)/shard_map/ppermute | solution.py:296
  52.9 0.4 project.3
  53.3 0.9 %collective-permute-start.4 = (f32[32,256]{1,0:T(8,128)S(1)}, f32[32,256]{1,0:T(8,128)S(1)}, u32[]{:S(2)}, u32[]{:S(2)}) collective-permute-start(f32[32,256]{1,0:T(8,128)S(1)} %get-tuple-element.26.own), channel_id=1, source_target_pairs={{0,192},{64,128},{128,64},{192,0},{1,193},{65,129},{129,65},{193,1... | collective-permute-start | bytes 98312 | tf_op jit(solution)/shard_map/ppermute | solution.py:296
  54.2 1.0 %collective-permute-start.3 = (f32[32,256]{1,0:T(8,128)S(1)}, f32[32,256]{1,0:T(8,128)S(1)}, u32[]{:S(2)}, u32[]{:S(2)}) collective-permute-start(f32[32,256]{1,0:T(8,128)S(1)} %get-tuple-element.26.own), channel_id=1, source_target_pairs={{0,128},{64,192},{128,0},{192,64},{1,129},{65,193},{129,1},{193,65... | collective-permute-start | bytes 98312 | tf_op jit(solution)/shard_map/ppermute | solution.py:296
  55.2 1.5 %collective-permute-start.2 = (f32[32,256]{1,0:T(8,128)S(1)}, f32[32,256]{1,0:T(8,128)S(1)}, u32[]{:S(2)}, u32[]{:S(2)}) collective-permute-start(f32[32,256]{1,0:T(8,128)S(1)} %get-tuple-element.26.own), channel_id=1, source_target_pairs={{0,64},{64,0},{128,192},{192,128},{1,65},{65,1},{129,193},{193,129... | collective-permute-start | bytes 98312 | tf_op jit(solution)/shard_map/ppermute | solution.py:296
  56.6 2.3 %factor.1 = (f32[32,32]{1,0:T(8,128)S(1)}, bf16[64,2048]{1,0:T(8,128)(2,1)S(1)}, bf16[64,2048]{1,0:T(8,128)(2,1)S(1)}) custom-call(bf16[96,2048]{1,0:T(8,128)(2,1)S(1)} %get-tuple-element.27.own_terms, bf16[96,2048]{1,0:T(8,128)(2,1)S(1)} %get-tuple-element.28.other_terms), custom_call_target="tpu_custom_call" | custom-call | flops 1000000000 | bytes 10000000 | tf_op jit(solution)/shard_map/factor/pallas_call | solution.py:209
  59.0 0.0 collective-permute-done.4.second
  59.0 0.0 collective-permute-done.3.first
  59.0 0.0 collective-permute-done.2.pair
  59.0 3.0 %apply.1 = (f32[224,4096]{1,0:T(8,128)}, bf16[224,4096]{1,0:T(8,128)(2,1)}, f32[32,224]{1,0:T(8,128)}) custom-call(f32[224,2048]{1,0:T(8,128)S(1)} %get-tuple-element.19.own_comp, f32[224,2048]{1,0:T(8,128)S(1)} %get-tuple-element.20.other_comp, f32[32,256]{1,0:T(8,128)S(1)} %get-tuple-element.26.own, f32[32,256]{1,0:T(8,128)S(1)} %collective-permute-done.2.pair, ...), custom_call_target="tpu_custom_call" | custom-call | tf_op jit(solution)/shard_map/apply/pallas_call | solution.py:273
  (5 shorter events, 0.1 us)
Async XLA Ops:
  2.7 5.4 %collective-permute-start = (f32[16,32,128]{2,1,0:T(8,128)S(1)}, f32[16,32,128]{2,1,0:T(8,128)S(1)}, u32[]{:S(2)}, u32[]{:S(2)}) collective-permute-start(f32[16,32,128]{2,1,0:T(8,128)S(1)} %get-tuple-element.23), channel_id=1, source_target_pairs={{0,1},{1,0},{2,3},{3,2},{4,5},{5,4},{6,7},{7,6},{8,9},{9,8},{10,11... | collective-permute-start | bytes 786440 | tf_op jit(solution)/shard_map/ppermute | solution.py:296
  47.9 5.0 %collective-permute-start.1 = (f32[16,32,128]{2,1,0:T(8,128)S(1)}, f32[16,32,128]{2,1,0:T(8,128)S(1)}, u32[]{:S(2)}, u32[]{:S(2)}) collective-permute-start(f32[16,32,128]{2,1,0:T(8,128)S(1)} %all_to_all.17.blocks), channel_id=1, source_target_pairs={{0,1},{1,0},{2,3},{3,2},{4,5},{5,4},{6,7},{7,6},{8,9},{9,8},{10,11... | collective-permute-start | bytes 786440 | tf_op jit(solution)/shard_map/ppermute | solution.py:296
  53.3 5.7 %collective-permute-start.4 = (f32[32,256]{1,0:T(8,128)S(1)}, f32[32,256]{1,0:T(8,128)S(1)}, u32[]{:S(2)}, u32[]{:S(2)}) collective-permute-start(f32[32,256]{1,0:T(8,128)S(1)} %get-tuple-element.26.own), channel_id=1, source_target_pairs={{0,192},{64,128},{128,64},{192,0},{1,193},{65,129},{129,65},{193,1... | collective-permute-start | bytes 98312 | tf_op jit(solution)/shard_map/ppermute | solution.py:296
  54.2 4.8 %collective-permute-start.3 = (f32[32,256]{1,0:T(8,128)S(1)}, f32[32,256]{1,0:T(8,128)S(1)}, u32[]{:S(2)}, u32[]{:S(2)}) collective-permute-start(f32[32,256]{1,0:T(8,128)S(1)} %get-tuple-element.26.own), channel_id=1, source_target_pairs={{0,128},{64,192},{128,0},{192,64},{1,129},{65,193},{129,1},{193,65... | collective-permute-start | bytes 98312 | tf_op jit(solution)/shard_map/ppermute | solution.py:296
  55.2 3.8 %collective-permute-start.2 = (f32[32,256]{1,0:T(8,128)S(1)}, f32[32,256]{1,0:T(8,128)S(1)}, u32[]{:S(2)}, u32[]{:S(2)}) collective-permute-start(f32[32,256]{1,0:T(8,128)S(1)} %get-tuple-element.26.own), channel_id=1, source_target_pairs={{0,64},{64,0},{128,192},{192,128},{1,65},{65,1},{129,193},{193,129... | collective-permute-start | bytes 98312 | tf_op jit(solution)/shard_map/ppermute | solution.py:296

commit v8 on v7

--- a/solution.py
+++ b/solution.py
@@ -179,7 +179,13 @@
     return jnp.concatenate([w * lax.rsqrt(d) for w, d in zip(work, scale)])[:, RANK:]
 
 
-def factor_kernel(own_terms, other_terms, inverse, own_ortho, other_ortho):
+def ortho_terms(weights, terms):
+    one, two, three = (terms[t * RANK : (t + 1) * RANK] for t in range(3))
+    stack = jnp.concatenate([one, two, one, three, two, one])
+    return jnp.concatenate(two_terms(jnp.dot(weights, stack, preferred_element_type=F32)))
+
+
+def factor_kernel(own_terms, other_terms, inverse, weights, ortho):
     stacked = sum(
         lax.dot_general(terms[...], terms[...], CONTRACT_LAST, preferred_element_type=F32)
         for terms in (own_terms, other_terms)
@@ -193,22 +199,19 @@
     lower_inverse = inverse_of_lower(gram)
     inverse[...] = lower_inverse
     one, two, three = (term.astype(F32) for term in three_terms(lower_inverse))
-    weights = jnp.concatenate([one, one, two, one, two, three], axis=1).astype(BF16)
-    for terms, ortho in ((own_terms, own_ortho), (other_terms, other_ortho)):
-        for chunk in range(CHUNKS):
-            cols = in_half(chunk)
-            one, two, three = (terms[t * RANK : (t + 1) * RANK, cols] for t in range(3))
-            stack = jnp.concatenate([one, two, one, three, two, one])
-            high, low = two_terms(jnp.dot(weights, stack, preferred_element_type=F32))
-            ortho[:RANK, cols] = high
-            ortho[RANK:, cols] = low
+    beside = jnp.concatenate([one, one, two, one, two, three], axis=1).astype(BF16)
+    weights[...] = beside
+    ortho[...] = ortho_terms(beside, own_terms[:, in_half(0)])
 
 
 def factor(own_terms, other_terms):
-    ortho = pltpu.VMEM((2 * RANK, HALF), BF16)
     return pl.pallas_call(
         factor_kernel,
-        out_shape=(pltpu.VMEM((RANK, RANK), F32), ortho, ortho),
+        out_shape=(
+            pltpu.VMEM((RANK, RANK), F32),
+            pltpu.VMEM((RANK, 6 * RANK), BF16),
+            pltpu.VMEM((2 * RANK, WIDTH), BF16),
+        ),
         in_specs=[VMEM] * 2,
         out_specs=[VMEM] * 3,
         compiler_params=params(12),
@@ -225,8 +228,10 @@
     first,
     second,
     inverse,
-    own_ortho,
-    other_ortho,
+    weights,
+    first_ortho,
+    own_terms,
+    other_terms,
     new_errors,
     update,
     new_q,
@@ -246,13 +251,14 @@
     copies[0].start()
     high = q_t.astype(BF16).astype(F32)
     stacked = jnp.concatenate([high, high, q_t - high]).T[:ROWS].astype(BF16)
-    for half, (comp, ortho) in enumerate(((own_comp, own_ortho), (other_comp, other_ortho))):
+    for half, (comp, terms) in enumerate(((own_comp, own_terms), (other_comp, other_terms))):
         start = half_start(half == 0)
         for chunk in range(CHUNKS):
             cols, at = in_half(chunk), in_hbm(start, chunk)
-            terms = ortho[:, cols]
-            terms = jnp.concatenate([terms, terms[:RANK]])
-            approx = jnp.dot(stacked, terms, preferred_element_type=F32)
+            ready = half == 0 and chunk == 0
+            ortho = first_ortho[...] if ready else ortho_terms(weights[...], terms[:, cols])
+            ortho = jnp.concatenate([ortho, ortho[:RANK]])
+            approx = jnp.dot(stacked, ortho, preferred_element_type=F32)
             update_buf[half, :, cols] = approx.astype(BF16)
             update_copy = pltpu.make_async_copy(
                 update_buf.at[half, :, cols], update.at[:, at], update_sems.at[half, chunk]
@@ -268,7 +274,7 @@
         copy.wait()
 
 
-def apply(own_comp, other_comp, own, pair, first, second, inverse, own_ortho, other_ortho):
+def apply(own_comp, other_comp, *operands):
     comps = [pltpu.with_memory_space_constraint(a, pltpu.VMEM) for a in (own_comp, other_comp)]
     return pl.pallas_call(
         apply_kernel,
@@ -277,7 +283,7 @@
             jax.ShapeDtypeStruct((ROWS, FEATURES), BF16),
             jax.ShapeDtypeStruct((RANK, ROWS), F32),
         ),
-        in_specs=[VMEM] * 9,
+        in_specs=[VMEM] * (2 + len(operands)),
         out_specs=[HBM] * 3,
         scratch_shapes=[
             pltpu.VMEM((C, ROWS, HALF), F32),
@@ -289,7 +295,7 @@
         ],
         compiler_params=params(20),
         name="apply",
-    )(*comps, own, pair, first, second, inverse, own_ortho, other_ortho)
+    )(*comps, *operands)
 
 
 def send(array, axis, targets):
@@ -323,9 +329,9 @@
     product, own_terms = project(own_low, mine)
     product, other_terms = project(other_low, other, product)
     pair, first, second = (send(product, "x", targets) for targets in REPLICAS)
-    inverse, own_ortho, other_ortho = factor(own_terms, other_terms)
+    factors = factor(own_terms, other_terms)
     new_errors, update, new_q = apply(
-        own_comp, other_comp, product, pair, first, second, inverse, own_ortho, other_ortho
+        own_comp, other_comp, product, pair, first, second, *factors, own_terms, other_terms
     )
     return (update, new_errors[None], new_q.T)
 

time: 62.4 us -> 62.2 us (level)
  transfers between devices with their start and end apart: 5 -> 5, of which waited for: 1 -> 1; matrix products, arithmetic and copies ran while one was open for 0% -> 0% of each run, Pallas kernels for 8% -> 7%
where the time goes in v8:
time: 62.2 us; the launch traced here: 61.6 us
  blocking collectives  39.7 us (64%)
  starting transfers between devices  10.5 us (17%)
  Pallas kernels  9.78 us (16%)
  waiting for transfers between devices  0.79 us (1%)
  between operations  0.71 us (1%)
    all_to_all x1, blocking collectives, reduce_and_gather(): block = add_up(lax.all_to_all(repeat(block, Z), 'z', 0, 0))  16 us
    all_to_all x1, blocking collectives, reduce_and_gather(): block = add_up(lax.all_to_all(mine, ('x', 'y'), 0, 0))  12.6 us
    all_to_all x1, blocking collectives, reduce_and_gather(): return lax.all_to_all(repeat(block, BLOCKS), ('x', 'y'), 0, 0)  11.1 us
    ppermute x5, starting transfers between devices, send(): return lax.ppermute(array, axis, list(enumerate(targets)))  10.5 us
    pallas_call x2, Pallas kernels, compensate(): pl.pallas_call(functools.partial(compensate_kernel, own), out_shape=(pltp...  4.07 us
    pallas_call x1, Pallas kernels, apply(): pl.pallas_call(apply_kernel, out_shape=(jax.ShapeDtypeStruct((ROWS, FEATU...  3.01 us
    pallas_call x1, Pallas kernels, factor(): pl.pallas_call(factor_kernel, out_shape=(pltpu.VMEM((RANK, RANK), F32), p...  1.86 us
  transfers between devices with their start and end apart: 5, of which 1 were waited for; matrix products, arithmetic and copies ran while one was open for 0% of the time, Pallas kernels for 7%

profile of v8, /device:TPU:1, one launch (start us, length us, event | category | flops | bytes accessed | tf_op | source)
XLA Modules:
  0.0 61.6 jit_solution(12926638477075930042)
XLA Ops:
  0.6 2.0 %compensate_other.1 = (f32[224,2048]{1,0:T(8,128)S(1)}, bf16[224,2048]{1,0:T(8,128)(2,1)S(1)}, f32[16,32,128]{2,1,0:T(8,128)S(1)}) custom-call(bf16[224,4096]{1,0:T(8,128)(2,1)} %bitcast.11, f32[224,4096]{1,0:T(8,128)} %bitcast.9, bf16[32,224]{1,0:T(8,128)(2,1)} %bitcast.13), custom_call_target="tpu_custom_call" | custom-call | flops 29360128 | bytes 2752512 | tf_op jit(solution)/shard_map/compensate_other/pallas_call | solution.py:92
  2.7 3.3 %collective-permute-start = (f32[16,32,128]{2,1,0:T(8,128)S(1)}, f32[16,32,128]{2,1,0:T(8,128)S(1)}, u32[]{:S(2)}, u32[]{:S(2)}) collective-permute-start(f32[16,32,128]{2,1,0:T(8,128)S(1)} %get-tuple-element.23), channel_id=1, source_target_pairs={{0,1},{1,0},{2,3},{3,2},{4,5},{5,4},{6,7},{7,6},{8,9},{9,8},{10,11... | collective-permute-start | bytes 786440 | tf_op jit(solution)/shard_map/ppermute | solution.py:302
  6.0 2.0 %compensate_own.1 = (f32[224,2048]{1,0:T(8,128)S(1)}, bf16[224,2048]{1,0:T(8,128)(2,1)S(1)}, f32[16,32,128]{2,1,0:T(8,128)S(1)}) custom-call(bf16[224,4096]{1,0:T(8,128)(2,1)} %bitcast.12, f32[224,4096]{1,0:T(8,128)} %bitcast.10, bf16[32,224]{1,0:T(8,128)(2,1)} %bitcast.14), custom_call_target="tpu_custom_call" | custom-call | flops 29360128 | bytes 2752512 | tf_op jit(solution)/shard_map/compensate_own/pallas_call | solution.py:92
  8.0 0.0 collective-permute-done
  8.1 12.6 %all_to_all.15 = f32[16,32,128]{2,1,0:T(8,128)S(1)} all-to-all(f32[16,32,128]{2,1,0:T(8,128)S(1)} %add.95), channel_id=1, replica_groups=mesh['x'=4,'y'=4,'z'=8,'c'=2] {'x','y'}, dimensions={0} | all-to-all | bytes 524288 | tf_op jit(solution)/shard_map/all_to_all | solution.py:317
  20.8 16.0 %all_to_all.16 = f32[8,32,128]{2,1,0:T(8,128)S(1)} all-to-all(f32[8,32,128]{2,1,0:T(8,128)S(1)} %broadcast_in_dim.9), channel_id=1, replica_groups=mesh['x'=4,'y'=4,'z'=8,'c'=2] {'z'}, dimensions={0} | all-to-all | bytes 262144 | tf_op jit(solution)/shard_map/all_to_all | solution.py:318
  36.8 11.1 %all_to_all.17.blocks = f32[16,32,128]{2,1,0:T(8,128)S(1)} all-to-all(f32[16,32,128]{2,1,0:T(8,128)S(1)} %broadcast_in_dim.10), channel_id=1, replica_groups=mesh['x'=4,'y'=4,'z'=8,'c'=2] {'x','y'}, dimensions={0} | all-to-all | bytes 524288 | tf_op jit(solution)/shard_map/all_to_all | solution.py:319
  47.9 3.8 %collective-permute-start.1 = (f32[16,32,128]{2,1,0:T(8,128)S(1)}, f32[16,32,128]{2,1,0:T(8,128)S(1)}, u32[]{:S(2)}, u32[]{:S(2)}) collective-permute-start(f32[16,32,128]{2,1,0:T(8,128)S(1)} %all_to_all.17.blocks), channel_id=1, source_target_pairs={{0,1},{1,0},{2,3},{3,2},{4,5},{5,4},{6,7},{7,6},{8,9},{9,8},{10,11... | collective-permute-start | bytes 786440 | tf_op jit(solution)/shard_map/ppermute | solution.py:302
  51.7 0.4 project.2
  52.1 0.8 %collective-permute-done.1.blocks = f32[16,32,128]{2,1,0:T(8,128)S(1)} collective-permute-done((f32[16,32,128]{2,1,0:T(8,128)S(1)}, f32[16,32,128]{2,1,0:T(8,128)S(1)}, u32[]{:S(2)}, u32[]{:S(2)}) %collective-permute-start.1) | collective-permute-done | bytes 262176 | tf_op jit(solution)/shard_map/ppermute | solution.py:302
  52.9 0.4 project.3
  53.3 0.9 %collective-permute-start.4 = (f32[32,256]{1,0:T(8,128)S(1)}, f32[32,256]{1,0:T(8,128)S(1)}, u32[]{:S(2)}, u32[]{:S(2)}) collective-permute-start(f32[32,256]{1,0:T(8,128)S(1)} %get-tuple-element.26.own), channel_id=1, source_target_pairs={{0,192},{64,128},{128,64},{192,0},{1,193},{65,129},{129,65},{193,1... | collective-permute-start | bytes 98312 | tf_op jit(solution)/shard_map/ppermute | solution.py:302
  54.2 1.0 %collective-permute-start.3 = (f32[32,256]{1,0:T(8,128)S(1)}, f32[32,256]{1,0:T(8,128)S(1)}, u32[]{:S(2)}, u32[]{:S(2)}) collective-permute-start(f32[32,256]{1,0:T(8,128)S(1)} %get-tuple-element.26.own), channel_id=1, source_target_pairs={{0,128},{64,192},{128,0},{192,64},{1,129},{65,193},{129,1},{193,65... | collective-permute-start | bytes 98312 | tf_op jit(solution)/shard_map/ppermute | solution.py:302
  55.2 1.5 %collective-permute-start.2 = (f32[32,256]{1,0:T(8,128)S(1)}, f32[32,256]{1,0:T(8,128)S(1)}, u32[]{:S(2)}, u32[]{:S(2)}) collective-permute-start(f32[32,256]{1,0:T(8,128)S(1)} %get-tuple-element.26.own), channel_id=1, source_target_pairs={{0,64},{64,0},{128,192},{192,128},{1,65},{65,1},{129,193},{193,129... | collective-permute-start | bytes 98312 | tf_op jit(solution)/shard_map/ppermute | solution.py:302
  56.6 1.9 %factor.1 = (f32[32,32]{1,0:T(8,128)S(1)}, bf16[32,192]{1,0:T(8,128)(2,1)S(1)}, bf16[64,1024]{1,0:T(8,128)(2,1)S(1)}) custom-call(bf16[96,2048]{1,0:T(8,128)(2,1)S(1)} %get-tuple-element.27.own_terms, bf16[96,2048]{1,0:T(8,128)(2,1)S(1)} %get-tuple-element.28.other_terms), custom_call_target="tpu_custom_call" | custom-call | flops 1000000000 | bytes 10000000 | tf_op jit(solution)/shard_map/factor/pallas_call | solution.py:208
  58.5 0.0 collective-permute-done.4.second
  58.5 0.0 collective-permute-done.3.first
  58.6 0.0 collective-permute-done.2.pair
  58.6 3.0 %apply.1 = (f32[224,4096]{1,0:T(8,128)}, bf16[224,4096]{1,0:T(8,128)(2,1)}, f32[32,224]{1,0:T(8,128)}) custom-call(f32[224,2048]{1,0:T(8,128)S(1)} %get-tuple-element.19.own_comp, f32[224,2048]{1,0:T(8,128)S(1)} %get-tuple-element.20.other_comp, f32[32,256]{1,0:T(8,128)S(1)} %get-tuple-element.26.own, f32[32,256]{1,0:T(8,128)S(1)} %collective-permute-done.2.pair, ...), custom_call_target="tpu_custom_call" | custom-call | tf_op jit(solution)/shard_map/apply/pallas_call | solution.py:279
  (5 shorter events, 0.1 us)
Async XLA Ops:
  2.7 5.4 %collective-permute-start = (f32[16,32,128]{2,1,0:T(8,128)S(1)}, f32[16,32,128]{2,1,0:T(8,128)S(1)}, u32[]{:S(2)}, u32[]{:S(2)}) collective-permute-start(f32[16,32,128]{2,1,0:T(8,128)S(1)} %get-tuple-element.23), channel_id=1, source_target_pairs={{0,1},{1,0},{2,3},{3,2},{4,5},{5,4},{6,7},{7,6},{8,9},{9,8},{10,11... | collective-permute-start | bytes 786440 | tf_op jit(solution)/shard_map/ppermute | solution.py:302
  47.9 5.0 %collective-permute-start.1 = (f32[16,32,128]{2,1,0:T(8,128)S(1)}, f32[16,32,128]{2,1,0:T(8,128)S(1)}, u32[]{:S(2)}, u32[]{:S(2)}) collective-permute-start(f32[16,32,128]{2,1,0:T(8,128)S(1)} %all_to_all.17.blocks), channel_id=1, source_target_pairs={{0,1},{1,0},{2,3},{3,2},{4,5},{5,4},{6,7},{7,6},{8,9},{9,8},{10,11... | collective-permute-start | bytes 786440 | tf_op jit(solution)/shard_map/ppermute | solution.py:302
  53.3 5.2 %collective-permute-start.4 = (f32[32,256]{1,0:T(8,128)S(1)}, f32[32,256]{1,0:T(8,128)S(1)}, u32[]{:S(2)}, u32[]{:S(2)}) collective-permute-start(f32[32,256]{1,0:T(8,128)S(1)} %get-tuple-element.26.own), channel_id=1, source_target_pairs={{0,192},{64,128},{128,64},{192,0},{1,193},{65,129},{129,65},{193,1... | collective-permute-start | bytes 98312 | tf_op jit(solution)/shard_map/ppermute | solution.py:302
  54.2 4.4 %collective-permute-start.3 = (f32[32,256]{1,0:T(8,128)S(1)}, f32[32,256]{1,0:T(8,128)S(1)}, u32[]{:S(2)}, u32[]{:S(2)}) collective-permute-start(f32[32,256]{1,0:T(8,128)S(1)} %get-tuple-element.26.own), channel_id=1, source_target_pairs={{0,128},{64,192},{128,0},{192,64},{1,129},{65,193},{129,1},{193,65... | collective-permute-start | bytes 98312 | tf_op jit(solution)/shard_map/ppermute | solution.py:302
  55.2 3.4 %collective-permute-start.2 = (f32[32,256]{1,0:T(8,128)S(1)}, f32[32,256]{1,0:T(8,128)S(1)}, u32[]{:S(2)}, u32[]{:S(2)}) collective-permute-start(f32[32,256]{1,0:T(8,128)S(1)} %get-tuple-element.26.own), channel_id=1, source_target_pairs={{0,64},{64,0},{128,192},{192,128},{1,65},{65,1},{129,193},{193,129... | collective-permute-start | bytes 98312 | tf_op jit(solution)/shard_map/ppermute | solution.py:302

commit v9 on v8

--- a/solution.py
+++ b/solution.py
@@ -21,6 +21,7 @@
 GROUP = 8
 SWAP = (1, 0)
 REPLICAS = ((1, 0, 3, 2), (2, 3, 0, 1), (3, 2, 1, 0))
+OWNERS = [[C * z + (half + z // (Z // C)) % C for z in range(Z)] for half in range(C)]
 F32, BF16 = jnp.float32, jnp.bfloat16
 CONTRACT_LAST = (((1,), (1,)), ((), ()))
 VMEM = pl.BlockSpec(memory_space=pltpu.VMEM)
@@ -28,8 +29,8 @@
 
 
 def half_start(own):
-    core = lax.axis_index("c")
-    return (core if own else 1 - core) * HALF
+    half = lax.rem(lax.axis_index("c") + lax.div(lax.axis_index("z"), Z // C), C)
+    return (half if own else 1 - half) * HALF
 
 
 def in_hbm(start, chunk):
@@ -315,7 +316,7 @@
 
 def reduce_and_gather(mine):
     block = add_up(lax.all_to_all(mine, ("x", "y"), 0, 0))
-    block = add_up(lax.all_to_all(repeat(block, Z), "z", 0, 0))
+    block = add_up(lax.all_to_all(repeat(block, Z), ("z", "c"), 0, 0, axis_index_groups=OWNERS))
     return lax.all_to_all(repeat(block, BLOCKS), ("x", "y"), 0, 0)
 
 

time: 62.2 us -> 60.9 us (0.979)
  starting transfers between devices: 10.5 us -> 6.67 us
  blocking collectives: 39.7 us -> 42.1 us
    ppermute x5, starting transfers between devices: 10.5 us -> 6.67 us  [send(): return lax.ppermute(array, axis, list(enumerate(targets)))]
    all_to_all x1, blocking collectives: 16 us -> 18.1 us  [reduce_and_gather(): lax.all_to_all(repeat(block, Z), ('z', 'c'), 0, 0, axis_index_groups=OWNERS)]
where the time goes in v9:
time: 60.9 us; the launch traced here: 60.5 us
  blocking collectives  42.1 us (69%)
  Pallas kernels  9.79 us (16%)
  starting transfers between devices  6.67 us (11%)
  waiting for transfers between devices  1.17 us (2%)
  between operations  0.71 us (1%)
    all_to_all x1, blocking collectives, reduce_and_gather(): lax.all_to_all(repeat(block, Z), ('z', 'c'), 0, 0, axis_index_groups=OWNERS)  18.1 us
    all_to_all x1, blocking collectives, reduce_and_gather(): block = add_up(lax.all_to_all(mine, ('x', 'y'), 0, 0))  12.6 us
    all_to_all x1, blocking collectives, reduce_and_gather(): return lax.all_to_all(repeat(block, BLOCKS), ('x', 'y'), 0, 0)  11.3 us
    ppermute x5, starting transfers between devices, send(): return lax.ppermute(array, axis, list(enumerate(targets)))  6.67 us
    pallas_call x2, Pallas kernels, compensate(): pl.pallas_call(functools.partial(compensate_kernel, own), out_shape=(pltp...  4.07 us
    pallas_call x1, Pallas kernels, apply(): pl.pallas_call(apply_kernel, out_shape=(jax.ShapeDtypeStruct((ROWS, FEATU...  3.02 us
    pallas_call x1, Pallas kernels, factor(): pl.pallas_call(factor_kernel, out_shape=(pltpu.VMEM((RANK, RANK), F32), p...  1.86 us
  transfers between devices with their start and end apart: 5, of which 1 were waited for; matrix products, arithmetic and copies ran while one was open for 0% of the time, Pallas kernels for 7%

profile of v9, /device:TPU:1, one launch (start us, length us, event | category | flops | bytes accessed | tf_op | source)
XLA Modules:
  0.0 60.5 jit_solution(10760501678562533316)
XLA Ops:
  0.6 2.0 %compensate_other.1 = (f32[224,2048]{1,0:T(8,128)S(1)}, bf16[224,2048]{1,0:T(8,128)(2,1)S(1)}, f32[16,32,128]{2,1,0:T(8,128)S(1)}) custom-call(bf16[224,4096]{1,0:T(8,128)(2,1)} %bitcast.11, f32[224,4096]{1,0:T(8,128)} %bitcast.9, bf16[32,224]{1,0:T(8,128)(2,1)} %bitcast.13), custom_call_target="tpu_custom_call" | custom-call | flops 29360128 | bytes 2752512 | tf_op jit(solution)/shard_map/compensate_other/pallas_call | solution.py:93
  2.7 3.3 %collective-permute-start = (f32[16,32,128]{2,1,0:T(8,128)S(1)}, f32[16,32,128]{2,1,0:T(8,128)S(1)}, u32[]{:S(2)}, u32[]{:S(2)}) collective-permute-start(f32[16,32,128]{2,1,0:T(8,128)S(1)} %get-tuple-element.23), channel_id=1, source_target_pairs={{0,1},{1,0},{2,3},{3,2},{4,5},{5,4},{6,7},{7,6},{8,9},{9,8},{10,11... | collective-permute-start | bytes 786440 | tf_op jit(solution)/shard_map/ppermute | solution.py:303
  6.0 2.0 %compensate_own.1 = (f32[224,2048]{1,0:T(8,128)S(1)}, bf16[224,2048]{1,0:T(8,128)(2,1)S(1)}, f32[16,32,128]{2,1,0:T(8,128)S(1)}) custom-call(bf16[224,4096]{1,0:T(8,128)(2,1)} %bitcast.12, f32[224,4096]{1,0:T(8,128)} %bitcast.10, bf16[32,224]{1,0:T(8,128)(2,1)} %bitcast.14), custom_call_target="tpu_custom_call" | custom-call | flops 29360128 | bytes 2752512 | tf_op jit(solution)/shard_map/compensate_own/pallas_call | solution.py:93
  8.0 0.0 collective-permute-done
  8.1 12.6 %all_to_all.15 = f32[16,32,128]{2,1,0:T(8,128)S(1)} all-to-all(f32[16,32,128]{2,1,0:T(8,128)S(1)} %add.95), channel_id=1, replica_groups=mesh['x'=4,'y'=4,'z'=8,'c'=2] {'x','y'}, dimensions={0} | all-to-all | bytes 524288 | tf_op jit(solution)/shard_map/all_to_all | solution.py:318
  20.8 18.1 %all_to_all.16 = f32[8,32,128]{2,1,0:T(8,128)S(1)} all-to-all(f32[8,32,128]{2,1,0:T(8,128)S(1)} %broadcast_in_dim.9), channel_id=1, replica_groups={{0,2,4,6,9,11,13,15},{1,3,5,7,8,10,12,14},{16,18,20,22,25,27,29,31},{17..., dimensions={0} | all-to-all | bytes 262144 | tf_op jit(solution)/shard_map/all_to_all | solution.py:319
  38.9 11.3 %all_to_all.17.blocks = f32[16,32,128]{2,1,0:T(8,128)S(1)} all-to-all(f32[16,32,128]{2,1,0:T(8,128)S(1)} %broadcast_in_dim.10), channel_id=1, replica_groups=mesh['x'=4,'y'=4,'z'=8,'c'=2] {'x','y'}, dimensions={0} | all-to-all | bytes 524288 | tf_op jit(solution)/shard_map/all_to_all | solution.py:320
  50.3 0.0 collective-permute-start.1
  50.3 0.4 project.2
  50.7 1.1 %collective-permute-done.1.blocks = f32[16,32,128]{2,1,0:T(8,128)S(1)} collective-permute-done((f32[16,32,128]{2,1,0:T(8,128)S(1)}, f32[16,32,128]{2,1,0:T(8,128)S(1)}, u32[]{:S(2)}, u32[]{:S(2)}) %collective-permute-start.1) | collective-permute-done | bytes 262176 | tf_op jit(solution)/shard_map/ppermute | solution.py:303
  51.8 0.4 project.3
  52.2 1.0 %collective-permute-start.4 = (f32[32,256]{1,0:T(8,128)S(1)}, f32[32,256]{1,0:T(8,128)S(1)}, u32[]{:S(2)}, u32[]{:S(2)}) collective-permute-start(f32[32,256]{1,0:T(8,128)S(1)} %get-tuple-element.26.own), channel_id=1, source_target_pairs={{0,192},{64,128},{128,64},{192,0},{1,193},{65,129},{129,65},{193,1... | collective-permute-start | bytes 98312 | tf_op jit(solution)/shard_map/ppermute | solution.py:303
  53.2 0.7 %collective-permute-start.3 = (f32[32,256]{1,0:T(8,128)S(1)}, f32[32,256]{1,0:T(8,128)S(1)}, u32[]{:S(2)}, u32[]{:S(2)}) collective-permute-start(f32[32,256]{1,0:T(8,128)S(1)} %get-tuple-element.26.own), channel_id=1, source_target_pairs={{0,128},{64,192},{128,0},{192,64},{1,129},{65,193},{129,1},{193,65... | collective-permute-start | bytes 98312 | tf_op jit(solution)/shard_map/ppermute | solution.py:303
  53.9 1.7 %collective-permute-start.2 = (f32[32,256]{1,0:T(8,128)S(1)}, f32[32,256]{1,0:T(8,128)S(1)}, u32[]{:S(2)}, u32[]{:S(2)}) collective-permute-start(f32[32,256]{1,0:T(8,128)S(1)} %get-tuple-element.26.own), channel_id=1, source_target_pairs={{0,64},{64,0},{128,192},{192,128},{1,65},{65,1},{129,193},{193,129... | collective-permute-start | bytes 98312 | tf_op jit(solution)/shard_map/ppermute | solution.py:303
  55.6 1.9 %factor.1 = (f32[32,32]{1,0:T(8,128)S(1)}, bf16[32,192]{1,0:T(8,128)(2,1)S(1)}, bf16[64,1024]{1,0:T(8,128)(2,1)S(1)}) custom-call(bf16[96,2048]{1,0:T(8,128)(2,1)S(1)} %get-tuple-element.27.own_terms, bf16[96,2048]{1,0:T(8,128)(2,1)S(1)} %get-tuple-element.28.other_terms), custom_call_target="tpu_custom_call" | custom-call | flops 1000000000 | bytes 10000000 | tf_op jit(solution)/shard_map/factor/pallas_call | solution.py:209
  57.5 0.0 collective-permute-done.4.second
  57.5 0.0 collective-permute-done.3.first
  57.5 0.0 collective-permute-done.2.pair
  57.5 3.0 %apply.1 = (f32[224,4096]{1,0:T(8,128)}, bf16[224,4096]{1,0:T(8,128)(2,1)}, f32[32,224]{1,0:T(8,128)}) custom-call(f32[224,2048]{1,0:T(8,128)S(1)} %get-tuple-element.19.own_comp, f32[224,2048]{1,0:T(8,128)S(1)} %get-tuple-element.20.other_comp, f32[32,256]{1,0:T(8,128)S(1)} %get-tuple-element.26.own, f32[32,256]{1,0:T(8,128)S(1)} %collective-permute-done.2.pair, ...), custom_call_target="tpu_custom_call" | custom-call | tf_op jit(solution)/shard_map/apply/pallas_call | solution.py:280
  (5 shorter events, 0.1 us)
Async XLA Ops:
  2.7 5.4 %collective-permute-start = (f32[16,32,128]{2,1,0:T(8,128)S(1)}, f32[16,32,128]{2,1,0:T(8,128)S(1)}, u32[]{:S(2)}, u32[]{:S(2)}) collective-permute-start(f32[16,32,128]{2,1,0:T(8,128)S(1)} %get-tuple-element.23), channel_id=1, source_target_pairs={{0,1},{1,0},{2,3},{3,2},{4,5},{5,4},{6,7},{7,6},{8,9},{9,8},{10,11... | collective-permute-start | bytes 786440 | tf_op jit(solution)/shard_map/ppermute | solution.py:303
  50.3 1.5 %collective-permute-start.1 = (f32[16,32,128]{2,1,0:T(8,128)S(1)}, f32[16,32,128]{2,1,0:T(8,128)S(1)}, u32[]{:S(2)}, u32[]{:S(2)}) collective-permute-start(f32[16,32,128]{2,1,0:T(8,128)S(1)} %all_to_all.17.blocks), channel_id=1, source_target_pairs={{0,1},{1,0},{2,3},{3,2},{4,5},{5,4},{6,7},{7,6},{8,9},{9,8},{10,11... | collective-permute-start | bytes 786440 | tf_op jit(solution)/shard_map/ppermute | solution.py:303
  52.2 5.2 %collective-permute-start.4 = (f32[32,256]{1,0:T(8,128)S(1)}, f32[32,256]{1,0:T(8,128)S(1)}, u32[]{:S(2)}, u32[]{:S(2)}) collective-permute-start(f32[32,256]{1,0:T(8,128)S(1)} %get-tuple-element.26.own), channel_id=1, source_target_pairs={{0,192},{64,128},{128,64},{192,0},{1,193},{65,129},{129,65},{193,1... | collective-permute-start | bytes 98312 | tf_op jit(solution)/shard_map/ppermute | solution.py:303
  53.2 4.3 %collective-permute-start.3 = (f32[32,256]{1,0:T(8,128)S(1)}, f32[32,256]{1,0:T(8,128)S(1)}, u32[]{:S(2)}, u32[]{:S(2)}) collective-permute-start(f32[32,256]{1,0:T(8,128)S(1)} %get-tuple-element.26.own), channel_id=1, source_target_pairs={{0,128},{64,192},{128,0},{192,64},{1,129},{65,193},{129,1},{193,65... | collective-permute-start | bytes 98312 | tf_op jit(solution)/shard_map/ppermute | solution.py:303
  53.9 3.6 %collective-permute-start.2 = (f32[32,256]{1,0:T(8,128)S(1)}, f32[32,256]{1,0:T(8,128)S(1)}, u32[]{:S(2)}, u32[]{:S(2)}) collective-permute-start(f32[32,256]{1,0:T(8,128)S(1)} %get-tuple-element.26.own), channel_id=1, source_target_pairs={{0,64},{64,0},{128,192},{192,128},{1,65},{65,1},{129,193},{193,129... | collective-permute-start | bytes 98312 | tf_op jit(solution)/shard_map/ppermute | solution.py:303

commit v10 on v9

--- a/solution.py
+++ b/solution.py
@@ -18,6 +18,7 @@
 BLOCK = HALF // BLOCKS
 CHUNKS = 2
 WIDTH = HALF // CHUNKS
+PARTS = ((0, 512), (512, HALF))
 GROUP = 8
 SWAP = (1, 0)
 REPLICAS = ((1, 0, 3, 2), (2, 3, 0, 1), (3, 2, 1, 0))
@@ -202,7 +203,7 @@
     one, two, three = (term.astype(F32) for term in three_terms(lower_inverse))
     beside = jnp.concatenate([one, one, two, one, two, three], axis=1).astype(BF16)
     weights[...] = beside
-    ortho[...] = ortho_terms(beside, own_terms[:, in_half(0)])
+    ortho[...] = ortho_terms(beside, own_terms[:, slice(*PARTS[0])])
 
 
 def factor(own_terms, other_terms):
@@ -211,7 +212,7 @@
         out_shape=(
             pltpu.VMEM((RANK, RANK), F32),
             pltpu.VMEM((RANK, 6 * RANK), BF16),
-            pltpu.VMEM((2 * RANK, WIDTH), BF16),
+            pltpu.VMEM((2 * RANK, PARTS[0][1]), BF16),
         ),
         in_specs=[VMEM] * 2,
         out_specs=[VMEM] * 3,
@@ -254,8 +255,9 @@
     stacked = jnp.concatenate([high, high, q_t - high]).T[:ROWS].astype(BF16)
     for half, (comp, terms) in enumerate(((own_comp, own_terms), (other_comp, other_terms))):
         start = half_start(half == 0)
-        for chunk in range(CHUNKS):
-            cols, at = in_half(chunk), in_hbm(start, chunk)
+        for chunk, (begin, end) in enumerate(PARTS):
+            cols = slice(begin, end)
+            at = pl.ds(pl.multiple_of(start + begin, PARTS[0][1]), end - begin)
             ready = half == 0 and chunk == 0
             ortho = first_ortho[...] if ready else ortho_terms(weights[...], terms[:, cols])
             ortho = jnp.concatenate([ortho, ortho[:RANK]])
@@ -290,8 +292,8 @@
             pltpu.VMEM((C, ROWS, HALF), F32),
             pltpu.VMEM((C, ROWS, HALF), BF16),
             pltpu.VMEM((RANK, ROWS), F32),
-            pltpu.SemaphoreType.DMA((C, CHUNKS)),
-            pltpu.SemaphoreType.DMA((C, CHUNKS)),
+            pltpu.SemaphoreType.DMA((C, len(PARTS))),
+            pltpu.SemaphoreType.DMA((C, len(PARTS))),
             pltpu.SemaphoreType.DMA,
         ],
         compiler_params=params(20),

time: 60.9 us -> 61 us (level)
  transfers between devices with their start and end apart: 5 -> 5, of which waited for: 1 -> 2; matrix products, arithmetic and copies ran while one was open for 0% -> 0% of each run, Pallas kernels for 7% -> 7%
where the time goes in v10:
time: 61 us; the launch traced here: 60.6 us
  blocking collectives  42.1 us (69%)
  Pallas kernels  9.79 us (16%)
  starting transfers between devices  6.67 us (11%)
  waiting for transfers between devices  1.25 us (2%)
  between operations  0.71 us (1%)
    all_to_all x1, blocking collectives, reduce_and_gather(): lax.all_to_all(repeat(block, Z), ('z', 'c'), 0, 0, axis_index_groups=OWNERS)  18.1 us
    all_to_all x1, blocking collectives, reduce_and_gather(): block = add_up(lax.all_to_all(mine, ('x', 'y'), 0, 0))  12.6 us
    all_to_all x1, blocking collectives, reduce_and_gather(): return lax.all_to_all(repeat(block, BLOCKS), ('x', 'y'), 0, 0)  11.3 us
    ppermute x5, starting transfers between devices, send(): return lax.ppermute(array, axis, list(enumerate(targets)))  6.67 us
    pallas_call x2, Pallas kernels, compensate(): pl.pallas_call(functools.partial(compensate_kernel, own), out_shape=(pltp...  4.07 us
    pallas_call x1, Pallas kernels, apply(): pl.pallas_call(apply_kernel, out_shape=(jax.ShapeDtypeStruct((ROWS, FEATU...  3.09 us
    pallas_call x1, Pallas kernels, factor(): pl.pallas_call(factor_kernel, out_shape=(pltpu.VMEM((RANK, RANK), F32), p...  1.78 us
    ppermute x5, waiting for transfers between devices, send(): return lax.ppermute(array, axis, list(enumerate(targets)))  1.25 us
  transfers between devices with their start and end apart: 5, of which 2 were waited for; matrix products, arithmetic and copies ran while one was open for 0% of the time, Pallas kernels for 7%

profile of v10, /device:TPU:1, one launch (start us, length us, event | category | flops | bytes accessed | tf_op | source)
XLA Modules:
  0.0 60.6 jit_solution(7233568552219924389)
XLA Ops:
  0.6 2.0 %compensate_other.1 = (f32[224,2048]{1,0:T(8,128)S(1)}, bf16[224,2048]{1,0:T(8,128)(2,1)S(1)}, f32[16,32,128]{2,1,0:T(8,128)S(1)}) custom-call(bf16[224,4096]{1,0:T(8,128)(2,1)} %bitcast.11, f32[224,4096]{1,0:T(8,128)} %bitcast.9, bf16[32,224]{1,0:T(8,128)(2,1)} %bitcast.13), custom_call_target="tpu_custom_call" | custom-call | flops 29360128 | bytes 2752512 | tf_op jit(solution)/shard_map/compensate_other/pallas_call | solution.py:94
  2.7 3.3 %collective-permute-start = (f32[16,32,128]{2,1,0:T(8,128)S(1)}, f32[16,32,128]{2,1,0:T(8,128)S(1)}, u32[]{:S(2)}, u32[]{:S(2)}) collective-permute-start(f32[16,32,128]{2,1,0:T(8,128)S(1)} %get-tuple-element.23), channel_id=1, source_target_pairs={{0,1},{1,0},{2,3},{3,2},{4,5},{5,4},{6,7},{7,6},{8,9},{9,8},{10,11... | collective-permute-start | bytes 786440 | tf_op jit(solution)/shard_map/ppermute | solution.py:305
  6.0 2.0 %compensate_own.1 = (f32[224,2048]{1,0:T(8,128)S(1)}, bf16[224,2048]{1,0:T(8,128)(2,1)S(1)}, f32[16,32,128]{2,1,0:T(8,128)S(1)}) custom-call(bf16[224,4096]{1,0:T(8,128)(2,1)} %bitcast.12, f32[224,4096]{1,0:T(8,128)} %bitcast.10, bf16[32,224]{1,0:T(8,128)(2,1)} %bitcast.14), custom_call_target="tpu_custom_call" | custom-call | flops 29360128 | bytes 2752512 | tf_op jit(solution)/shard_map/compensate_own/pallas_call | solution.py:94
  8.0 0.0 collective-permute-done
  8.1 12.6 %all_to_all.15 = f32[16,32,128]{2,1,0:T(8,128)S(1)} all-to-all(f32[16,32,128]{2,1,0:T(8,128)S(1)} %add.95), channel_id=1, replica_groups=mesh['x'=4,'y'=4,'z'=8,'c'=2] {'x','y'}, dimensions={0} | all-to-all | bytes 524288 | tf_op jit(solution)/shard_map/all_to_all | solution.py:320
  20.8 18.1 %all_to_all.16 = f32[8,32,128]{2,1,0:T(8,128)S(1)} all-to-all(f32[8,32,128]{2,1,0:T(8,128)S(1)} %broadcast_in_dim.9), channel_id=1, replica_groups={{0,2,4,6,9,11,13,15},{1,3,5,7,8,10,12,14},{16,18,20,22,25,27,29,31},{17..., dimensions={0} | all-to-all | bytes 262144 | tf_op jit(solution)/shard_map/all_to_all | solution.py:321
  38.9 11.3 %all_to_all.17.blocks = f32[16,32,128]{2,1,0:T(8,128)S(1)} all-to-all(f32[16,32,128]{2,1,0:T(8,128)S(1)} %broadcast_in_dim.10), channel_id=1, replica_groups=mesh['x'=4,'y'=4,'z'=8,'c'=2] {'x','y'}, dimensions={0} | all-to-all | bytes 524288 | tf_op jit(solution)/shard_map/all_to_all | solution.py:322
  50.3 0.0 collective-permute-start.1
  50.3 0.4 project.2
  50.7 1.1 %collective-permute-done.1.blocks = f32[16,32,128]{2,1,0:T(8,128)S(1)} collective-permute-done((f32[16,32,128]{2,1,0:T(8,128)S(1)}, f32[16,32,128]{2,1,0:T(8,128)S(1)}, u32[]{:S(2)}, u32[]{:S(2)}) %collective-permute-start.1) | collective-permute-done | bytes 262176 | tf_op jit(solution)/shard_map/ppermute | solution.py:305
  51.8 0.4 project.3
  52.2 1.0 %collective-permute-start.4 = (f32[32,256]{1,0:T(8,128)S(1)}, f32[32,256]{1,0:T(8,128)S(1)}, u32[]{:S(2)}, u32[]{:S(2)}) collective-permute-start(f32[32,256]{1,0:T(8,128)S(1)} %get-tuple-element.26.own), channel_id=1, source_target_pairs={{0,192},{64,128},{128,64},{192,0},{1,193},{65,129},{129,65},{193,1... | collective-permute-start | bytes 98312 | tf_op jit(solution)/shard_map/ppermute | solution.py:305
  53.2 0.7 %collective-permute-start.3 = (f32[32,256]{1,0:T(8,128)S(1)}, f32[32,256]{1,0:T(8,128)S(1)}, u32[]{:S(2)}, u32[]{:S(2)}) collective-permute-start(f32[32,256]{1,0:T(8,128)S(1)} %get-tuple-element.26.own), channel_id=1, source_target_pairs={{0,128},{64,192},{128,0},{192,64},{1,129},{65,193},{129,1},{193,65... | collective-permute-start | bytes 98312 | tf_op jit(solution)/shard_map/ppermute | solution.py:305
  53.9 1.7 %collective-permute-start.2 = (f32[32,256]{1,0:T(8,128)S(1)}, f32[32,256]{1,0:T(8,128)S(1)}, u32[]{:S(2)}, u32[]{:S(2)}) collective-permute-start(f32[32,256]{1,0:T(8,128)S(1)} %get-tuple-element.26.own), channel_id=1, source_target_pairs={{0,64},{64,0},{128,192},{192,128},{1,65},{65,1},{129,193},{193,129... | collective-permute-start | bytes 98312 | tf_op jit(solution)/shard_map/ppermute | solution.py:305
  55.6 1.8 %factor.1 = (f32[32,32]{1,0:T(8,128)S(1)}, bf16[32,192]{1,0:T(8,128)(2,1)S(1)}, bf16[64,512]{1,0:T(8,128)(2,1)S(1)}) custom-call(bf16[96,2048]{1,0:T(8,128)(2,1)S(1)} %get-tuple-element.27.own_terms, bf16[96,2048]{1,0:T(8,128)(2,1)S(1)} %get-tuple-element.28.other_terms), custom_call_target="tpu_custom_call" | custom-call | flops 1000000000 | bytes 10000000 | tf_op jit(solution)/shard_map/factor/pallas_call | solution.py:210
  57.4 0.0 collective-permute-done.4.second
  57.4 0.1 collective-permute-done.3.first
  57.5 0.0 collective-permute-done.2.pair
  57.5 3.1 %apply.1 = (f32[224,4096]{1,0:T(8,128)}, bf16[224,4096]{1,0:T(8,128)(2,1)}, f32[32,224]{1,0:T(8,128)}) custom-call(f32[224,2048]{1,0:T(8,128)S(1)} %get-tuple-element.19.own_comp, f32[224,2048]{1,0:T(8,128)S(1)} %get-tuple-element.20.other_comp, f32[32,256]{1,0:T(8,128)S(1)} %get-tuple-element.26.own, f32[32,256]{1,0:T(8,128)S(1)} %collective-permute-done.2.pair, ...), custom_call_target="tpu_custom_call" | custom-call | tf_op jit(solution)/shard_map/apply/pallas_call | solution.py:282
  (5 shorter events, 0.1 us)
Async XLA Ops:
  2.7 5.4 %collective-permute-start = (f32[16,32,128]{2,1,0:T(8,128)S(1)}, f32[16,32,128]{2,1,0:T(8,128)S(1)}, u32[]{:S(2)}, u32[]{:S(2)}) collective-permute-start(f32[16,32,128]{2,1,0:T(8,128)S(1)} %get-tuple-element.23), channel_id=1, source_target_pairs={{0,1},{1,0},{2,3},{3,2},{4,5},{5,4},{6,7},{7,6},{8,9},{9,8},{10,11... | collective-permute-start | bytes 786440 | tf_op jit(solution)/shard_map/ppermute | solution.py:305
  50.3 1.5 %collective-permute-start.1 = (f32[16,32,128]{2,1,0:T(8,128)S(1)}, f32[16,32,128]{2,1,0:T(8,128)S(1)}, u32[]{:S(2)}, u32[]{:S(2)}) collective-permute-start(f32[16,32,128]{2,1,0:T(8,128)S(1)} %all_to_all.17.blocks), channel_id=1, source_target_pairs={{0,1},{1,0},{2,3},{3,2},{4,5},{5,4},{6,7},{7,6},{8,9},{9,8},{10,11... | collective-permute-start | bytes 786440 | tf_op jit(solution)/shard_map/ppermute | solution.py:305
  52.2 5.1 %collective-permute-start.4 = (f32[32,256]{1,0:T(8,128)S(1)}, f32[32,256]{1,0:T(8,128)S(1)}, u32[]{:S(2)}, u32[]{:S(2)}) collective-permute-start(f32[32,256]{1,0:T(8,128)S(1)} %get-tuple-element.26.own), channel_id=1, source_target_pairs={{0,192},{64,128},{128,64},{192,0},{1,193},{65,129},{129,65},{193,1... | collective-permute-start | bytes 98312 | tf_op jit(solution)/shard_map/ppermute | solution.py:305
  53.2 4.3 %collective-permute-start.3 = (f32[32,256]{1,0:T(8,128)S(1)}, f32[32,256]{1,0:T(8,128)S(1)}, u32[]{:S(2)}, u32[]{:S(2)}) collective-permute-start(f32[32,256]{1,0:T(8,128)S(1)} %get-tuple-element.26.own), channel_id=1, source_target_pairs={{0,128},{64,192},{128,0},{192,64},{1,129},{65,193},{129,1},{193,65... | collective-permute-start | bytes 98312 | tf_op jit(solution)/shard_map/ppermute | solution.py:305
  53.9 3.6 %collective-permute-start.2 = (f32[32,256]{1,0:T(8,128)S(1)}, f32[32,256]{1,0:T(8,128)S(1)}, u32[]{:S(2)}, u32[]{:S(2)}) collective-permute-start(f32[32,256]{1,0:T(8,128)S(1)} %get-tuple-element.26.own), channel_id=1, source_target_pairs={{0,64},{64,0},{128,192},{192,128},{1,65},{65,1},{129,193},{193,129... | collective-permute-start | bytes 98312 | tf_op jit(solution)/shard_map/ppermute | solution.py:305

commit v11 on v9

--- a/solution.py
+++ b/solution.py
@@ -20,7 +20,11 @@
 WIDTH = HALF // CHUNKS
 GROUP = 8
 SWAP = (1, 0)
-REPLICAS = ((1, 0, 3, 2), (2, 3, 0, 1), (3, 2, 1, 0))
+REPLICAS = (
+    ((1, 0, 3, 2), (2, 0, 3, 1)),
+    ((3, 2, 0, 1), (3, 2, 1, 0)),
+    ((2, 3, 1, 0), (1, 3, 0, 2)),
+)
 OWNERS = [[C * z + (half + z // (Z // C)) % C for z in range(Z)] for half in range(C)]
 F32, BF16 = jnp.float32, jnp.bfloat16
 CONTRACT_LAST = (((1,), (1,)), ((), ()))
@@ -243,7 +247,9 @@
     update_sems,
     q_sem,
 ):
-    total = (own[...] + pair[...]) + (first[...] + second[...])
+    swapped = lax.axis_index("c") == 0
+    one, two = pair[...], first[...]
+    total = (own[...] + jnp.where(swapped, one, two)) + (jnp.where(swapped, two, one) + second[...])
     q_t = jnp.dot(
         inverse[...], total * (1.0 / X), precision=lax.Precision.HIGHEST, preferred_element_type=F32
     )
@@ -310,6 +316,11 @@
     return terms[0]
 
 
+def send_by_core(array, targets):
+    pairs = [(C * x + c, C * targets[c][x] + c) for x in range(X) for c in range(C)]
+    return lax.ppermute(array, ("x", "c"), pairs)
+
+
 def repeat(block, times):
     return jnp.broadcast_to(block, (times,) + block.shape)
 
@@ -329,7 +340,7 @@
     other = send(mine, "c", SWAP)
     product, own_terms = project(own_low, mine)
     product, other_terms = project(other_low, other, product)
-    pair, first, second = (send(product, "x", targets) for targets in REPLICAS)
+    pair, first, second = (send_by_core(product, targets) for targets in REPLICAS)
     factors = factor(own_terms, other_terms)
     new_errors, update, new_q = apply(
         own_comp, other_comp, product, pair, first, second, *factors, own_terms, other_terms

time: 60.9 us -> 61 us (level)
    ppermute x5 -> x2, starting transfers between devices: 6.67 us -> 3.33 us  [send(): return lax.ppermute(array, axis, list(enumerate(targets)))]
    ppermute x0 -> x3, starting transfers between devices: none -> 3.34 us  [send_by_core(): return lax.ppermute(array, ('x', 'c'), pairs)]
where the time goes in v11:
time: 61 us; the launch traced here: 60.5 us
  blocking collectives  42.1 us (69%)
  Pallas kernels  9.8 us (16%)
  starting transfers between devices  6.67 us (11%)
  waiting for transfers between devices  1.13 us (2%)
  between operations  0.73 us (1%)
    all_to_all x1, blocking collectives, reduce_and_gather(): lax.all_to_all(repeat(block, Z), ('z', 'c'), 0, 0, axis_index_groups=OWNERS)  18.1 us
    all_to_all x1, blocking collectives, reduce_and_gather(): block = add_up(lax.all_to_all(mine, ('x', 'y'), 0, 0))  12.6 us
    all_to_all x1, blocking collectives, reduce_and_gather(): return lax.all_to_all(repeat(block, BLOCKS), ('x', 'y'), 0, 0)  11.3 us
    pallas_call x2, Pallas kernels, compensate(): pl.pallas_call(functools.partial(compensate_kernel, own), out_shape=(pltp...  4.07 us
    ppermute x3, starting transfers between devices, send_by_core(): return lax.ppermute(array, ('x', 'c'), pairs)  3.34 us
    ppermute x2, starting transfers between devices, send(): return lax.ppermute(array, axis, list(enumerate(targets)))  3.33 us
    pallas_call x1, Pallas kernels, apply(): pl.pallas_call(apply_kernel, out_shape=(jax.ShapeDtypeStruct((ROWS, FEATU...  3.02 us
    pallas_call x1, Pallas kernels, factor(): pl.pallas_call(factor_kernel, out_shape=(pltpu.VMEM((RANK, RANK), F32), p...  1.86 us
  transfers between devices with their start and end apart: 5, of which 1 were waited for; matrix products, arithmetic and copies ran while one was open for 0% of the time, Pallas kernels for 7%

profile of v11, /device:TPU:1, one launch (start us, length us, event | category | flops | bytes accessed | tf_op | source)
XLA Modules:
  0.0 60.5 jit_solution(2606139350315620487)
XLA Ops:
  0.6 2.0 %compensate_other.1 = (f32[224,2048]{1,0:T(8,128)S(1)}, bf16[224,2048]{1,0:T(8,128)(2,1)S(1)}, f32[16,32,128]{2,1,0:T(8,128)S(1)}) custom-call(bf16[224,4096]{1,0:T(8,128)(2,1)} %bitcast.11, f32[224,4096]{1,0:T(8,128)} %bitcast.9, bf16[32,224]{1,0:T(8,128)(2,1)} %bitcast.13), custom_call_target="tpu_custom_call" | custom-call | flops 29360128 | bytes 2752512 | tf_op jit(solution)/shard_map/compensate_other/pallas_call | solution.py:97
  2.7 3.3 %collective-permute-start = (f32[16,32,128]{2,1,0:T(8,128)S(1)}, f32[16,32,128]{2,1,0:T(8,128)S(1)}, u32[]{:S(2)}, u32[]{:S(2)}) collective-permute-start(f32[16,32,128]{2,1,0:T(8,128)S(1)} %get-tuple-element.23), channel_id=1, source_target_pairs={{0,1},{1,0},{2,3},{3,2},{4,5},{5,4},{6,7},{7,6},{8,9},{9,8},{10,11... | collective-permute-start | bytes 786440 | tf_op jit(solution)/shard_map/ppermute | solution.py:309
  6.0 2.0 %compensate_own.1 = (f32[224,2048]{1,0:T(8,128)S(1)}, bf16[224,2048]{1,0:T(8,128)(2,1)S(1)}, f32[16,32,128]{2,1,0:T(8,128)S(1)}) custom-call(bf16[224,4096]{1,0:T(8,128)(2,1)} %bitcast.12, f32[224,4096]{1,0:T(8,128)} %bitcast.10, bf16[32,224]{1,0:T(8,128)(2,1)} %bitcast.14), custom_call_target="tpu_custom_call" | custom-call | flops 29360128 | bytes 2752512 | tf_op jit(solution)/shard_map/compensate_own/pallas_call | solution.py:97
  8.0 0.0 collective-permute-done
  8.1 12.6 %all_to_all.15 = f32[16,32,128]{2,1,0:T(8,128)S(1)} all-to-all(f32[16,32,128]{2,1,0:T(8,128)S(1)} %add.95), channel_id=1, replica_groups=mesh['x'=4,'y'=4,'z'=8,'c'=2] {'x','y'}, dimensions={0} | all-to-all | bytes 524288 | tf_op jit(solution)/shard_map/all_to_all | solution.py:329
  20.8 18.1 %all_to_all.16 = f32[8,32,128]{2,1,0:T(8,128)S(1)} all-to-all(f32[8,32,128]{2,1,0:T(8,128)S(1)} %broadcast_in_dim.9), channel_id=1, replica_groups={{0,2,4,6,9,11,13,15},{1,3,5,7,8,10,12,14},{16,18,20,22,25,27,29,31},{17..., dimensions={0} | all-to-all | bytes 262144 | tf_op jit(solution)/shard_map/all_to_all | solution.py:330
  38.9 11.3 %all_to_all.17.blocks = f32[16,32,128]{2,1,0:T(8,128)S(1)} all-to-all(f32[16,32,128]{2,1,0:T(8,128)S(1)} %broadcast_in_dim.10), channel_id=1, replica_groups=mesh['x'=4,'y'=4,'z'=8,'c'=2] {'x','y'}, dimensions={0} | all-to-all | bytes 524288 | tf_op jit(solution)/shard_map/all_to_all | solution.py:331
  50.3 0.0 collective-permute-start.1
  50.3 0.4 project.2
  50.7 1.1 %collective-permute-done.1.blocks = f32[16,32,128]{2,1,0:T(8,128)S(1)} collective-permute-done((f32[16,32,128]{2,1,0:T(8,128)S(1)}, f32[16,32,128]{2,1,0:T(8,128)S(1)}, u32[]{:S(2)}, u32[]{:S(2)}) %collective-permute-start.1) | collective-permute-done | bytes 262176 | tf_op jit(solution)/shard_map/ppermute | solution.py:309
  51.8 0.4 project.3
  52.2 0.1 collective-permute-start.4
  52.3 1.3 %collective-permute-start.3 = (f32[32,256]{1,0:T(8,128)S(1)}, f32[32,256]{1,0:T(8,128)S(1)}, u32[]{:S(2)}, u32[]{:S(2)}) collective-permute-start(f32[32,256]{1,0:T(8,128)S(1)} %get-tuple-element.26.own), channel_id=1, source_target_pairs={{0,192},{1,193},{64,128},{65,129},{128,0},{129,65},{192,64},{193,1... | collective-permute-start | bytes 98312 | tf_op jit(solution)/shard_map/ppermute | solution.py:321
  53.6 2.0 %collective-permute-start.2 = (f32[32,256]{1,0:T(8,128)S(1)}, f32[32,256]{1,0:T(8,128)S(1)}, u32[]{:S(2)}, u32[]{:S(2)}) collective-permute-start(f32[32,256]{1,0:T(8,128)S(1)} %get-tuple-element.26.own), channel_id=1, source_target_pairs={{0,64},{1,129},{64,0},{65,1},{128,192},{129,193},{192,128},{193,65... | collective-permute-start | bytes 98312 | tf_op jit(solution)/shard_map/ppermute | solution.py:321
  55.6 1.9 %factor.1 = (f32[32,32]{1,0:T(8,128)S(1)}, bf16[32,192]{1,0:T(8,128)(2,1)S(1)}, bf16[64,1024]{1,0:T(8,128)(2,1)S(1)}) custom-call(bf16[96,2048]{1,0:T(8,128)(2,1)S(1)} %get-tuple-element.27.own_terms, bf16[96,2048]{1,0:T(8,128)(2,1)S(1)} %get-tuple-element.28.other_terms), custom_call_target="tpu_custom_call" | custom-call | flops 1000000000 | bytes 10000000 | tf_op jit(solution)/shard_map/factor/pallas_call | solution.py:213
  57.5 0.0 collective-permute-done.4.second
  57.5 0.0 collective-permute-done.3.first
  57.5 0.0 collective-permute-done.2.pair
  57.5 3.0 %apply.1 = (f32[224,4096]{1,0:T(8,128)}, bf16[224,4096]{1,0:T(8,128)(2,1)}, f32[32,224]{1,0:T(8,128)}) custom-call(f32[224,2048]{1,0:T(8,128)S(1)} %get-tuple-element.19.own_comp, f32[224,2048]{1,0:T(8,128)S(1)} %get-tuple-element.20.other_comp, f32[32,256]{1,0:T(8,128)S(1)} %get-tuple-element.26.own, f32[32,256]{1,0:T(8,128)S(1)} %collective-permute-done.2.pair, ...), custom_call_target="tpu_custom_call" | custom-call | tf_op jit(solution)/shard_map/apply/pallas_call | solution.py:286
  (5 shorter events, 0.1 us)
Async XLA Ops:
  2.7 5.4 %collective-permute-start = (f32[16,32,128]{2,1,0:T(8,128)S(1)}, f32[16,32,128]{2,1,0:T(8,128)S(1)}, u32[]{:S(2)}, u32[]{:S(2)}) collective-permute-start(f32[16,32,128]{2,1,0:T(8,128)S(1)} %get-tuple-element.23), channel_id=1, source_target_pairs={{0,1},{1,0},{2,3},{3,2},{4,5},{5,4},{6,7},{7,6},{8,9},{9,8},{10,11... | collective-permute-start | bytes 786440 | tf_op jit(solution)/shard_map/ppermute | solution.py:309
  50.3 1.5 %collective-permute-start.1 = (f32[16,32,128]{2,1,0:T(8,128)S(1)}, f32[16,32,128]{2,1,0:T(8,128)S(1)}, u32[]{:S(2)}, u32[]{:S(2)}) collective-permute-start(f32[16,32,128]{2,1,0:T(8,128)S(1)} %all_to_all.17.blocks), channel_id=1, source_target_pairs={{0,1},{1,0},{2,3},{3,2},{4,5},{5,4},{6,7},{7,6},{8,9},{9,8},{10,11... | collective-permute-start | bytes 786440 | tf_op jit(solution)/shard_map/ppermute | solution.py:309
  52.2 5.2 %collective-permute-start.4 = (f32[32,256]{1,0:T(8,128)S(1)}, f32[32,256]{1,0:T(8,128)S(1)}, u32[]{:S(2)}, u32[]{:S(2)}) collective-permute-start(f32[32,256]{1,0:T(8,128)S(1)} %get-tuple-element.26.own), channel_id=1, source_target_pairs={{0,128},{1,65},{64,192},{65,193},{128,64},{129,1},{192,0},{193,129... | collective-permute-start | bytes 98312 | tf_op jit(solution)/shard_map/ppermute | solution.py:321
  52.3 5.1 %collective-permute-start.3 = (f32[32,256]{1,0:T(8,128)S(1)}, f32[32,256]{1,0:T(8,128)S(1)}, u32[]{:S(2)}, u32[]{:S(2)}) collective-permute-start(f32[32,256]{1,0:T(8,128)S(1)} %get-tuple-element.26.own), channel_id=1, source_target_pairs={{0,192},{1,193},{64,128},{65,129},{128,0},{129,65},{192,64},{193,1... | collective-permute-start | bytes 98312 | tf_op jit(solution)/shard_map/ppermute | solution.py:321
  53.6 3.9 %collective-permute-start.2 = (f32[32,256]{1,0:T(8,128)S(1)}, f32[32,256]{1,0:T(8,128)S(1)}, u32[]{:S(2)}, u32[]{:S(2)}) collective-permute-start(f32[32,256]{1,0:T(8,128)S(1)} %get-tuple-element.26.own), channel_id=1, source_target_pairs={{0,64},{1,129},{64,0},{65,1},{128,192},{129,193},{192,128},{193,65... | collective-permute-start | bytes 98312 | tf_op jit(solution)/shard_map/ppermute | solution.py:321

commit v12 on v11

--- a/solution.py
+++ b/solution.py
@@ -18,6 +18,7 @@
 BLOCK = HALF // BLOCKS
 CHUNKS = 2
 WIDTH = HALF // CHUNKS
+PARTS = ((0, 512), (512, HALF))
 GROUP = 8
 SWAP = (1, 0)
 REPLICAS = (
@@ -206,7 +207,7 @@
     one, two, three = (term.astype(F32) for term in three_terms(lower_inverse))
     beside = jnp.concatenate([one, one, two, one, two, three], axis=1).astype(BF16)
     weights[...] = beside
-    ortho[...] = ortho_terms(beside, own_terms[:, in_half(0)])
+    ortho[...] = ortho_terms(beside, own_terms[:, slice(*PARTS[0])])
 
 
 def factor(own_terms, other_terms):
@@ -215,7 +216,7 @@
         out_shape=(
             pltpu.VMEM((RANK, RANK), F32),
             pltpu.VMEM((RANK, 6 * RANK), BF16),
-            pltpu.VMEM((2 * RANK, WIDTH), BF16),
+            pltpu.VMEM((2 * RANK, PARTS[0][1]), BF16),
         ),
         in_specs=[VMEM] * 2,
         out_specs=[VMEM] * 3,
@@ -260,8 +261,9 @@
     stacked = jnp.concatenate([high, high, q_t - high]).T[:ROWS].astype(BF16)
     for half, (comp, terms) in enumerate(((own_comp, own_terms), (other_comp, other_terms))):
         start = half_start(half == 0)
-        for chunk in range(CHUNKS):
-            cols, at = in_half(chunk), in_hbm(start, chunk)
+        for chunk, (begin, end) in enumerate(PARTS):
+            cols = slice(begin, end)
+            at = pl.ds(pl.multiple_of(start + begin, PARTS[0][1]), end - begin)
             ready = half == 0 and chunk == 0
             ortho = first_ortho[...] if ready else ortho_terms(weights[...], terms[:, cols])
             ortho = jnp.concatenate([ortho, ortho[:RANK]])
@@ -296,8 +298,8 @@
             pltpu.VMEM((C, ROWS, HALF), F32),
             pltpu.VMEM((C, ROWS, HALF), BF16),
             pltpu.VMEM((RANK, ROWS), F32),
-            pltpu.SemaphoreType.DMA((C, CHUNKS)),
-            pltpu.SemaphoreType.DMA((C, CHUNKS)),
+            pltpu.SemaphoreType.DMA((C, len(PARTS))),
+            pltpu.SemaphoreType.DMA((C, len(PARTS))),
             pltpu.SemaphoreType.DMA,
         ],
         compiler_params=params(20),

time: 61 us -> 61.1 us (level)
  no operation moved by 1% of the time
where the time goes in v12:
time: 61.1 us; the launch traced here: 60.5 us
  blocking collectives  42.1 us (69%)
  Pallas kernels  9.81 us (16%)
  starting transfers between devices  6.67 us (11%)
  waiting for transfers between devices  1.13 us (2%)
  between operations  0.73 us (1%)
    all_to_all x1, blocking collectives, reduce_and_gather(): lax.all_to_all(repeat(block, Z), ('z', 'c'), 0, 0, axis_index_groups=OWNERS)  18.1 us
    all_to_all x1, blocking collectives, reduce_and_gather(): block = add_up(lax.all_to_all(mine, ('x', 'y'), 0, 0))  12.6 us
    all_to_all x1, blocking collectives, reduce_and_gather(): return lax.all_to_all(repeat(block, BLOCKS), ('x', 'y'), 0, 0)  11.3 us
    pallas_call x2, Pallas kernels, compensate(): pl.pallas_call(functools.partial(compensate_kernel, own), out_shape=(pltp...  4.07 us
    ppermute x3, starting transfers between devices, send_by_core(): return lax.ppermute(array, ('x', 'c'), pairs)  3.34 us
    ppermute x2, starting transfers between devices, send(): return lax.ppermute(array, axis, list(enumerate(targets)))  3.33 us
    pallas_call x1, Pallas kernels, apply(): pl.pallas_call(apply_kernel, out_shape=(jax.ShapeDtypeStruct((ROWS, FEATU...  3.11 us
    pallas_call x1, Pallas kernels, factor(): pl.pallas_call(factor_kernel, out_shape=(pltpu.VMEM((RANK, RANK), F32), p...  1.79 us
  transfers between devices with their start and end apart: 5, of which 1 were waited for; matrix products, arithmetic and copies ran while one was open for 0% of the time, Pallas kernels for 7%

profile of v12, /device:TPU:1, one launch (start us, length us, event | category | flops | bytes accessed | tf_op | source)
XLA Modules:
  0.0 60.5 jit_solution(5070359220633206859)
XLA Ops:
  0.6 2.0 %compensate_other.1 = (f32[224,2048]{1,0:T(8,128)S(1)}, bf16[224,2048]{1,0:T(8,128)(2,1)S(1)}, f32[16,32,128]{2,1,0:T(8,128)S(1)}) custom-call(bf16[224,4096]{1,0:T(8,128)(2,1)} %bitcast.11, f32[224,4096]{1,0:T(8,128)} %bitcast.9, bf16[32,224]{1,0:T(8,128)(2,1)} %bitcast.13), custom_call_target="tpu_custom_call" | custom-call | flops 29360128 | bytes 2752512 | tf_op jit(solution)/shard_map/compensate_other/pallas_call | solution.py:98
  2.7 3.3 %collective-permute-start = (f32[16,32,128]{2,1,0:T(8,128)S(1)}, f32[16,32,128]{2,1,0:T(8,128)S(1)}, u32[]{:S(2)}, u32[]{:S(2)}) collective-permute-start(f32[16,32,128]{2,1,0:T(8,128)S(1)} %get-tuple-element.23), channel_id=1, source_target_pairs={{0,1},{1,0},{2,3},{3,2},{4,5},{5,4},{6,7},{7,6},{8,9},{9,8},{10,11... | collective-permute-start | bytes 786440 | tf_op jit(solution)/shard_map/ppermute | solution.py:311
  6.0 2.0 %compensate_own.1 = (f32[224,2048]{1,0:T(8,128)S(1)}, bf16[224,2048]{1,0:T(8,128)(2,1)S(1)}, f32[16,32,128]{2,1,0:T(8,128)S(1)}) custom-call(bf16[224,4096]{1,0:T(8,128)(2,1)} %bitcast.12, f32[224,4096]{1,0:T(8,128)} %bitcast.10, bf16[32,224]{1,0:T(8,128)(2,1)} %bitcast.14), custom_call_target="tpu_custom_call" | custom-call | flops 29360128 | bytes 2752512 | tf_op jit(solution)/shard_map/compensate_own/pallas_call | solution.py:98
  8.0 0.0 collective-permute-done
  8.1 12.6 %all_to_all.15 = f32[16,32,128]{2,1,0:T(8,128)S(1)} all-to-all(f32[16,32,128]{2,1,0:T(8,128)S(1)} %add.95), channel_id=1, replica_groups=mesh['x'=4,'y'=4,'z'=8,'c'=2] {'x','y'}, dimensions={0} | all-to-all | bytes 524288 | tf_op jit(solution)/shard_map/all_to_all | solution.py:331
  20.8 18.1 %all_to_all.16 = f32[8,32,128]{2,1,0:T(8,128)S(1)} all-to-all(f32[8,32,128]{2,1,0:T(8,128)S(1)} %broadcast_in_dim.9), channel_id=1, replica_groups={{0,2,4,6,9,11,13,15},{1,3,5,7,8,10,12,14},{16,18,20,22,25,27,29,31},{17..., dimensions={0} | all-to-all | bytes 262144 | tf_op jit(solution)/shard_map/all_to_all | solution.py:332
  38.9 11.3 %all_to_all.17.blocks = f32[16,32,128]{2,1,0:T(8,128)S(1)} all-to-all(f32[16,32,128]{2,1,0:T(8,128)S(1)} %broadcast_in_dim.10), channel_id=1, replica_groups=mesh['x'=4,'y'=4,'z'=8,'c'=2] {'x','y'}, dimensions={0} | all-to-all | bytes 524288 | tf_op jit(solution)/shard_map/all_to_all | solution.py:333
  50.3 0.0 collective-permute-start.1
  50.3 0.4 project.2
  50.7 1.1 %collective-permute-done.1.blocks = f32[16,32,128]{2,1,0:T(8,128)S(1)} collective-permute-done((f32[16,32,128]{2,1,0:T(8,128)S(1)}, f32[16,32,128]{2,1,0:T(8,128)S(1)}, u32[]{:S(2)}, u32[]{:S(2)}) %collective-permute-start.1) | collective-permute-done | bytes 262176 | tf_op jit(solution)/shard_map/ppermute | solution.py:311
  51.8 0.4 project.3
  52.2 0.1 collective-permute-start.4
  52.3 1.3 %collective-permute-start.3 = (f32[32,256]{1,0:T(8,128)S(1)}, f32[32,256]{1,0:T(8,128)S(1)}, u32[]{:S(2)}, u32[]{:S(2)}) collective-permute-start(f32[32,256]{1,0:T(8,128)S(1)} %get-tuple-element.26.own), channel_id=1, source_target_pairs={{0,192},{1,193},{64,128},{65,129},{128,0},{129,65},{192,64},{193,1... | collective-permute-start | bytes 98312 | tf_op jit(solution)/shard_map/ppermute | solution.py:323
  53.6 2.0 %collective-permute-start.2 = (f32[32,256]{1,0:T(8,128)S(1)}, f32[32,256]{1,0:T(8,128)S(1)}, u32[]{:S(2)}, u32[]{:S(2)}) collective-permute-start(f32[32,256]{1,0:T(8,128)S(1)} %get-tuple-element.26.own), channel_id=1, source_target_pairs={{0,64},{1,129},{64,0},{65,1},{128,192},{129,193},{192,128},{193,65... | collective-permute-start | bytes 98312 | tf_op jit(solution)/shard_map/ppermute | solution.py:323
  55.6 1.8 %factor.1 = (f32[32,32]{1,0:T(8,128)S(1)}, bf16[32,192]{1,0:T(8,128)(2,1)S(1)}, bf16[64,512]{1,0:T(8,128)(2,1)S(1)}) custom-call(bf16[96,2048]{1,0:T(8,128)(2,1)S(1)} %get-tuple-element.27.own_terms, bf16[96,2048]{1,0:T(8,128)(2,1)S(1)} %get-tuple-element.28.other_terms), custom_call_target="tpu_custom_call" | custom-call | flops 1000000000 | bytes 10000000 | tf_op jit(solution)/shard_map/factor/pallas_call | solution.py:214
  57.4 0.0 collective-permute-done.4.second
  57.4 0.0 collective-permute-done.3.first
  57.4 0.0 collective-permute-done.2.pair
  57.4 3.1 %apply.1 = (f32[224,4096]{1,0:T(8,128)}, bf16[224,4096]{1,0:T(8,128)(2,1)}, f32[32,224]{1,0:T(8,128)}) custom-call(f32[224,2048]{1,0:T(8,128)S(1)} %get-tuple-element.19.own_comp, f32[224,2048]{1,0:T(8,128)S(1)} %get-tuple-element.20.other_comp, f32[32,256]{1,0:T(8,128)S(1)} %get-tuple-element.26.own, f32[32,256]{1,0:T(8,128)S(1)} %collective-permute-done.2.pair, ...), custom_call_target="tpu_custom_call" | custom-call | tf_op jit(solution)/shard_map/apply/pallas_call | solution.py:288
  (5 shorter events, 0.1 us)
Async XLA Ops:
  2.7 5.4 %collective-permute-start = (f32[16,32,128]{2,1,0:T(8,128)S(1)}, f32[16,32,128]{2,1,0:T(8,128)S(1)}, u32[]{:S(2)}, u32[]{:S(2)}) collective-permute-start(f32[16,32,128]{2,1,0:T(8,128)S(1)} %get-tuple-element.23), channel_id=1, source_target_pairs={{0,1},{1,0},{2,3},{3,2},{4,5},{5,4},{6,7},{7,6},{8,9},{9,8},{10,11... | collective-permute-start | bytes 786440 | tf_op jit(solution)/shard_map/ppermute | solution.py:311
  50.3 1.5 %collective-permute-start.1 = (f32[16,32,128]{2,1,0:T(8,128)S(1)}, f32[16,32,128]{2,1,0:T(8,128)S(1)}, u32[]{:S(2)}, u32[]{:S(2)}) collective-permute-start(f32[16,32,128]{2,1,0:T(8,128)S(1)} %all_to_all.17.blocks), channel_id=1, source_target_pairs={{0,1},{1,0},{2,3},{3,2},{4,5},{5,4},{6,7},{7,6},{8,9},{9,8},{10,11... | collective-permute-start | bytes 786440 | tf_op jit(solution)/shard_map/ppermute | solution.py:311
  52.2 5.1 %collective-permute-start.4 = (f32[32,256]{1,0:T(8,128)S(1)}, f32[32,256]{1,0:T(8,128)S(1)}, u32[]{:S(2)}, u32[]{:S(2)}) collective-permute-start(f32[32,256]{1,0:T(8,128)S(1)} %get-tuple-element.26.own), channel_id=1, source_target_pairs={{0,128},{1,65},{64,192},{65,193},{128,64},{129,1},{192,0},{193,129... | collective-permute-start | bytes 98312 | tf_op jit(solution)/shard_map/ppermute | solution.py:323
  52.3 5.1 %collective-permute-start.3 = (f32[32,256]{1,0:T(8,128)S(1)}, f32[32,256]{1,0:T(8,128)S(1)}, u32[]{:S(2)}, u32[]{:S(2)}) collective-permute-start(f32[32,256]{1,0:T(8,128)S(1)} %get-tuple-element.26.own), channel_id=1, source_target_pairs={{0,192},{1,193},{64,128},{65,129},{128,0},{129,65},{192,64},{193,1... | collective-permute-start | bytes 98312 | tf_op jit(solution)/shard_map/ppermute | solution.py:323
  53.6 3.8 %collective-permute-start.2 = (f32[32,256]{1,0:T(8,128)S(1)}, f32[32,256]{1,0:T(8,128)S(1)}, u32[]{:S(2)}, u32[]{:S(2)}) collective-permute-start(f32[32,256]{1,0:T(8,128)S(1)} %get-tuple-element.26.own), channel_id=1, source_target_pairs={{0,64},{1,129},{64,0},{65,1},{128,192},{129,193},{192,128},{193,65... | collective-permute-start | bytes 98312 | tf_op jit(solution)/shard_map/ppermute | solution.py:323
